TPU v7x, 32 devices: a whole 2x2x4 slice. The times are simulated.
32 devices in a mesh: narrow: 4 (over y, x), wide: 8 (over z, core).
Axes of the slice: x: 2, y: 2, z: 4, core: 2. Of those that a mesh axis runs over, the one named last changes fastest.
Arguments:
- lengths: int32 [32], P(('narrow', 'wide')), may hold values from 40 to 512, as said below
- char_ids: int32 [32, 512, 50], P(('narrow', 'wide')), may hold values from 0 to 261
- char_counts: int32 [32, 512], P(('narrow', 'wide')), may hold values from 1 to 50
- token_types: int32 [32, 512], P(('narrow', 'wide')), may hold values from 0 to 1
- out_grad: bfloat16 [32, 512, 768], P(('narrow', 'wide')), may hold values from -6 to 6
- char_table: bfloat16 [4192], P('wide'), may hold values from -6 to 6
- conv_1: bfloat16 [16, 32], P(None, 'wide'), may hold values from -1.5 to 1.5
- conv_2: bfloat16 [32, 32], P(None, 'wide'), may hold values from -1 to 1
- conv_3: bfloat16 [48, 64], P(None, 'wide'), may hold values from -0.875 to 0.875
- conv_4: bfloat16 [64, 128], P(None, 'wide'), may hold values from -0.75 to 0.75
- conv_5: bfloat16 [80, 256], P(None, 'wide'), may hold values from -0.625 to 0.625
- conv_6: bfloat16 [96, 512], P(None, 'wide'), may hold values from -0.625 to 0.625
- conv_7: bfloat16 [112, 1024], P(None, 'wide'), may hold values from -0.5 to 0.5
- conv_bias: bfloat16 [2048], P('wide'), may hold values from -2 to 2
- highway_weight: bfloat16 [2, 2048, 4096], P(None, 'wide'), may hold values from -0.125 to 0.125
- highway_bias: bfloat16 [2, 4096], P(None, 'wide'), may hold values from -2 to 2
- projection: bfloat16 [2048, 768], P('wide'), may hold values from -0.125 to 0.125
- position_table: bfloat16 [512, 768], P('wide'), may hold values from -3 to 3
- type_table: bfloat16 [2, 768], P(None, 'wide'), may hold values from -3 to 3
- embed_gain: bfloat16 [768], P('wide'), may hold values from 0.5 to 1.5
- embed_biases: bfloat16 [2, 768], P(None, 'wide'), may hold values from -2 to 2
- qkv_weight: bfloat16 [768, 2304], P('wide'), may hold values from -0.21875 to 0.21875
- out_weight: bfloat16 [768, 768], P('wide'), may hold values from -0.875 to 0.875
- ff_in: bfloat16 [768, 3072], P('wide'), may hold values from -0.21875 to 0.21875
- ff_in_bias: bfloat16 [3072], P('wide'), may hold values from -2 to 2
- ff_out: bfloat16 [3072, 768], P('wide'), may hold values from -0.109375 to 0.109375
- layer_gains: bfloat16 [2, 768], P(None, 'wide'), may hold values from 0.5 to 1.5
- layer_biases: bfloat16 [6, 768], P(None, 'wide'), may hold values from -2 to 2
Outputs:
- hidden_out: float32 [32, 512, 768], P(('narrow', 'wide'))
- grad_char_table: float32 [4192], P('wide')
- grad_conv_1: float32 [16, 32], P(None, 'wide')
- grad_conv_2: float32 [32, 32], P(None, 'wide')
- grad_conv_3: float32 [48, 64], P(None, 'wide')
- grad_conv_4: float32 [64, 128], P(None, 'wide')
- grad_conv_5: float32 [80, 256], P(None, 'wide')
- grad_conv_6: float32 [96, 512], P(None, 'wide')
- grad_conv_7: float32 [112, 1024], P(None, 'wide')
- grad_conv_bias: float32 [2048], P('wide')
- grad_highway_weight: float32 [2, 2048, 4096], P(None, 'wide')
- grad_highway_bias: float32 [2, 4096], P(None, 'wide')
- grad_projection: float32 [2048, 768], P('wide')
- grad_position_table: float32 [512, 768], P('wide')
- grad_type_table: float32 [2, 768], P(None, 'wide')
- grad_embed_gain: float32 [768], P('wide')
- grad_embed_biases: float32 [2, 768], P(None, 'wide')
- grad_qkv_weight: float32 [768, 2304], P('wide')
- grad_out_weight: float32 [768, 768], P('wide')
- grad_ff_in: float32 [768, 3072], P('wide')
- grad_ff_in_bias: float32 [3072], P('wide')
- grad_ff_out: float32 [3072, 768], P('wide')
- grad_layer_gains: float32 [2, 768], P(None, 'wide')
- grad_layer_biases: float32 [6, 768], P(None, 'wide')
Inputs may be any that keep to these rules, and one draw needn't show every extreme that they name: `lengths`: words of each sequence; at least one sequence has 512 words and one has 40.
All inputs are finite; a program needn't handle non-finite values.
Results may differ from a plain program's by a relative error of at most 0.024.
Values may be sent and summed in bfloat16 or wider, within the bound.
No kernel may reach another device: no remote copies, remote signals or barrier semaphores. Data moves between devices by JAX's collectives and lax.ppermute only.
A program may use at most 384 MiB of HBM per device.

v0:
```python
import math

import jax
import jax.numpy as jnp
from jax import lax
from jax.sharding import PartitionSpec as P

HEADS = 12
HDIM = 64
CDIM = 16


EPSILON = 1e-06
MASKED_SCORE = -1e30
ROOT_HALF = 0.7071067811865476
NORMAL_PEAK = 0.3989422804014327
CONTRACT_ROWS = (((0,), (0,)), ((), ()))
CONTRACT_COLS = (((1,), (1,)), ((), ()))
INNER_FIRST = (((1,), (0,)), ((), ()))


def gelu_curve(value):
    return 0.5 * value * (1.0 + lax.erf(value * ROOT_HALF))


def gelu_slope(value):
    return 0.5 * (1.0 + lax.erf(value * ROOT_HALF)) + value * NORMAL_PEAK * jnp.exp(
        -0.5 * value * value
    )


def normalize(value, gain, shift):
    average = jnp.mean(value, axis=-1, keepdims=True)
    centred = value - average
    spread = jnp.mean(centred * centred, axis=-1, keepdims=True)
    return centred * lax.rsqrt(spread + EPSILON) * gain + shift


def highway_mix(carried, mixing):
    half_rows = carried.shape[0]
    gate_part = jax.nn.sigmoid(mixing[half_rows:])
    return gate_part * carried + (1.0 - gate_part) * gelu_curve(mixing[:half_rows])


def matmul(left, right, dims):
    return lax.dot_general(left, right, dims, preferred_element_type=jnp.float32)


def char_tables(embed_full):
    table_cols = embed_full[0].reshape(-1, CDIM).T
    kernels = [piece for piece in embed_full[1:8]]
    return (table_cols, kernels)


def encode_chars(table_cols, ids_block, count_block):
    vocab_size = table_cols.shape[1]
    onehot = (
        ids_block[:, None, :] == lax.broadcasted_iota(jnp.int32, (1, vocab_size, 1), 1)
    ).astype(jnp.bfloat16)
    present = (lax.broadcasted_iota(jnp.int32, ids_block.shape, 0) < count_block[None, :]).astype(
        jnp.float32
    )
    looked_up = jnp.einsum("dv,cvw->cdw", table_cols, onehot, preferred_element_type=jnp.float32)
    return (onehot, present, (looked_up * present[:, None, :]).astype(jnp.bfloat16))


def convolve(kernel_flat, char_vecs, conv_shift):
    feature_count = char_vecs.shape[1]
    window = kernel_flat.shape[0] // feature_count
    extent = char_vecs.shape[0] - window + 1
    stacked = jnp.concatenate(
        [char_vecs[offset : offset + extent] for offset in range(window)], axis=1
    )
    summed = (
        jnp.einsum("kh,pkw->phw", kernel_flat, stacked, preferred_element_type=jnp.float32)
        + conv_shift[None, :, None]
    )
    return (summed, stacked)


def pool_parts(summed, count_block, window):
    extent = summed.shape[0]
    limit = jnp.maximum(count_block - window, 0)
    valid = (
        lax.broadcasted_iota(jnp.int32, (extent, count_block.shape[0]), 0) <= limit[None, :]
    ).astype(jnp.float32)
    exponent = jnp.exp(summed) * valid[:, None, :]
    denominator = jnp.sum(exponent, axis=0)
    return (exponent, denominator, (limit + 1).astype(jnp.float32))


def embed_block(table_cols, kernels, conv_shift, ids_block, count_block):
    onehot, present, char_vecs = encode_chars(table_cols, ids_block, count_block)
    pieces = []
    channel_start = 0
    for kernel_flat in kernels:
        channels = kernel_flat.shape[1]
        summed, stacked = convolve(
            kernel_flat, char_vecs, conv_shift[channel_start : channel_start + channels]
        )
        exponent, denominator, valid_count = pool_parts(
            summed, count_block, kernel_flat.shape[0] // CDIM
        )
        pieces.append(jnp.log(denominator / valid_count[None, :]))
        channel_start += channels
    return jnp.concatenate(pieces, axis=0)


def char_back(table_cols, kernels, conv_shift, totals, inputs):
    kernel_sums, shift_sum, table_sum = totals
    ids_block, count_block, grad_block = inputs
    onehot, present, char_vecs = encode_chars(table_cols, ids_block, count_block)
    grad_chars = jnp.zeros(char_vecs.shape, jnp.float32)
    new_kernels = []
    shift_parts = []
    channel_start = 0
    for kernel_flat, kernel_sum in zip(kernels, kernel_sums):
        window = kernel_flat.shape[0] // CDIM
        channels = kernel_flat.shape[1]
        summed, stacked = convolve(
            kernel_flat, char_vecs, conv_shift[channel_start : channel_start + channels]
        )
        exponent, denominator, valid_count = pool_parts(summed, count_block, window)
        grad_conv = (
            exponent * (grad_block[channel_start : channel_start + channels] / denominator)[None]
        ).astype(jnp.bfloat16)
        shift_parts.append(jnp.sum(grad_conv, axis=(0, 2), dtype=jnp.float32))
        extent = summed.shape[0]
        new_kernels.append(
            kernel_sum
            + jnp.einsum("pkw,phw->kh", stacked, grad_conv, preferred_element_type=jnp.float32)
        )
        chars_part = jnp.einsum(
            "kh,phw->pkw", kernel_flat, grad_conv, preferred_element_type=jnp.float32
        )
        for offset in range(window):
            grad_chars = grad_chars.at[offset : offset + extent].add(
                chars_part[:, offset * CDIM : (offset + 1) * CDIM]
            )
        channel_start += channels
    masked = jnp.where(
        present[:, None, :] > 0, grad_chars.astype(jnp.bfloat16), jnp.zeros((), jnp.bfloat16)
    )
    table_sum = table_sum + jnp.einsum(
        "cdw,cvw->dv", masked, onehot, preferred_element_type=jnp.float32
    )
    return (new_kernels, shift_sum + jnp.concatenate(shift_parts), table_sum)


def score_block(heads_all, length):
    seq_len = heads_all.shape[0]
    scale_factor = 1.0 / math.sqrt(HDIM)
    scores = (
        jnp.einsum(
            "qhe,khe->hqk", heads_all[:, 0], heads_all[:, 1], preferred_element_type=jnp.float32
        )
        * scale_factor
    )
    keep_keys = lax.broadcasted_iota(jnp.int32, (1, 1, seq_len), 2) < length
    return jnp.where(keep_keys, scores, MASKED_SCORE)


def attend(proj_seq, length):
    seq_len = proj_seq.shape[0]
    heads_all = proj_seq.reshape(seq_len, 3, HEADS, HDIM)
    scores = score_block(heads_all, length)
    highest = jnp.max(scores, axis=2, keepdims=True)
    exponent = jnp.exp(scores - highest)
    denominator = jnp.sum(exponent, axis=2, keepdims=True)
    attention = (exponent / denominator).astype(jnp.bfloat16)
    context = jnp.einsum(
        "hqk,khe->qhe", attention, heads_all[:, 2], preferred_element_type=jnp.float32
    )
    return (context.reshape(seq_len, -1).astype(jnp.bfloat16), highest + jnp.log(denominator))


def attend_back(proj_seq, log_total, grad_context, length):
    seq_len = proj_seq.shape[0]
    scale_factor = 1.0 / math.sqrt(HDIM)
    heads_all = proj_seq.reshape(seq_len, 3, HEADS, HDIM)
    grad_heads = grad_context.reshape(seq_len, HEADS, HDIM)
    attention = jnp.exp(score_block(heads_all, length) - log_total)
    grad_attention = jnp.einsum(
        "qhe,khe->hqk", grad_heads, heads_all[:, 2], preferred_element_type=jnp.float32
    )
    grad_values = jnp.einsum(
        "hqk,qhe->khe",
        attention.astype(jnp.bfloat16),
        grad_heads,
        preferred_element_type=jnp.float32,
    )
    row_dot = jnp.sum(attention * grad_attention, axis=2, keepdims=True)
    grad_scores = (attention * (grad_attention - row_dot)).astype(jnp.bfloat16)
    grad_queries = (
        jnp.einsum("hqk,khe->qhe", grad_scores, heads_all[:, 1], preferred_element_type=jnp.float32)
        * scale_factor
    )
    grad_keys = (
        jnp.einsum("hqk,qhe->khe", grad_scores, heads_all[:, 0], preferred_element_type=jnp.float32)
        * scale_factor
    )
    return (
        jnp.stack([grad_queries, grad_keys, grad_values], axis=1)
        .reshape(seq_len, -1)
        .astype(jnp.bfloat16)
    )


def fetch_embed(
    char_table,
    conv_1,
    conv_2,
    conv_3,
    conv_4,
    conv_5,
    conv_6,
    conv_7,
    conv_bias,
    highway_weight,
    highway_bias,
    projection,
    position_table,
    type_table,
    embed_gain,
    embed_biases,
):
    return (
        lax.all_gather(char_table, "wide", axis=0, tiled=True),
        lax.all_gather(conv_1, "wide", axis=1, tiled=True),
        lax.all_gather(conv_2, "wide", axis=1, tiled=True),
        lax.all_gather(conv_3, "wide", axis=1, tiled=True),
        lax.all_gather(conv_4, "wide", axis=1, tiled=True),
        lax.all_gather(conv_5, "wide", axis=1, tiled=True),
        lax.all_gather(conv_6, "wide", axis=1, tiled=True),
        lax.all_gather(conv_7, "wide", axis=1, tiled=True),
        lax.all_gather(conv_bias, "wide", axis=0, tiled=True),
        lax.all_gather(highway_weight, "wide", axis=1, tiled=True),
        lax.all_gather(highway_bias, "wide", axis=1, tiled=True),
        lax.all_gather(projection, "wide", axis=0, tiled=True),
        lax.all_gather(position_table, "wide", axis=0, tiled=True),
        lax.all_gather(type_table, "wide", axis=1, tiled=True),
        lax.all_gather(embed_gain, "wide", axis=0, tiled=True),
        lax.all_gather(embed_biases, "wide", axis=1, tiled=True),
    )


def fetch_layer(qkv_weight, out_weight, ff_in, ff_in_bias, ff_out, layer_gains, layer_biases):
    return (
        lax.all_gather(qkv_weight, "wide", axis=0, tiled=True),
        lax.all_gather(out_weight, "wide", axis=0, tiled=True),
        lax.all_gather(ff_in, "wide", axis=0, tiled=True),
        lax.all_gather(ff_in_bias, "wide", axis=0, tiled=True),
        lax.all_gather(ff_out, "wide", axis=0, tiled=True),
        lax.all_gather(layer_gains, "wide", axis=1, tiled=True),
        lax.all_gather(layer_biases, "wide", axis=1, tiled=True),
    )


def fetch_embed_again(
    char_table,
    conv_1,
    conv_2,
    conv_3,
    conv_4,
    conv_5,
    conv_6,
    conv_7,
    conv_bias,
    highway_weight,
    highway_bias,
    projection,
    position_table,
    type_table,
    embed_gain,
    embed_biases,
):
    return (
        lax.all_gather(char_table, "wide", axis=0, tiled=True),
        lax.all_gather(conv_1, "wide", axis=1, tiled=True),
        lax.all_gather(conv_2, "wide", axis=1, tiled=True),
        lax.all_gather(conv_3, "wide", axis=1, tiled=True),
        lax.all_gather(conv_4, "wide", axis=1, tiled=True),
        lax.all_gather(conv_5, "wide", axis=1, tiled=True),
        lax.all_gather(conv_6, "wide", axis=1, tiled=True),
        lax.all_gather(conv_7, "wide", axis=1, tiled=True),
        lax.all_gather(conv_bias, "wide", axis=0, tiled=True),
        lax.all_gather(highway_weight, "wide", axis=1, tiled=True),
        lax.all_gather(highway_bias, "wide", axis=1, tiled=True),
        lax.all_gather(projection, "wide", axis=0, tiled=True),
        lax.all_gather(position_table, "wide", axis=0, tiled=True),
        lax.all_gather(type_table, "wide", axis=1, tiled=True),
        lax.all_gather(embed_gain, "wide", axis=0, tiled=True),
        lax.all_gather(embed_biases, "wide", axis=1, tiled=True),
    )


def fetch_layer_again(qkv_weight, out_weight, ff_in, ff_in_bias, ff_out, layer_gains, layer_biases):
    return (
        lax.all_gather(qkv_weight, "wide", axis=0, tiled=True),
        lax.all_gather(out_weight, "wide", axis=0, tiled=True),
        lax.all_gather(ff_in, "wide", axis=0, tiled=True),
        lax.all_gather(ff_in_bias, "wide", axis=0, tiled=True),
        lax.all_gather(ff_out, "wide", axis=0, tiled=True),
        lax.all_gather(layer_gains, "wide", axis=1, tiled=True),
        lax.all_gather(layer_biases, "wide", axis=1, tiled=True),
    )


def sum_embed(gradients):
    shares = (
        lax.psum_scatter(
            gradients[0].astype(jnp.bfloat16), "wide", scatter_dimension=0, tiled=True
        ).astype(jnp.float32),
        lax.psum_scatter(
            gradients[1].astype(jnp.bfloat16), "wide", scatter_dimension=1, tiled=True
        ).astype(jnp.float32),
        lax.psum_scatter(
            gradients[2].astype(jnp.bfloat16), "wide", scatter_dimension=1, tiled=True
        ).astype(jnp.float32),
        lax.psum_scatter(
            gradients[3].astype(jnp.bfloat16), "wide", scatter_dimension=1, tiled=True
        ).astype(jnp.float32),
        lax.psum_scatter(
            gradients[4].astype(jnp.bfloat16), "wide", scatter_dimension=1, tiled=True
        ).astype(jnp.float32),
        lax.psum_scatter(
            gradients[5].astype(jnp.bfloat16), "wide", scatter_dimension=1, tiled=True
        ).astype(jnp.float32),
        lax.psum_scatter(
            gradients[6].astype(jnp.bfloat16), "wide", scatter_dimension=1, tiled=True
        ).astype(jnp.float32),
        lax.psum_scatter(
            gradients[7].astype(jnp.bfloat16), "wide", scatter_dimension=1, tiled=True
        ).astype(jnp.float32),
        lax.psum_scatter(
            gradients[8].astype(jnp.bfloat16), "wide", scatter_dimension=0, tiled=True
        ).astype(jnp.float32),
        lax.psum_scatter(
            gradients[9].astype(jnp.bfloat16), "wide", scatter_dimension=1, tiled=True
        ).astype(jnp.float32),
        lax.psum_scatter(
            gradients[10].astype(jnp.bfloat16), "wide", scatter_dimension=1, tiled=True
        ).astype(jnp.float32),
        lax.psum_scatter(
            gradients[11].astype(jnp.bfloat16), "wide", scatter_dimension=0, tiled=True
        ).astype(jnp.float32),
        lax.psum_scatter(
            gradients[12].astype(jnp.bfloat16), "wide", scatter_dimension=0, tiled=True
        ).astype(jnp.float32),
        lax.psum_scatter(
            gradients[13].astype(jnp.bfloat16), "wide", scatter_dimension=1, tiled=True
        ).astype(jnp.float32),
        lax.psum_scatter(
            gradients[14].astype(jnp.bfloat16), "wide", scatter_dimension=0, tiled=True
        ).astype(jnp.float32),
        lax.psum_scatter(
            gradients[15].astype(jnp.bfloat16), "wide", scatter_dimension=1, tiled=True
        ).astype(jnp.float32),
    )
    return tuple(
        (
            lax.psum(shares[0].astype(jnp.bfloat16), "narrow").astype(jnp.float32),
            lax.psum(shares[1].astype(jnp.bfloat16), "narrow").astype(jnp.float32),
            lax.psum(shares[2].astype(jnp.bfloat16), "narrow").astype(jnp.float32),
            lax.psum(shares[3].astype(jnp.bfloat16), "narrow").astype(jnp.float32),
            lax.psum(shares[4].astype(jnp.bfloat16), "narrow").astype(jnp.float32),
            lax.psum(shares[5].astype(jnp.bfloat16), "narrow").astype(jnp.float32),
            lax.psum(shares[6].astype(jnp.bfloat16), "narrow").astype(jnp.float32),
            lax.psum(shares[7].astype(jnp.bfloat16), "narrow").astype(jnp.float32),
            lax.psum(shares[8].astype(jnp.bfloat16), "narrow").astype(jnp.float32),
            lax.psum(shares[9].astype(jnp.bfloat16), "narrow").astype(jnp.float32),
            lax.psum(shares[10].astype(jnp.bfloat16), "narrow").astype(jnp.float32),
            lax.psum(shares[11].astype(jnp.bfloat16), "narrow").astype(jnp.float32),
            lax.psum(shares[12].astype(jnp.bfloat16), "narrow").astype(jnp.float32),
            lax.psum(shares[13].astype(jnp.bfloat16), "narrow").astype(jnp.float32),
            lax.psum(shares[14].astype(jnp.bfloat16), "narrow").astype(jnp.float32),
            lax.psum(shares[15].astype(jnp.bfloat16), "narrow").astype(jnp.float32),
        )
    )


def sum_layer(gradients):
    shares = (
        lax.psum_scatter(
            gradients[0].astype(jnp.bfloat16), "wide", scatter_dimension=0, tiled=True
        ).astype(jnp.float32),
        lax.psum_scatter(
            gradients[1].astype(jnp.bfloat16), "wide", scatter_dimension=0, tiled=True
        ).astype(jnp.float32),
        lax.psum_scatter(
            gradients[2].astype(jnp.bfloat16), "wide", scatter_dimension=0, tiled=True
        ).astype(jnp.float32),
        lax.psum_scatter(
            gradients[3].astype(jnp.bfloat16), "wide", scatter_dimension=0, tiled=True
        ).astype(jnp.float32),
        lax.psum_scatter(
            gradients[4].astype(jnp.bfloat16), "wide", scatter_dimension=0, tiled=True
        ).astype(jnp.float32),
        lax.psum_scatter(
            gradients[5].astype(jnp.bfloat16), "wide", scatter_dimension=1, tiled=True
        ).astype(jnp.float32),
        lax.psum_scatter(
            gradients[6].astype(jnp.bfloat16), "wide", scatter_dimension=1, tiled=True
        ).astype(jnp.float32),
    )
    return tuple(
        (
            lax.psum(shares[0].astype(jnp.bfloat16), "narrow").astype(jnp.float32),
            lax.psum(shares[1].astype(jnp.bfloat16), "narrow").astype(jnp.float32),
            lax.psum(shares[2].astype(jnp.bfloat16), "narrow").astype(jnp.float32),
            lax.psum(shares[3].astype(jnp.bfloat16), "narrow").astype(jnp.float32),
            lax.psum(shares[4].astype(jnp.bfloat16), "narrow").astype(jnp.float32),
            lax.psum(shares[5].astype(jnp.bfloat16), "narrow").astype(jnp.float32),
            lax.psum(shares[6].astype(jnp.bfloat16), "narrow").astype(jnp.float32),
        )
    )


def shards(
    lengths,
    char_ids,
    char_counts,
    token_types,
    out_grad,
    char_table,
    conv_1,
    conv_2,
    conv_3,
    conv_4,
    conv_5,
    conv_6,
    conv_7,
    conv_bias,
    highway_weight,
    highway_bias,
    projection,
    position_table,
    type_table,
    embed_gain,
    embed_biases,
    qkv_weight,
    out_weight,
    ff_in,
    ff_in_bias,
    ff_out,
    layer_gains,
    layer_biases,
):
    embed_shards = (
        char_table,
        conv_1,
        conv_2,
        conv_3,
        conv_4,
        conv_5,
        conv_6,
        conv_7,
        conv_bias,
        highway_weight,
        highway_bias,
        projection,
        position_table,
        type_table,
        embed_gain,
        embed_biases,
    )
    layer_shards = (qkv_weight, out_weight, ff_in, ff_in_bias, ff_out, layer_gains, layer_biases)
    embed_full = fetch_embed(*embed_shards)
    layer_full = fetch_layer(*layer_shards)
    seq_count, seq_len, char_slots = char_ids.shape
    word_count = seq_count * seq_len
    block_words = math.gcd(word_count, 256)
    block_count = word_count // block_words
    ids_blocks = char_ids.reshape(block_count, block_words, char_slots).transpose(0, 2, 1)
    count_blocks = char_counts.reshape(block_count, block_words)
    row_keep = (
        (lax.broadcasted_iota(jnp.int32, (seq_count, seq_len), 1) < lengths[:, None])
        .astype(jnp.float32)
        .reshape(word_count, 1)
    )
    type_one = (token_types.reshape(word_count, 1) == 1).astype(jnp.float32)
    table_cols, kernels = char_tables(embed_full)
    conv_shift = embed_full[8].astype(jnp.float32)
    pooled_blocks = lax.map(
        lambda block_pair: embed_block(
            table_cols, kernels, conv_shift, block_pair[0], block_pair[1]
        ),
        (ids_blocks, count_blocks),
    )
    filters = pooled_blocks.shape[1]
    pooled = pooled_blocks.transpose(1, 0, 2).reshape(filters, word_count)
    highway_shift = embed_full[10].astype(jnp.float32)
    carried = gelu_curve(pooled)
    states = []
    low_states = []
    mix_list = []
    for number in range(2):
        low_state = carried.astype(jnp.bfloat16)
        mixing = (
            matmul(embed_full[9][number], low_state, CONTRACT_ROWS) + highway_shift[number][:, None]
        )
        states.append(carried)
        low_states.append(low_state)
        mix_list.append(mixing)
        carried = highway_mix(carried, mixing)
    low_top = carried.astype(jnp.bfloat16)
    embed_shift = embed_full[15].astype(jnp.float32)
    position_rows = jnp.tile(embed_full[12].astype(jnp.float32), (seq_count, 1))
    type_rows = embed_full[13].astype(jnp.float32)
    embed_sum = (
        matmul(low_top, embed_full[11], CONTRACT_ROWS)
        + embed_shift[0]
        + position_rows
        + type_rows[0] * (1.0 - type_one)
        + type_rows[1] * type_one
    )
    embedded = normalize(embed_sum, embed_full[14].astype(jnp.float32), embed_shift[1])
    gain_rows = layer_full[5].astype(jnp.float32)
    shift_rows = layer_full[6].astype(jnp.float32)
    low_in = embedded.astype(jnp.bfloat16)
    model_width = low_in.shape[1]
    bias_full = jnp.concatenate([shift_rows[0], jnp.zeros_like(shift_rows[0]), shift_rows[1]])
    projected = (matmul(low_in, layer_full[0], INNER_FIRST) + bias_full).astype(jnp.bfloat16)
    proj_seqs = projected.reshape(seq_count, seq_len, -1)
    context_seqs, log_totals = lax.map(
        lambda seq_pair: attend(seq_pair[0], seq_pair[1]), (proj_seqs, lengths)
    )
    context = context_seqs.reshape(word_count, -1)
    first_in = embedded + matmul(context, layer_full[1], INNER_FIRST) + shift_rows[2]
    first_out = normalize(first_in, gain_rows[0], shift_rows[3])
    low_first = first_out.astype(jnp.bfloat16)
    inner_pre = matmul(low_first, layer_full[2], INNER_FIRST) + layer_full[3].astype(jnp.float32)
    activated = gelu_curve(inner_pre).astype(jnp.bfloat16)
    second_in = first_out + matmul(activated, layer_full[4], INNER_FIRST) + shift_rows[4]
    final_out = normalize(second_in, gain_rows[1], shift_rows[5])
    hidden_out = (final_out * row_keep).reshape(seq_count, seq_len, -1)
    back_embed = fetch_embed_again(*embed_shards)
    back_layer = fetch_layer_again(*layer_shards)
    gain_back = back_layer[5].astype(jnp.float32)
    grad_top = out_grad.reshape(word_count, -1).astype(jnp.float32) * row_keep
    norm_pull = jax.vjp(normalize, second_in, gain_back[1], shift_rows[5])[1]
    grad_second, grad_gain_two, grad_shift_five = norm_pull(grad_top)
    grad_ffn = grad_second.astype(jnp.bfloat16)
    grad_shift_four = jnp.sum(grad_ffn, axis=0, dtype=jnp.float32)
    weight_ff_out = matmul(activated, grad_ffn, CONTRACT_ROWS)
    grad_inner = (matmul(grad_ffn, back_layer[4], CONTRACT_COLS) * gelu_slope(inner_pre)).astype(
        jnp.bfloat16
    )
    grad_ff_bias = jnp.sum(grad_inner, axis=0, dtype=jnp.float32)
    weight_ff_in = matmul(low_first, grad_inner, CONTRACT_ROWS)
    grad_first = grad_second + matmul(grad_inner, back_layer[2], CONTRACT_COLS)
    norm_pull = jax.vjp(normalize, first_in, gain_back[0], shift_rows[3])[1]
    grad_res, grad_gain_one, grad_shift_three = norm_pull(grad_first)
    grad_attn = grad_res.astype(jnp.bfloat16)
    grad_shift_two = jnp.sum(grad_attn, axis=0, dtype=jnp.float32)
    weight_out = matmul(context, grad_attn, CONTRACT_ROWS)
    grad_context = matmul(grad_attn, back_layer[1], CONTRACT_COLS).astype(jnp.bfloat16)
    grad_seqs = lax.map(
        lambda seq_quad: attend_back(seq_quad[0], seq_quad[1], seq_quad[2], seq_quad[3]),
        (proj_seqs, log_totals, grad_context.reshape(seq_count, seq_len, -1), lengths),
    )
    grad_proj = grad_seqs.reshape(word_count, -1)
    grad_shift_zero = jnp.sum(grad_proj[:, :model_width], axis=0, dtype=jnp.float32)
    grad_shift_one = jnp.sum(grad_proj[:, 2 * model_width :], axis=0, dtype=jnp.float32)
    weight_qkv = matmul(low_in, grad_proj, CONTRACT_ROWS)
    grad_embedded = grad_res + matmul(grad_proj, back_layer[0], CONTRACT_COLS)
    layer_terms = (
        weight_qkv,
        weight_out,
        weight_ff_in,
        grad_ff_bias,
        weight_ff_out,
        jnp.stack([grad_gain_one, grad_gain_two]),
        jnp.stack(
            [
                grad_shift_zero,
                grad_shift_one,
                grad_shift_two,
                grad_shift_three,
                grad_shift_four,
                grad_shift_five,
            ]
        ),
    )
    layer_sums = sum_layer(layer_terms)
    norm_pull = jax.vjp(normalize, embed_sum, back_embed[14].astype(jnp.float32), embed_shift[1])[1]
    grad_sum, grad_embed_gain, grad_embed_shift = norm_pull(grad_embedded)
    grad_embed = grad_sum.astype(jnp.bfloat16)
    grad_embed_zero = jnp.sum(grad_embed, axis=0, dtype=jnp.float32)
    grad_position = jnp.sum(grad_embed.reshape(seq_count, seq_len, -1), axis=0, dtype=jnp.float32)
    type_mask = type_one.astype(jnp.bfloat16)
    grad_type_one = jnp.sum(grad_embed * type_mask, axis=0, dtype=jnp.float32)
    grad_type_zero = jnp.sum(grad_embed * (1 - type_mask), axis=0, dtype=jnp.float32)
    weight_proj = matmul(low_top, grad_embed, INNER_FIRST)
    grad_carry = matmul(back_embed[11], grad_embed, CONTRACT_COLS)
    weight_high = [None, None]
    shift_high = [None, None]
    for number in (1, 0):
        mix_pull = jax.vjp(highway_mix, states[number], mix_list[number])[1]
        grad_state, grad_mix = mix_pull(grad_carry)
        grad_mix_low = grad_mix.astype(jnp.bfloat16)
        shift_high[number] = jnp.sum(grad_mix_low, axis=1, dtype=jnp.float32)
        weight_high[number] = matmul(low_states[number], grad_mix_low, CONTRACT_COLS)
        grad_carry = grad_state + matmul(back_embed[9][number], grad_mix_low, INNER_FIRST)
    grad_pooled = grad_carry * gelu_slope(pooled)
    grad_blocks = grad_pooled.reshape(filters, block_count, block_words).transpose(1, 0, 2)
    table_back, kernels_back = char_tables(back_embed)
    shift_back = back_embed[8].astype(jnp.float32)
    start_totals = (
        [jnp.zeros(kernel_flat.shape, jnp.float32) for kernel_flat in kernels_back],
        jnp.zeros((filters,), jnp.float32),
        jnp.zeros(table_back.shape, jnp.float32),
    )

    def back_block(totals, inputs):
        return (char_back(table_back, kernels_back, shift_back, totals, inputs), None)

    scanned = lax.scan(back_block, start_totals, (ids_blocks, count_blocks, grad_blocks))[0]
    kernel_grads, conv_shift_grad, table_grad = scanned
    embed_terms = (
        table_grad.T.reshape(-1),
        kernel_grads[0],
        kernel_grads[1],
        kernel_grads[2],
        kernel_grads[3],
        kernel_grads[4],
        kernel_grads[5],
        kernel_grads[6],
        conv_shift_grad,
        jnp.stack(weight_high),
        jnp.stack(shift_high),
        weight_proj,
        grad_position,
        jnp.stack([grad_type_zero, grad_type_one]),
        grad_embed_gain,
        jnp.stack([grad_embed_zero, grad_embed_shift]),
    )
    embed_sums = sum_embed(embed_terms)
    return (hidden_out,) + embed_sums + layer_sums


def solution(mesh):
    in_specs = (
        P(("narrow", "wide")),
        P(("narrow", "wide"), None, None),
        P(("narrow", "wide"), None),
        P(("narrow", "wide"), None),
        P(("narrow", "wide"), None, None),
        P("wide"),
        P(None, "wide"),
        P(None, "wide"),
        P(None, "wide"),
        P(None, "wide"),
        P(None, "wide"),
        P(None, "wide"),
        P(None, "wide"),
        P("wide"),
        P(None, "wide", None),
        P(None, "wide"),
        P("wide", None),
        P("wide", None),
        P(None, "wide"),
        P("wide"),
        P(None, "wide"),
        P("wide", None),
        P("wide", None),
        P("wide", None),
        P("wide"),
        P("wide", None),
        P(None, "wide"),
        P(None, "wide"),
    )
    out_specs = (
        P(("narrow", "wide"), None, None),
        P("wide"),
        P(None, "wide"),
        P(None, "wide"),
        P(None, "wide"),
        P(None, "wide"),
        P(None, "wide"),
        P(None, "wide"),
        P(None, "wide"),
        P("wide"),
        P(None, "wide", None),
        P(None, "wide"),
        P("wide", None),
        P("wide", None),
        P(None, "wide"),
        P("wide"),
        P(None, "wide"),
        P("wide", None),
        P("wide", None),
        P("wide", None),
        P("wide"),
        P("wide", None),
        P(None, "wide"),
        P(None, "wide"),
    )
    return jax.shard_map(shards, mesh=mesh, in_specs=in_specs, out_specs=out_specs, check_vma=False)
```

profile of v0, /device:TPU:0, one launch (start us, length us, event | category | flops | bytes accessed | tf_op | source)
XLA Modules:
  0.0 1617.8 jit_solution(5162380376880645582)
XLA Ops:
  17.5 13.4 all-gather.4
  31.6 8.7 all-gather.3
  41.0 18.5 %all-gather.6 = bf16[8,96,2]{1,2,0:T(2,128)(2,1)S(1)} all-gather(bf16[1,96,2]{1,2,0:T(2,128)(2,1)S(1)} %bitcast.809), channel_id=1, replica_groups=mesh['narrow'=4,'wide'=8] {'wide'}, dimensions={0}, use_global_device_ids=true | all-gather | bytes 3456 | tf_op jit(solution)/shard_map/all_gather | solution.py:254
  60.2 15.5 all-gather.1
  76.3 21.9 %all-gather.2 = bf16[8,4,32]{2,1,0:T(4,128)(2,1)S(1)} all-gather(bf16[1,4,32]{2,1,0:T(4,128)(2,1)S(1)} %bitcast.805), channel_id=1, replica_groups=mesh['narrow'=4,'wide'=8] {'wide'}, dimensions={0}, use_global_device_ids=true | all-gather | bytes 2304 | tf_op jit(solution)/shard_map/all_gather | solution.py:230
  98.2 11.1 all-gather
  109.9 38.8 %all-reduce.14 = (bf16[4192]{0:T(1024)(128)(2,1)S(1)}, bf16[768]{0:T(1024)(128)(2,1)S(1)}) all-reduce(bf16[4192]{0:T(1024)(128)(2,1)S(1)} %dynamic-update-slice.191, bf16[768]{0:T(1024)(128)(2,1)S(1)} %dynamic-update-slice.192), channel_id=1, replica_groups=mesh['narrow'=4,'wide'=8] {'wide'}, use_global_device_ids=true, to_apply=%add.4 | all-reduce | flops 4960 | bytes 19840
  149.3 18.2 %all-gather.7 = bf16[8,1,384]{2,1,0:T(2,128)(2,1)S(1)} all-gather(bf16[1,1,384]{2,1,0:T(2,128)(2,1)S(1)} %reshape.1515), channel_id=1, replica_groups=mesh['narrow'=4,'wide'=8] {'wide'}, dimensions={0}, use_global_device_ids=true | all-gather | bytes 6912 | tf_op jit(solution)/shard_map/all_gather | solution.py:252
  168.1 24.8 %all_gather.90 = bf16[48,64]{0,1:T(8,128)(2,1)S(1)} all-gather(bf16[48,8]{0,1:T(8,128)(2,1)S(1)} %copy-done.133), channel_id=1, replica_groups=mesh['narrow'=4,'wide'=8] {'wide'}, dimensions={1}, use_global_device_ids=true | all-gather | bytes 6912 | tf_op jit(solution)/shard_map/all_gather | solution.py:231
  193.0 22.6 %all_gather.96 = bf16[2,4096]{1,0:T(2,128)(2,1)S(1)} all-gather(bf16[2,512]{1,0:T(2,128)(2,1)S(1)} %copy-done.134), channel_id=1, replica_groups=mesh['narrow'=4,'wide'=8] {'wide'}, dimensions={1}, use_global_device_ids=true | all-gather | bytes 18432 | tf_op jit(solution)/shard_map/all_gather | solution.py:238
  215.6 22.6 %all-gather.5 = bf16[8,96,6]{1,2,0:T(8,128)(2,1)S(1)} all-gather(bf16[1,96,6]{1,2,0:T(8,128)(2,1)S(1)} %bitcast.804), channel_id=1, replica_groups=mesh['narrow'=4,'wide'=8] {'wide'}, dimensions={0}, use_global_device_ids=true | all-gather | bytes 10368 | tf_op jit(solution)/shard_map/all_gather | solution.py:255
  239.6 21.1 %all_gather.91 = bf16[64,128]{0,1:T(8,128)(2,1)S(1)} all-gather(bf16[64,16]{0,1:T(8,128)(2,1)S(1)} %copy-done.124), channel_id=1, replica_groups=mesh['narrow'=4,'wide'=8] {'wide'}, dimensions={1}, use_global_device_ids=true | all-gather | bytes 18432 | tf_op jit(solution)/shard_map/all_gather | solution.py:232
  261.0 22.2 %all_gather.92 = bf16[80,256]{0,1:T(8,128)(2,1)S(1)} all-gather(bf16[80,32]{0,1:T(8,128)(2,1)S(1)} %copy-done.120), channel_id=1, replica_groups=mesh['narrow'=4,'wide'=8] {'wide'}, dimensions={1}, use_global_device_ids=true | all-gather | bytes 46080 | tf_op jit(solution)/shard_map/all_gather | solution.py:233
  284.3 20.2 %all_gather.93 = bf16[96,512]{0,1:T(8,128)(2,1)S(1)} all-gather(bf16[96,64]{0,1:T(8,128)(2,1)S(1)} %copy-done.102), channel_id=1, replica_groups=mesh['narrow'=4,'wide'=8] {'wide'}, dimensions={1}, use_global_device_ids=true | all-gather | bytes 110592 | tf_op jit(solution)/shard_map/all_gather | solution.py:234
  305.2 13.3 all_gather.94
  318.5 19.9 %all_gather.99 = bf16[512,768]{1,0:T(8,128)(2,1)} all-gather(bf16[64,768]{1,0:T(8,128)(2,1)S(1)} %copy-done.74), channel_id=1, replica_groups=mesh['narrow'=4,'wide'=8] {'wide'}, dimensions={0}, use_global_device_ids=true | all-gather | bytes 884736 | tf_op jit(solution)/shard_map/all_gather | solution.py:240
  338.4 87.5 %while.80 = (s32[]{:T(128)}, f32[2,2048,256]{1,2,0:T(8,128)}, s32[2,50,256]{2,1,0:T(8,128)}, bf16[16,262]{1,0:T(8,128)(2,1)S(1)}, s32[2,256]{1,0:T(2,128)S(1)}, ...) while((s32[]{:T(128)}, f32[2,2048,256]{1,2,0:T(8,128)}, ...), condition=%wide.region_8.9_spmd, body=%wide.region_0.8_spmd.sunk | while | flops 4703264768 | bytes 48250108 | solution.py:484
  368.5 9.4 multiply_reduce_fusion.30
  412.1 9.4 multiply_reduce_fusion.30
  428.9 12.0 add_bitcast_fusion.1
  447.0 13.4 add_bitcast_fusion
  496.8 8.6 multiply_convert_fusion.1
  505.4 13.9 all-gather.25.cloned.1.call-done
  519.3 6.5 fusion.238
  545.3 6.8 fusion.189
  552.1 8.9 multiply_reduce_fusion.7
  561.0 6.8 multiply_convert_fusion
  603.3 6.7 convolution_convert_fusion
  610.2 12.5 multiply_add_fusion.1
  622.7 24.4 %multiply_add_fusion = (f32[2048,512]{0,1:T(8,128)}, f32[2048,512]{0,1:T(8,128)}, f32[2048,512]{0,1:T(8,128)}) fusion(f32[4096,512]{0,1:T(8,128)} %copy-done.17, f32[2048,512]{0,1:T(8,128)} %get-tuple-element.1440, bf16[2,2048,4096]{2,1,0:T(8,128)(2,1)} %all-gather.15.cloned.1.call-done, f32[2048,512]{0,1:T(8,128)} %get-tuple-element.1504, ...), kind=kOutput, calls=%fused_computation.390 | convolution fusion | flops 8624537600 | bytes 58720256 | tf_op jit(solution)/shard_map/dot_general | solution.py:46
  649.1 20.2 %fusion.159 = f32[2048,512]{0,1:T(8,128)} fusion(f32[2,2048,256]{1,2,0:T(8,128)} %get-tuple-element.965, f32[2048,512]{0,1:T(8,128)} %get-tuple-element.1441, f32[2048,512]{0,1:T(8,128)} %get-tuple-element.1525, bf16[2,2048,4096]{2,1,0:T(8,128)(2,1)} %all-gather.15.cloned.1.call-done, f32[2048,512]{0,1:T(8,128)} %get-tuple-element.1502, ...), kind=kOutput, calls=%fused_computation.362 | convolution fusion | flops 8606711808 | bytes 46137344 | tf_op jit(solution)/shard_map/dot_general | solution.py:46
  674.8 16.8 %convert_bitcast_fusion.1 = bf16[1,2048,4096]{2,1,0:T(8,128)(2,1)} fusion(f32[2048,512]{0,1:T(8,128)} %get-tuple-element.1440, f32[2048,512]{0,1:T(8,128)} %get-tuple-element.1502, f32[2048,512]{0,1:T(8,128)} %get-tuple-element.1501), kind=kOutput, calls=%fused_computation.314 | convolution fusion | flops 8603566080 | bytes 29360128 | tf_op jit(solution)/shard_map/dot_general | solution.py:46
  691.6 16.8 %convert_bitcast_fusion = bf16[1,2048,4096]{2,1,0:T(8,128)(2,1)} fusion(f32[2048,512]{0,1:T(8,128)} %copy-done.5, f32[2048,512]{0,1:T(8,128)} %get-tuple-element.1504, f32[2048,512]{0,1:T(8,128)} %copy-done.32), kind=kOutput, calls=%fused_computation.313 | convolution fusion | flops 8603566080 | bytes 29360128 | tf_op jit(solution)/shard_map/dot_general | solution.py:46
  708.3 23.0 %pad_maximum_fusion.9 = bf16[2,2048,4096]{2,1,0:T(8,128)(2,1)} fusion(bf16[1,2048,4096]{2,1,0:T(8,128)(2,1)} %convert_bitcast_fusion, bf16[1,2048,4096]{2,1,0:T(8,128)(2,1)} %convert_bitcast_fusion.1), kind=kLoop, calls=%fused_computation.310 | loop fusion | flops 16777216 | bytes 67108864 | tf_op jit(solution)/shard_map/stack | solution.py:630
  732.1 385.9 %while.81 = (s32[]{:T(128)}, f32[16,32]{1,0:T(8,128)S(1)}, f32[32,32]{1,0:T(8,128)S(1)}, f32[48,64]{1,0:T(8,128)}, f32[64,128]{1,0:T(8,128)}, /*index=5*/f32[80,...) while((s32[]{:T(128)}, f32[16,32]{1,0:T(8,128)S(1)}, ...), condition=%wide.region_39.40_spmd.clone, body=%wide.region_24.39_spmd.clone.sunk | while | flops 13990870016 | bytes 519937152 | solution.py:618
  777.8 8.0 bitcast_reduce_fusion.18
  791.1 7.4 convert_reduce_fusion.18
  805.2 11.4 bitcast_reduce_fusion.19
  822.8 11.6 convert_reduce_fusion.19
  842.9 19.6 %bitcast_reduce_fusion.20 = (f32[1024,256]{0,1:T(8,128)}, f32[44,256,1024]{2,1,0:T(8,128)}) fusion(f32[44,256]{1,0:T(8,128)S(1)} %fusion.490, f32[1024]{0:T(1024)S(1)} %slice.2308, bf16[44,112,256]{2,1,0:T(8,128)(2,1)S(1)} %slice_dynamic-update-slice_fusion.107, bf16[112,1024]{1,0:T(8,128)(2,1)} %get-tuple-element.2019), kind=kOutput, calls=%fused_computation.98.clone.1 | convolution fusion | flops 2618032128 | bytes 49987584 | tf_op jit(solution)/shard_map/while/body/eval_jaxpr/kh,pkw->phw/dot_general | solution.py:75
  870.2 24.6 %convert_reduce_fusion.20 = (f32[1024]{0:T(1024)S(1)}, bf16[44,1024,256]{1,2,0:T(8,128)(2,1)}) fusion(f32[1024,256]{0,1:T(8,128)} %copy.393, f32[44,256]{1,0:T(8,128)S(1)} %fusion.490, f32[44,256,1024]{2,1,0:T(8,128)} %get-tuple-element.1886, f32[1024]{0:T(1024)S(1)} %slice.2308), kind=kLoop, calls=%fused_computation.100.clone.1 | loop fusion | flops 69204992 | bytes 70307840 | tf_op jit(solution)/shard_map/while/body/eval_jaxpr/reduce_sum | solution.py:127
  894.9 10.4 fusion.492
  905.5 12.4 convolution_bitcast_fusion.27
  968.3 8.0 bitcast_reduce_fusion.18
  981.7 7.1 convert_reduce_fusion.18
  995.5 11.4 bitcast_reduce_fusion.19
  1013.0 11.9 convert_reduce_fusion.19
  1033.5 19.0 %bitcast_reduce_fusion.20 = (f32[1024,256]{0,1:T(8,128)}, f32[44,256,1024]{2,1,0:T(8,128)}) fusion(f32[44,256]{1,0:T(8,128)S(1)} %fusion.490, f32[1024]{0:T(1024)S(1)} %slice.2308, bf16[44,112,256]{2,1,0:T(8,128)(2,1)S(1)} %slice_dynamic-update-slice_fusion.107, bf16[112,1024]{1,0:T(8,128)(2,1)} %get-tuple-element.2019), kind=kOutput, calls=%fused_computation.98.clone.1 | convolution fusion | flops 2618032128 | bytes 49987584 | tf_op jit(solution)/shard_map/while/body/eval_jaxpr/kh,pkw->phw/dot_general | solution.py:75
  1060.3 24.8 %convert_reduce_fusion.20 = (f32[1024]{0:T(1024)S(1)}, bf16[44,1024,256]{1,2,0:T(8,128)(2,1)}) fusion(f32[1024,256]{0,1:T(8,128)} %copy.393, f32[44,256]{1,0:T(8,128)S(1)} %fusion.490, f32[44,256,1024]{2,1,0:T(8,128)} %get-tuple-element.1886, f32[1024]{0:T(1024)S(1)} %slice.2308), kind=kLoop, calls=%fused_computation.100.clone.1 | loop fusion | flops 69204992 | bytes 70307840 | tf_op jit(solution)/shard_map/while/body/eval_jaxpr/reduce_sum | solution.py:127
  1085.1 11.1 fusion.492
  1096.3 12.2 convolution_bitcast_fusion.27
  1127.5 6.5 fusion.208
  1139.2 28.9 %reduce-scatter.35.cloned.1.call-done = bf16[2,256,4096]{2,1,0:T(8,128)(2,1)} async-done(((bf16[2,2048,4096]{2,1,0:T(8,128)(2,1)}), bf16[2,256,4096]{2,1,0:T(8,128)(2,1)}) %reduce-scatter.35.cloned.1.call-update) | async-done | bytes 4194320 | tf_op jit(solution)/shard_map/reduce_scatter | solution.py:338
  1172.6 26.5 %all-reduce.13 = (bf16[4192]{0:T(1024)(128)(2,1)S(1)}, bf16[16,32]{0,1:T(8,128)(2,1)S(1)}, bf16[32,32]{0,1:T(8,128)(2,1)S(1)}, bf16[48,64]{0,1:T(8,128)(2,1)S(1)...) all-reduce(bf16[4192]{0:T(1024)(128)(2,1)S(1)} %convert_element_typ, ...), channel_id=2, replica_groups=mesh['narrow'=4,'wide'=8] {'wide'}, use_global_device_ids=true, to_apply=%region_40.41.clone | all-reduce | flops 14688 | bytes 58752
  1200.3 29.9 %reduce-scatter.61.cloned.1.call-done = bf16[96,2]{1,0:T(8,128)(2,1)} async-done(((bf16[768,2]{1,0:T(8,128)(2,1)}), bf16[96,2]{1,0:T(8,128)(2,1)}) %reduce-scatter.61.cloned.1.call-update) | async-done | bytes 400
  1231.0 30.4 %reduce-scatter.59.cloned.1.call-done = bf16[96,2]{1,0:T(8,128)(2,1)} async-done(((bf16[768,2]{1,0:T(8,128)(2,1)}), bf16[96,2]{1,0:T(8,128)(2,1)}) %reduce-scatter.59.cloned.1.call-update) | async-done | bytes 400
  1262.2 29.7 %reduce-scatter.65.cloned.1.call-done = bf16[96,6]{1,0:T(8,128)(2,1)} async-done(((bf16[768,6]{1,0:T(8,128)(2,1)}), bf16[96,6]{1,0:T(8,128)(2,1)}) %reduce-scatter.65.cloned.1.call-update) | async-done | bytes 1168
  1292.7 30.1 %reduce-scatter.49.cloned.1.call-done = bf16[16,64]{1,0:T(8,128)(2,1)} async-done(((bf16[128,64]{1,0:T(8,128)(2,1)}), bf16[16,64]{1,0:T(8,128)(2,1)}) %reduce-scatter.49.cloned.1.call-update) | async-done | bytes 2064
  1323.5 32.7 %reduce-scatter.57.cloned.1.call-done = bf16[512,2]{1,0:T(8,128)(2,1)} async-done(((bf16[4096,2]{1,0:T(8,128)(2,1)}), bf16[512,2]{1,0:T(8,128)(2,1)}) %reduce-scatter.57.cloned.1.call-update) | async-done | bytes 2064
  1357.2 29.3 %reduce-scatter.51.cloned.1.call-done = bf16[32,80]{1,0:T(8,128)(2,1)} async-done(((bf16[256,80]{1,0:T(8,128)(2,1)}), bf16[32,80]{1,0:T(8,128)(2,1)}) %reduce-scatter.51.cloned.1.call-update) | async-done | bytes 5136
  1387.3 30.4 %reduce-scatter.53.cloned.1.call-done = bf16[64,96]{1,0:T(8,128)(2,1)} async-done(((bf16[512,96]{1,0:T(8,128)(2,1)}), bf16[64,96]{1,0:T(8,128)(2,1)}) %reduce-scatter.53.cloned.1.call-update) | async-done | bytes 12304
  1418.6 30.6 %reduce-scatter.55.cloned.1.call-done = bf16[128,112]{1,0:T(8,128)(2,1)} async-done(((bf16[1024,112]{1,0:T(8,128)(2,1)}), bf16[128,112]{1,0:T(8,128)(2,1)}) %reduce-scatter.55.cloned.1.call-update) | async-done | bytes 28688
  1450.0 20.1 %all-reduce.15 = (bf16[64,16]{1,0:T(8,128)(2,1)S(1)}, bf16[80,32]{1,0:T(8,128)(2,1)S(1)}, bf16[96,64]{1,0:T(8,128)(2,1)S(1)}, bf16[524]{0:T(1024)(128)(2,1)S(1)}...) all-reduce(bf16[64,16]{1,0:T(8,128)(2,1)S(1)} %copy.351, ...), channel_id=1, replica_groups=mesh['narrow'=4,'wide'=8] {'narrow'}, use_global_device_ids=true, to_apply=%region_49.50 | all-reduce | flops 28076 | bytes 112304 | tf_op jit(solution)/shard_map/psum | solution.py:366
  1479.7 117.1 %all-reduce.19.cloned.1.call-done = (bf16[2,256,4096]{2,1,0:T(8,128)(2,1)}, bf16[256,768]{1,0:T(8,128)(2,1)}, bf16[64,768]{1,0:T(8,128)(2,1)}, bf16[96,2304]{1,0...) async-done(((bf16[2,256,4096]{2,1,0:T(8,128)(2,1)}, bf16[256,768]{1,0:T(8,128)(2,1)}, bf16[64,768]{1,0:T(8,128)(2,1)}, ...) | async-done | bytes 6455312 | tf_op jit(solution)/shard_map/psum | solution.py:371
  (1004 shorter events, 405.9 us)
Async XLA Ops:
  7.3 24.3 %copy-start.146 = (bf16[2,96]{1,0:T(2,128)(2,1)S(1)}, bf16[2,96]{1,0:T(2,128)(2,1)}, u32[]{:S(2)}) copy-start(bf16[2,96]{1,0:T(2,128)(2,1)} %param.110) | copy-start | bytes 1156
  7.3 33.7 %copy-start.147 = (bf16[2,96]{1,0:T(2,128)(2,1)S(1)}, bf16[2,96]{1,0:T(2,128)(2,1)}, u32[]{:S(2)}) copy-start(bf16[2,96]{1,0:T(2,128)(2,1)} %param.116) | copy-start | bytes 1156
  7.3 69.0 %copy-start.141 = (bf16[32,4]{0,1:T(4,128)(2,1)S(1)}, bf16[32,4]{0,1:T(4,128)(2,1)}, u32[]{:S(2)}) copy-start(bf16[32,4]{0,1:T(4,128)(2,1)} %param.97) | copy-start | bytes 772
  7.3 90.9 %copy-start.142 = (bf16[16,4]{0,1:T(4,128)(2,1)S(1)}, bf16[16,4]{0,1:T(4,128)(2,1)}, u32[]{:S(2)}) copy-start(bf16[16,4]{0,1:T(4,128)(2,1)} %param.96) | copy-start | bytes 388
  7.3 102.2 %copy-start.151 = (bf16[96]{0:T(256)(128)(2,1)S(1)}, bf16[96]{0:T(256)(128)(2,1)}, u32[]{:S(2)}) copy-start(bf16[96]{0:T(256)(128)(2,1)} %param.109) | copy-start | bytes 580
  7.3 102.4 %copy-start.139 = (bf16[524]{0:T(1024)(128)(2,1)S(1)}, bf16[524]{0:T(1024)(128)(2,1)}, u32[]{:S(2)}) copy-start(bf16[524]{0:T(1024)(128)(2,1)} %param.95) | copy-start | bytes 3148
  7.3 160.8 %copy-start.133 = (bf16[48,8]{0,1:T(8,128)(2,1)S(1)}, bf16[48,8]{0,1:T(8,128)(2,1)}, u32[]{:S(2)}) copy-start(bf16[48,8]{0,1:T(8,128)(2,1)} %param.98) | copy-start | bytes 2308
  7.3 185.7 %copy-start.134 = (bf16[2,512]{1,0:T(2,128)(2,1)S(1)}, bf16[2,512]{1,0:T(2,128)(2,1)}, u32[]{:S(2)}) copy-start(bf16[2,512]{1,0:T(2,128)(2,1)} %param.105) | copy-start | bytes 6148
  7.3 208.2 %copy-start.135 = (bf16[6,96]{1,0:T(8,128)(2,1)S(1)}, bf16[6,96]{1,0:T(8,128)(2,1)}, u32[]{:S(2)}) copy-start(bf16[6,96]{1,0:T(8,128)(2,1)} %param.117) | copy-start | bytes 3460
  7.4 232.2 %copy-start.124 = (bf16[64,16]{0,1:T(8,128)(2,1)S(1)}, bf16[64,16]{0,1:T(8,128)(2,1)}, u32[]{:S(2)}) copy-start(bf16[64,16]{0,1:T(8,128)(2,1)} %param.99) | copy-start | bytes 6148
  7.4 253.6 %copy-start.120 = (bf16[80,32]{0,1:T(8,128)(2,1)S(1)}, bf16[80,32]{0,1:T(8,128)(2,1)}, u32[]{:S(2)}) copy-start(bf16[80,32]{0,1:T(8,128)(2,1)} %param.100) | copy-start | bytes 15364
  7.4 275.9 %copy-start.73 = (s32[1,512,50]{1,0,2:T(1,128)S(1)}, s32[1,512,50]{1,0,2:T(1,128)}, u32[]{:S(2)}) copy-start(s32[1,512,50]{1,0,2:T(1,128)} %param.91) | copy-start | bytes 307204
  7.4 276.9 %copy-start.102 = (bf16[96,64]{0,1:T(8,128)(2,1)S(1)}, bf16[96,64]{0,1:T(8,128)(2,1)}, u32[]{:S(2)}) copy-start(bf16[96,64]{0,1:T(8,128)(2,1)} %param.101) | copy-start | bytes 36868
  7.4 421.4 %all-gather.15.cloned.1.call-start = ((), (), s32[]{:S(2)}) async-start(), calls=%async_computation.16 | async-start | bytes 37748736 | tf_op jit(solution)/shard_map/all_gather | solution.py:237
  8.1 297.1 %copy-start.91 = (bf16[112,128]{1,0:T(8,128)(2,1)S(1)}, bf16[112,128]{1,0:T(8,128)(2,1)}, u32[]{:S(2)}) copy-start(bf16[112,128]{1,0:T(8,128)(2,1)} %param.102) | copy-start | bytes 86020
  8.1 310.4 %copy-start.74 = (bf16[64,768]{1,0:T(8,128)(2,1)S(1)}, bf16[64,768]{1,0:T(8,128)(2,1)}, u32[]{:S(2)}) copy-start(bf16[64,768]{1,0:T(8,128)(2,1)} %param.107) | copy-start | bytes 294916
  8.2 458.6 %all-gather.17.cloned.1.call-start = ((), (), s32[]{:S(2)}) async-start(), calls=%async_computation.17 | async-start | bytes 3538944 | tf_op jit(solution)/shard_map/all_gather | solution.py:239
  8.9 462.8 %all-gather.19.cloned.1.call-start = ((), (), s32[]{:S(2)}) async-start(), calls=%async_computation.18 | async-start | bytes 3981312 | tf_op jit(solution)/shard_map/all_gather | solution.py:249
  9.6 482.5 %all-gather.21.cloned.1.call-start = ((), (), s32[]{:S(2)}) async-start(), calls=%async_computation.19 | async-start | bytes 1327104 | tf_op jit(solution)/shard_map/all_gather | solution.py:250
  10.2 486.5 %all-gather.23.cloned.1.call-start = ((), (), s32[]{:S(2)}) async-start(), calls=%async_computation.20 | async-start | bytes 5308416 | tf_op jit(solution)/shard_map/all_gather | solution.py:251
  10.8 508.5 %all-gather.25.cloned.1.call-start = ((), (), s32[]{:S(2)}) async-start(), calls=%async_computation.21 | async-start | bytes 5308416 | tf_op jit(solution)/shard_map/all_gather | solution.py:253
  11.4 1127.7 %reduce-scatter.39.cloned.1.call-start = ((), (), s32[]{:S(2)}) async-start(), calls=%async_computation.24 | async-start | bytes 884736 | tf_op jit(solution)/shard_map/reduce_scatter | solution.py:347
  338.6 12.4 copy-start.59
  338.6 14.1 copy-start.50
  382.2 12.4 copy-start.59
  382.2 14.1 copy-start.50
  428.8 12.0 copy-start.6
  446.9 13.4 copy-start.5
  496.8 22.5 %copy-start.130 = (f32[768]{0:T(1024)S(1)}, f32[768]{0:T(1024)}, u32[]{:S(2)}) copy-start(f32[768]{0:T(1024)} %get-tuple-element.1295) | copy-start | bytes 9220
  545.3 15.7 slice-start
  545.3 15.7 slice-start.1
  571.3 17.5 %copy-start.22 = (bf16[512,3,12,64]{0,3,2,1:T(8,128)(2,1)}, bf16[512,3,12,64]{0,3,2,1:T(8,128)(2,1)S(1)}, u32[]{:S(2)}) copy-start(bf16[512,3,12,64]{0,3,2,1:T(8,128)(2,1)S(1)} %pad_maximum_fusion.10) | copy-start | bytes 7077892
  579.8 559.3 %reduce-scatter.43.cloned.1.call-start = ((), (), s32[]{:S(2)}) async-start(), calls=%async_computation.26 | async-start | bytes 1327104 | tf_op jit(solution)/shard_map/reduce_scatter | solution.py:387
  583.1 556.1 %reduce-scatter.37.cloned.1.call-start = ((), (), s32[]{:S(2)}) async-start(), calls=%async_computation.23 | async-start | bytes 3538944 | tf_op jit(solution)/shard_map/reduce_scatter | solution.py:344
  588.3 550.9 %reduce-scatter.41.cloned.1.call-start = ((), (), s32[]{:S(2)}) async-start(), calls=%async_computation.25 | async-start | bytes 3981312 | tf_op jit(solution)/shard_map/reduce_scatter | solution.py:384
  594.3 544.9 %reduce-scatter.45.cloned.1.call-start = ((), (), s32[]{:S(2)}) async-start(), calls=%async_computation.27 | async-start | bytes 5308416 | tf_op jit(solution)/shard_map/reduce_scatter | solution.py:390
  602.1 537.1 %reduce-scatter.47.cloned.1.call-start = ((), (), s32[]{:S(2)}) async-start(), calls=%async_computation.28 | async-start | bytes 5308416 | tf_op jit(solution)/shard_map/reduce_scatter | solution.py:396
  609.9 558.1 %reduce-scatter.35.cloned.1.call-start = ((), (), s32[]{:S(2)}) async-start(), calls=%async_computation.22 | async-start | bytes 37748736 | tf_op jit(solution)/shard_map/reduce_scatter | solution.py:338
  622.7 24.4 %copy-start.32 = (f32[2048,512]{0,1:T(8,128)}, f32[2048,512]{0,1:T(8,128)S(1)}, u32[]{:S(2)}) copy-start(f32[2048,512]{0,1:T(8,128)S(1)} %get-tuple-element.1503) | copy-start | bytes 12582916
  731.4 468.1 %reduce-scatter.63.cloned.1.call-start = ((), (), s32[]{:S(2)}) async-start(), calls=%async_computation.36 | async-start | bytes 221184
  732.5 15.5 copy-start.65
  733.2 26.4 %copy-start.113 = (f32[128]{0:T(128)}, f32[128]{0:T(128)S(1)}, u32[]{:S(2)}) copy-start(f32[128]{0:T(128)S(1)} %slice.2305) | copy-start | bytes 1540 | tf_op jit(solution)/shard_map/while
  738.1 21.4 %copy-start.30 = (f32[47,256]{1,0:T(8,128)}, f32[47,256]{1,0:T(8,128)S(1)}, u32[]{:S(2)}) copy-start(f32[47,256]{1,0:T(8,128)S(1)} %fusion.480) | copy-start | bytes 144388 | tf_op jit(solution)/shard_map/while
  743.3 16.3 %copy-start.9 = (bf16[47,16,256]{2,1,0:T(8,128)(2,1)}, bf16[47,16,256]{2,1,0:T(8,128)(2,1)S(1)}, u32[]{:S(2)}) copy-start(bf16[47,16,256]{2,1,0:T(8,128)(2,1)S(1)} %get-tuple-element.1872) | copy-start | bytes 1155076 | tf_op jit(solution)/shard_map/while
  743.3 16.3 %copy-start.11 = (bf16[47,16,256]{2,1,0:T(8,128)(2,1)}, bf16[47,16,256]{2,1,0:T(8,128)(2,1)S(1)}, u32[]{:S(2)}) copy-start(bf16[47,16,256]{2,1,0:T(8,128)(2,1)S(1)} %get-tuple-element.1869) | copy-start | bytes 1155076 | tf_op jit(solution)/shard_map/while
  743.3 16.2 %copy-start.13 = (bf16[47,16,256]{2,1,0:T(8,128)(2,1)}, bf16[47,16,256]{2,1,0:T(8,128)(2,1)S(1)}, u32[]{:S(2)}) copy-start(bf16[47,16,256]{2,1,0:T(8,128)(2,1)S(1)} %get-tuple-element.1870) | copy-start | bytes 1155076 | tf_op jit(solution)/shard_map/while
  743.3 16.2 %copy-start.15 = (bf16[47,16,256]{2,1,0:T(8,128)(2,1)}, bf16[47,16,256]{2,1,0:T(8,128)(2,1)S(1)}, u32[]{:S(2)}) copy-start(bf16[47,16,256]{2,1,0:T(8,128)(2,1)S(1)} %get-tuple-element.1871) | copy-start | bytes 1155076 | tf_op jit(solution)/shard_map/while
  922.9 15.5 copy-start.65
  923.6 26.4 %copy-start.113 = (f32[128]{0:T(128)}, f32[128]{0:T(128)S(1)}, u32[]{:S(2)}) copy-start(f32[128]{0:T(128)S(1)} %slice.2305) | copy-start | bytes 1540 | tf_op jit(solution)/shard_map/while
  928.6 21.4 %copy-start.30 = (f32[47,256]{1,0:T(8,128)}, f32[47,256]{1,0:T(8,128)S(1)}, u32[]{:S(2)}) copy-start(f32[47,256]{1,0:T(8,128)S(1)} %fusion.480) | copy-start | bytes 144388 | tf_op jit(solution)/shard_map/while
  933.8 16.2 %copy-start.9 = (bf16[47,16,256]{2,1,0:T(8,128)(2,1)}, bf16[47,16,256]{2,1,0:T(8,128)(2,1)S(1)}, u32[]{:S(2)}) copy-start(bf16[47,16,256]{2,1,0:T(8,128)(2,1)S(1)} %get-tuple-element.1872) | copy-start | bytes 1155076 | tf_op jit(solution)/shard_map/while
  933.8 16.2 %copy-start.11 = (bf16[47,16,256]{2,1,0:T(8,128)(2,1)}, bf16[47,16,256]{2,1,0:T(8,128)(2,1)S(1)}, u32[]{:S(2)}) copy-start(bf16[47,16,256]{2,1,0:T(8,128)(2,1)S(1)} %get-tuple-element.1869) | copy-start | bytes 1155076 | tf_op jit(solution)/shard_map/while
  933.8 16.2 %copy-start.13 = (bf16[47,16,256]{2,1,0:T(8,128)(2,1)}, bf16[47,16,256]{2,1,0:T(8,128)(2,1)S(1)}, u32[]{:S(2)}) copy-start(bf16[47,16,256]{2,1,0:T(8,128)(2,1)S(1)} %get-tuple-element.1870) | copy-start | bytes 1155076 | tf_op jit(solution)/shard_map/while
  933.8 16.2 %copy-start.15 = (bf16[47,16,256]{2,1,0:T(8,128)(2,1)}, bf16[47,16,256]{2,1,0:T(8,128)(2,1)S(1)}, u32[]{:S(2)}) copy-start(bf16[47,16,256]{2,1,0:T(8,128)(2,1)S(1)} %get-tuple-element.1871) | copy-start | bytes 1155076 | tf_op jit(solution)/shard_map/while
  1013.0 11.9 copy-start.19
  1118.0 112.1 %reduce-scatter.61.cloned.1.call-start = ((), (), s32[]{:S(2)}) async-start(), calls=%async_computation.35 | async-start | bytes 221184
  1121.0 140.3 %reduce-scatter.59.cloned.1.call-start = ((), (), s32[]{:S(2)}) async-start(), calls=%async_computation.34 | async-start | bytes 221184
  1122.0 169.9 %reduce-scatter.65.cloned.1.call-start = ((), (), s32[]{:S(2)}) async-start(), calls=%async_computation.37 | async-start | bytes 221184
  1127.4 195.3 %reduce-scatter.49.cloned.1.call-start = ((), (), s32[]{:S(2)}) async-start(), calls=%async_computation.29 | async-start | bytes 36864
  1134.8 221.4 %reduce-scatter.57.cloned.1.call-start = ((), (), s32[]{:S(2)}) async-start(), calls=%async_computation.33 | async-start | bytes 1179648
  1136.3 250.2 %reduce-scatter.51.cloned.1.call-start = ((), (), s32[]{:S(2)}) async-start(), calls=%async_computation.30 | async-start | bytes 73728
  1137.2 280.6 %reduce-scatter.53.cloned.1.call-start = ((), (), s32[]{:S(2)}) async-start(), calls=%async_computation.31 | async-start | bytes 147456
  1138.0 311.1 %reduce-scatter.55.cloned.1.call-start = ((), (), s32[]{:S(2)}) async-start(), calls=%async_computation.32 | async-start | bytes 294912
  1139.0 457.9 %all-reduce.19.cloned.1.call-start = ((), (), s32[]{:S(2)}) async-start(), calls=%async_computation.38 | async-start | bytes 12910592 | tf_op jit(solution)/shard_map/psum | solution.py:371
  (180 other events, 742.4 us)
Sparse Core Ops, SparseCore 0:
  9.8 294.5 all-gather.14
  306.0 43.0 all-gather.16
  350.8 40.2 all-gather.18
  392.6 21.5 all-gather.20
  415.7 51.4 all-gather.22
  468.7 50.5 all-gather.24
  579.9 30.6 reduce-scatter.38
  613.5 30.6 reduce-scatter.42
  646.6 38.5 reduce-scatter.36
  687.5 42.9 reduce-scatter.40
  732.8 53.4 reduce-scatter.44
  788.4 53.3 reduce-scatter.46
  844.1 323.8 reduce-scatter.34
  1170.2 28.6 reduce-scatter.62
  1201.7 28.4 reduce-scatter.60
  1232.9 28.3 reduce-scatter.58
  1263.5 28.3 reduce-scatter.64
  1294.6 28.0 reduce-scatter.48
  1325.6 30.5 reduce-scatter.56
  1358.3 28.1 reduce-scatter.50
  1389.4 28.2 reduce-scatter.52
  1420.6 28.5 reduce-scatter.54
  1454.5 142.3 all-reduce.18
where the time goes:
time: 1630 us; the launch traced here: 1620 us
  matrix products  440 us (27%)
  waiting for transfers between devices  407 us (25%)
  blocking collectives  360 us (22%)
  other arithmetic  238 us (15%)
  local copies, waits for them, and re-layouts  141 us (9%)
  between operations  21.8 us (1%)
    unnamed x32, waiting for transfers between devices  247 us
    dot_general x21, matrix products, matmul(): lax.dot_general(left, right, dims, preferred_element_type=jnp.float32)  185 us
    dot_general x28, matrix products, convolve(): jnp.einsum('kh,pkw->phw', kernel_flat, stacked, preferred_element_type=jn...  139 us
    psum x1, waiting for transfers between devices, sum_embed(): lax.psum(shares[9].astype(jnp.bfloat16), 'narrow').astype(jnp.float32)  117 us
    reduce_sum x14, other arithmetic, char_back(): shift_parts.append(jnp.sum(grad_conv, axis=(0, 2), dtype=jnp.float32))  105 us
    unnamed x2, blocking collectives  65.3 us
    dot_general x14, matrix products, char_back(): jnp.einsum('kh,phw->pkw', kernel_flat, grad_conv, preferred_element_type=...  42.1 us
    dot_general x14, matrix products, char_back(): jnp.einsum('pkw,phw->kh', stacked, grad_conv, preferred_element_type=jnp....  34.9 us
  transfers between devices with their start and end apart: 23, of which 11 were waited for; matrix products, arithmetic and copies ran while one was open for 45% of the time, Pallas kernels for 0%

commit v1 on v0

v1 whole, which is shorter than its diff:
```python
import functools
import math

import jax
import jax.numpy as jnp
from jax import lax
from jax.experimental import pallas as pl
from jax.experimental.pallas import tpu as pltpu
from jax.sharding import PartitionSpec as P

HEADS = 12
HDIM = 64
CDIM = 16
WCH = 50
TAP = 112
KROWS = 128
MASK_LOW = -1e30
VPAD = 384
VROWS = 272
FLAT = 896
CONV_BLOCK = 128

EPSILON = 1e-06
MASKED_SCORE = -1e30
ROOT_HALF = 0.7071067811865476
NORMAL_PEAK = 0.3989422804014327
CONTRACT_ROWS = (((0,), (0,)), ((), ()))
CONTRACT_COLS = (((1,), (1,)), ((), ()))
INNER_FIRST = (((1,), (0,)), ((), ()))


def gelu_curve(value):
    return 0.5 * value * (1.0 + lax.erf(value * ROOT_HALF))


def gelu_slope(value):
    return 0.5 * (1.0 + lax.erf(value * ROOT_HALF)) + value * NORMAL_PEAK * jnp.exp(
        -0.5 * value * value
    )


def normalize(value, gain, shift):
    average = jnp.mean(value, axis=-1, keepdims=True)
    centred = value - average
    spread = jnp.mean(centred * centred, axis=-1, keepdims=True)
    return centred * lax.rsqrt(spread + EPSILON) * gain + shift


def matmul(left, right, dims=INNER_FIRST):
    return lax.dot_general(left, right, dims, preferred_element_type=jnp.float32)


def conv_fwd_body(block, filters, held, ids_ref, cnt_ref, table_ref, kern_ref, *rest):
    x_ref, den_ref, flat, hot = rest[held:]
    lane = lax.broadcasted_iota(jnp.int32, (block, VPAD), 1)
    groups = FLAT // 128
    for turn in range(8):
        for g in range(groups):
            slot = 8 * g + turn
            if slot < WCH:
                col = ids_ref[:, slot:slot + 1]
                hot[g * block:(g + 1) * block, :] = (col == lane).astype(jnp.float32).astype(jnp.bfloat16)
            else:
                hot[g * block:(g + 1) * block, :] = jnp.zeros((block, VPAD), jnp.bfloat16)
        found = matmul(hot[...], table_ref[turn])
        for g in range(groups):
            part = found[g * block:(g + 1) * block, :]
            if turn == 0:
                flat[:, g * 128:(g + 1) * 128] = part
            else:
                flat[:, g * 128:(g + 1) * 128] += part
    flat[:, FLAT:] = jnp.zeros((block, 128), jnp.float32)
    lane_x = lax.broadcasted_iota(jnp.int32, (block, KROWS), 1)
    width = lane_x - TAP
    count = jnp.broadcast_to(cnt_ref[...], (block, KROWS))
    reach = jnp.maximum(count, width)
    for place in range(WCH):
        a, r = divmod(place, 8)
        first = flat[:, a * 128:(a + 1) * 128]
        if r:
            second = flat[:, (a + 1) * 128:(a + 2) * 128]
            first = pltpu.roll(first, 128 - 16 * r, 1)
            second = pltpu.roll(second, 128 - 16 * r, 1)
            first = jnp.where(lane_x < 128 - 16 * r, first, second)
        extra = jnp.where(width == 0, 1.0, jnp.where((width <= 7) & (place + width > reach), MASK_LOW, 0.0))
        x_ref[place * block:(place + 1) * block, :] = jnp.where(width < 0, first, extra).astype(jnp.bfloat16)

    step = 4
    den_ref[...] = jnp.zeros_like(den_ref)
    tile = 512

    def piece(start, count_p, lo, hi):
        rows = x_ref[pl.ds(start, count_p * block), :]
        summed = matmul(rows, kern_ref[:, lo:hi])
        e = jnp.exp(summed)
        total = e[:block]
        for i in range(1, count_p):
            total = total + e[i * block:(i + 1) * block]
        den_ref[:, lo:hi] += total

    def chunk(i, carry):
        start = pl.multiple_of(i * step * block, step * block)
        for lo in range(0, filters, tile):
            piece(start, step, lo, lo + tile)
        return carry

    lax.fori_loop(0, 11, chunk, 0)
    for lo in range(0, 1024, tile):
        piece(44 * block, 4, lo, lo + tile)
    piece(48 * block, 2, 0, 256)


def conv_forward(call, ids, counts, tables, kern, state):
    block = CONV_BLOCK
    words, filters = ids.shape[0], kern.shape[1]
    return pl.pallas_call(
        functools.partial(conv_fwd_body, block, filters, len(state)),
        grid=(1,),
        in_specs=[
            pl.BlockSpec((block, ids.shape[1]), lambda i: (call, 0)),
            pl.BlockSpec((block, 1), lambda i: (call, 0)),
            pl.BlockSpec(tables.shape, lambda i: (0, 0, 0)),
            pl.BlockSpec(kern.shape, lambda i: (0, 0)),
        ]
        + [pl.BlockSpec(memory_space=pl.ANY)] * len(state),
        out_specs=[
            pl.BlockSpec((WCH * block, KROWS), lambda i: (call, 0)),
            pl.BlockSpec((block, filters), lambda i: (call, 0)),
        ],
        out_shape=[
            jax.ShapeDtypeStruct((words * WCH, KROWS), jnp.bfloat16),
            jax.ShapeDtypeStruct((words, filters), jnp.float32),
        ],
        input_output_aliases={4: 0, 5: 1} if state else {},
        scratch_shapes=[
            pltpu.VMEM((block, FLAT + 128), jnp.float32),
            pltpu.VMEM((FLAT // 128 * block, VPAD), jnp.bfloat16),
        ],
        compiler_params=pltpu.CompilerParams(vmem_limit_bytes=40 << 20),
        cost_estimate=pl.CostEstimate(
            flops=block * WCH * 32 * filters,
            bytes_accessed=block * filters,
            transcendentals=0,
        ),
        name="conv_forward",
    )(ids, counts, tables, kern, *state)


def conv_bwd_body(block, filters, idst_ref, x_ref, ginv_ref, kern_ref, kern_in_ref, table_in_ref, kern_grad_ref, table_grad_ref, gx, flat, hot, part):
    kern_grad_ref[...] = kern_in_ref[...]
    table_grad_ref[...] = table_in_ref[...]

    tile = 512
    step = 4

    def piece(start, count_p, lo, hi):
        rows = x_ref[pl.ds(start, count_p * block), :]
        k = kern_ref[:, lo:hi]
        e = jnp.exp(matmul(rows, k))
        scale = ginv_ref[:, lo:hi]
        g = jnp.concatenate([e[i * block:(i + 1) * block] * scale for i in range(count_p)], axis=0).astype(jnp.bfloat16)
        kern_grad_ref[:, lo:hi] += matmul(rows, g, CONTRACT_ROWS)
        return matmul(g, k, CONTRACT_COLS)

    def chunk(i, carry):
        start = pl.multiple_of(i * step * block, step * block)
        total = piece(start, step, 0, tile)
        for lo in range(tile, filters, tile):
            total = total + piece(start, step, lo, lo + tile)
        gx[pl.ds(start, step * block), :] = total
        return carry

    lax.fori_loop(0, 11, chunk, 0)
    gx[44 * block:48 * block, :] = piece(44 * block, 4, 0, 512) + piece(44 * block, 4, 512, 1024)
    gx[48 * block:50 * block, :] = piece(48 * block, 2, 0, 256)

    flat[...] = jnp.zeros_like(flat)
    lane_x = lax.broadcasted_iota(jnp.int32, (block, 128), 1)
    for place in range(WCH):
        a, r = divmod(place, 8)
        value = jnp.where(lane_x < TAP, gx[place * block:(place + 1) * block, :], 0.0)
        if r:
            value = pltpu.roll(value, 16 * r, 1)
            flat[:, a * 128:(a + 1) * 128] += jnp.where(lane_x >= 16 * r, value, 0.0)
            flat[:, (a + 1) * 128:(a + 2) * 128] += jnp.where(lane_x < 16 * r, value, 0.0)
        else:
            flat[:, a * 128:(a + 1) * 128] += value
    groups = FLAT // 128
    for g in range(groups):
        part[g * block:(g + 1) * block, :] = flat[:, g * 128:(g + 1) * 128].astype(jnp.bfloat16)
    sub = lax.broadcasted_iota(jnp.int32, (VROWS, block), 0)
    lane_t = lax.broadcasted_iota(jnp.int32, (VROWS, 128), 1)
    for turn in range(8):
        for g in range(groups):
            slot = 8 * g + turn
            if slot < WCH:
                row = idst_ref[slot:slot + 1, :]
                hot[:, g * block:(g + 1) * block] = (row == sub).astype(jnp.float32).astype(jnp.bfloat16)
            else:
                hot[:, g * block:(g + 1) * block] = jnp.zeros((VROWS, block), jnp.bfloat16)
        found = matmul(hot[...], part[...])
        table_grad_ref[...] += jnp.where((lane_t >= 16 * turn) & (lane_t < 16 * turn + 16), found, 0.0)


def conv_backward(call, ids_t, x, ginv, kern, state):
    block = CONV_BLOCK
    filters = ginv.shape[1]
    whole = [pl.BlockSpec(kern.shape, lambda i: (0, 0)), pl.BlockSpec((VROWS, 128), lambda i: (0, 0))]
    return pl.pallas_call(
        functools.partial(conv_bwd_body, block, filters),
        grid=(1,),
        in_specs=[
            pl.BlockSpec((ids_t.shape[0], block), lambda i: (0, call)),
            pl.BlockSpec((WCH * block, KROWS), lambda i: (call, 0)),
            pl.BlockSpec((block, filters), lambda i: (call, 0)),
            pl.BlockSpec(kern.shape, lambda i: (0, 0)),
        ]
        + whole,
        out_specs=whole,
        out_shape=[
            jax.ShapeDtypeStruct(kern.shape, jnp.float32),
            jax.ShapeDtypeStruct((VROWS, 128), jnp.float32),
        ],
        input_output_aliases={4: 0, 5: 1},
        scratch_shapes=[
            pltpu.VMEM((WCH * block, 128), jnp.float32),
            pltpu.VMEM((block, FLAT + 128), jnp.float32),
            pltpu.VMEM((VROWS, FLAT // 128 * block), jnp.bfloat16),
            pltpu.VMEM((FLAT // 128 * block, 128), jnp.bfloat16),
        ],
        compiler_params=pltpu.CompilerParams(vmem_limit_bytes=40 << 20),
        cost_estimate=pl.CostEstimate(
            flops=block * WCH * 64 * filters,
            bytes_accessed=block * filters,
            transcendentals=0,
        ),
        name="conv_backward",
    )(ids_t, x, ginv, kern, *state)


def table_turns(table):
    padded = jnp.pad(table, ((0, VPAD - table.shape[0]), (0, 0)))
    return jnp.stack([jnp.pad(padded, ((0, 0), (16 * r, 112 - 16 * r))) for r in range(8)])


def score_block(heads_all, length):
    seq_len = heads_all.shape[0]
    scale_factor = 1.0 / math.sqrt(HDIM)
    scores = (
        jnp.einsum(
            "qhe,khe->hqk", heads_all[:, 0], heads_all[:, 1], preferred_element_type=jnp.float32
        )
        * scale_factor
    )
    keep_keys = lax.broadcasted_iota(jnp.int32, (1, 1, seq_len), 2) < length
    return jnp.where(keep_keys, scores, MASKED_SCORE)


def attend(proj_seq, length):
    seq_len = proj_seq.shape[0]
    heads_all = proj_seq.reshape(seq_len, 3, HEADS, HDIM)
    scores = score_block(heads_all, length)
    highest = jnp.max(scores, axis=2, keepdims=True)
    exponent = jnp.exp(scores - highest)
    denominator = jnp.sum(exponent, axis=2, keepdims=True)
    attention = (exponent / denominator).astype(jnp.bfloat16)
    context = jnp.einsum(
        "hqk,khe->qhe", attention, heads_all[:, 2], preferred_element_type=jnp.float32
    )
    return (context.reshape(seq_len, -1).astype(jnp.bfloat16), highest + jnp.log(denominator))


def attend_back(proj_seq, log_total, grad_context, length):
    seq_len = proj_seq.shape[0]
    scale_factor = 1.0 / math.sqrt(HDIM)
    heads_all = proj_seq.reshape(seq_len, 3, HEADS, HDIM)
    grad_heads = grad_context.reshape(seq_len, HEADS, HDIM)
    attention = jnp.exp(score_block(heads_all, length) - log_total)
    grad_attention = jnp.einsum(
        "qhe,khe->hqk", grad_heads, heads_all[:, 2], preferred_element_type=jnp.float32
    )
    grad_values = jnp.einsum(
        "hqk,qhe->khe",
        attention.astype(jnp.bfloat16),
        grad_heads,
        preferred_element_type=jnp.float32,
    )
    row_dot = jnp.sum(attention * grad_attention, axis=2, keepdims=True)
    grad_scores = (attention * (grad_attention - row_dot)).astype(jnp.bfloat16)
    grad_queries = (
        jnp.einsum("hqk,khe->qhe", grad_scores, heads_all[:, 1], preferred_element_type=jnp.float32)
        * scale_factor
    )
    grad_keys = (
        jnp.einsum("hqk,qhe->khe", grad_scores, heads_all[:, 0], preferred_element_type=jnp.float32)
        * scale_factor
    )
    return (
        jnp.stack([grad_queries, grad_keys, grad_values], axis=1)
        .reshape(seq_len, -1)
        .astype(jnp.bfloat16)
    )


def core_swap(value, wide):
    return lax.ppermute(value, "wide", [(i, i ^ 1) for i in range(wide)])


def chip_shift(value, wide, step):
    return lax.ppermute(value, "wide", [(i, (i + 2 * step) % wide) for i in range(wide)])


def hop(value, narrow, bit):
    return lax.ppermute(value, "narrow", [(i, i ^ bit) for i in range(narrow)])


def low_bit(mask):
    return mask & -mask


def high_bit(mask):
    return 1 << (mask.bit_length() - 1)


def masks_of(narrow, level):
    return [mask for mask in range(narrow) if bin(mask).count("1") == level]


def levels_of(narrow):
    return range(1, narrow.bit_length())


def spread_level(known, narrow, level):
    for mask in masks_of(narrow, level):
        if level == 1:
            known[mask] = hop(known[0], narrow, mask)
        else:
            high, low = high_bit(mask), low_bit(mask)
            known[mask] = (hop(known[mask ^ high][0], narrow, high), hop(known[mask ^ low][1], narrow, low))


def add_low(left, right):
    return (left.astype(jnp.float32) + right.astype(jnp.float32)).astype(jnp.bfloat16)


def bits_of(narrow, half):
    bits = [1 << i for i in range(narrow.bit_length() - 1)]
    return bits if half else bits[::-1]


def sides(half, count):
    if half:
        return slice(1, count, 2), slice(0, count, 2)
    return slice(count // 2, count), slice(0, count // 2)


def collect_round(terms, narrow, turn):
    following = []
    for half, (parts, arrived) in enumerate(terms):
        leaving, staying = sides(half, parts.shape[0])
        sent = hop(add_low(parts[leaving], arrived[leaving]), narrow, bits_of(narrow, half)[turn])
        following.append((add_low(parts[staying], arrived[staying]), sent))
    return following


def tie(*groups):
    return lax.optimization_barrier(groups)


def own_columns(shard, place, narrow):
    rows, columns = shard.shape
    part = columns // 2 // narrow
    return jnp.stack(
        [lax.dynamic_slice(shard, (0, half * (columns // 2) + place * part), (rows, part)) for half in range(2)]
    )


def chip_groups(wide):
    return [[2 * chip + core for chip in range(wide // 2)] for core in range(2)]


def gather_chips(own, wide):
    return lax.all_gather(own, "wide", axis=0, tiled=False, axis_index_groups=chip_groups(wide))


def other_chips(value, chip):
    chips = value.shape[0]
    pieces = [
        lax.dynamic_index_in_dim(value, lax.rem(chip + chips - step, chips), 0, keepdims=False) for step in range(1, chips)
    ]
    return jnp.concatenate(pieces, axis=1)


def swap_known(known, narrow, wide):
    return core_swap(jnp.stack([jnp.stack(known[m]) if m & (m - 1) else known[m] for m in range(narrow)]), wide)


def weight_copies(narrow, layer, where_ref, mask, shard_ref, twin_ref, mine, other, slot_ref, sems):
    rows = shard_ref.shape[1]
    part = slot_ref.shape[2]
    filters = part * narrow
    chips = slot_ref.shape[1] // (2 * rows)
    copies = []
    for half in range(2):
        column = pl.multiple_of(half * filters + (where_ref[0] ^ mask) * part, part)
        for side, (near, far) in enumerate(((shard_ref, mine), (twin_ref, other))):
            for step in range(chips):
                src = near.at[layer, :, pl.ds(column, part)]
                if step:
                    src = far(mask, half).at[(step - 1) * rows : step * rows, :]
                copies.append((src, slot_ref.at[half, pl.ds(block_start(where_ref, side, step, chips, rows), rows), :]))
    return [pltpu.make_async_copy(src, dst, sems.at[i]) for i, (src, dst) in enumerate(copies)]


def block_start(where_ref, side, step, chips, rows):
    block = lax.rem(where_ref[1] + (chips - step), chips) * 2 + (where_ref[2] ^ side)
    return pl.multiple_of(block * rows, rows)


def weights_of_step(narrow, layer, where_ref, shard_ref, twin_ref, mine, other, slots, sems):
    step = pl.program_id(0)

    def copies(mask):
        return weight_copies(
            narrow, layer, where_ref, mask, shard_ref, twin_ref, mine, other, slots.at[mask % 2], sems.at[mask % 2]
        )

    for mask in range(narrow):
        @pl.when(step == mask)
        def _():
            if mask == 0:
                for copy in copies(0):
                    copy.start()
            if mask + 1 < narrow:
                for copy in copies(mask + 1):
                    copy.start()
            for copy in copies(mask):
                copy.wait()
    return slots.at[lax.rem(step, 2)]


def weight_refs(refs, narrow):
    places, count = {}, 0
    for mask in range(narrow):
        for half in range(2):
            if mask & (mask - 1):
                places[mask, half] = refs[count]
                count += 1
            else:
                places[mask, half] = refs[count].at[half]
        if not mask & (mask - 1):
            count += 1
    twin = refs[count]
    return lambda mask, half: places[mask, half], lambda mask, half: twin.at[mask, half], refs[count + 1 :]


def mix_forward_body(narrow, layer, where_ref, low_ref, carry_ref, shift_a_ref, shift_g_ref, shard_ref, twin_ref, *rest):
    mine, other, (next_ref, low_next_ref, a_ref, g_ref, slots, sems) = weight_refs(rest, narrow)
    slot = weights_of_step(narrow, layer, where_ref, shard_ref, twin_ref, mine, other, slots, sems)
    low = low_ref[...]
    a = matmul(low, slot[0]) + shift_a_ref[...]
    g = matmul(low, slot[1]) + shift_g_ref[...]
    a_ref[...] = a
    g_ref[...] = g
    gate = jax.nn.sigmoid(g)
    following = gate * carry_ref[...] + (1.0 - gate) * gelu_curve(a)
    next_ref[...] = following
    low_next_ref[...] = following.astype(jnp.bfloat16)


def mix_forward(layer, where, low, carry, shift, shard, twin, mine, other):
    narrow = other.shape[0]
    words, filters = carry.shape
    part = filters // narrow
    flat = [*jax.tree.leaves(mine), other]
    block = pl.BlockSpec((words, part), lambda i, where: (0, where[0] ^ i))
    return pl.pallas_call(
        functools.partial(mix_forward_body, narrow, layer),
        grid_spec=pltpu.PrefetchScalarGridSpec(
            num_scalar_prefetch=1,
            grid=(narrow,),
            in_specs=[
                pl.BlockSpec((words, filters), lambda i, where: (0, 0)),
                block,
                pl.BlockSpec((1, part), lambda i, where: (0, where[0] ^ i)),
                pl.BlockSpec((1, part), lambda i, where: (0, narrow + (where[0] ^ i))),
            ]
            + [pl.BlockSpec(memory_space=pl.ANY)] * (2 + len(flat)),
            out_specs=[block] * 4,
            scratch_shapes=[
                pltpu.VMEM((2, 2, filters, part), jnp.bfloat16),
                pltpu.SemaphoreType.DMA((2, 4 * (filters // shard.shape[1] // 2))),
            ],
        ),
        out_shape=[
            jax.ShapeDtypeStruct((words, filters), kind) for kind in (jnp.float32, jnp.bfloat16, jnp.float32, jnp.float32)
        ],
        compiler_params=pltpu.CompilerParams(vmem_limit_bytes=48 << 20),
        cost_estimate=pl.CostEstimate(
            flops=words * filters * filters, bytes_accessed=filters * filters,
            transcendentals=0,
        ),
        name="mix_forward",
    )(where, low, carry, shift, shift, shard, twin, *flat)


def mix_backward_body(narrow, layer, where_ref, low_ref, carry_ref, a_ref, g_ref, pull_ref, shard_ref, twin_ref, *rest):
    mine, other, (own_ref, oth_ref, shift_ref, back_ref, slots, low_t_ref, sems) = weight_refs(rest, narrow)
    slot = weights_of_step(narrow, layer, where_ref, shard_ref, twin_ref, mine, other, slots, sems)

    @pl.when(pl.program_id(0) == 0)
    def _():
        for start in range(0, low_ref.shape[1], 256):
            low_t_ref[start : start + 256, :] = low_ref[:, start : start + 256].T

    a = a_ref[...]
    gate = jax.nn.sigmoid(g_ref[...])
    pull = pull_ref[...]
    pull_a = ((1.0 - gate) * gelu_slope(a) * pull).astype(jnp.bfloat16)
    pull_g = (gate * (1.0 - gate) * (carry_ref[...] - gelu_curve(a)) * pull).astype(jnp.bfloat16)
    half_rows = own_ref.shape[2]
    rows = shard_ref.shape[1]
    for half, grad in enumerate((pull_a, pull_g)):
        shift_ref[half, :, :] = jnp.sum(grad.astype(jnp.float32), axis=0, keepdims=True)
        for side, out_ref in enumerate((own_ref, oth_ref)):
            for chip in range(half_rows // rows):
                start = pl.multiple_of((2 * chip + (where_ref[2] ^ side)) * rows, rows)
                out_ref[0, half, chip * rows : (chip + 1) * rows, :] = matmul(
                    low_t_ref[pl.ds(start, rows), :], grad
                ).astype(jnp.bfloat16)
    back = matmul(pull_a, slot[0], CONTRACT_COLS) + matmul(pull_g, slot[1], CONTRACT_COLS)

    @pl.when(pl.program_id(0) == 0)
    def _():
        back_ref[...] = back

    @pl.when(pl.program_id(0) > 0)
    def _():
        back_ref[...] += back

    part = gate.shape[1]
    column = pl.multiple_of((where_ref[0] ^ pl.program_id(0)) * part, part)
    back_ref[:, pl.ds(column, part)] += gate * pull


def mix_backward(layer, where, low, carry, a, g, pull, shard, twin, mine, other):
    narrow = other.shape[0]
    words, filters = carry.shape
    part = filters // narrow
    flat = [*jax.tree.leaves(mine), other]
    block = pl.BlockSpec((words, part), lambda i, where: (0, where[0] ^ i))
    grad_block = pl.BlockSpec((1, 2, filters // 2, part), lambda i, where: (i, 0, 0, 0))
    grad_shape = jax.ShapeDtypeStruct((narrow, 2, filters // 2, part), jnp.bfloat16)
    return pl.pallas_call(
        functools.partial(mix_backward_body, narrow, layer),
        grid_spec=pltpu.PrefetchScalarGridSpec(
            num_scalar_prefetch=1,
            grid=(narrow,),
            in_specs=[pl.BlockSpec((words, filters), lambda i, where: (0, 0))]
            + [block] * 4
            + [pl.BlockSpec(memory_space=pl.ANY)] * (2 + len(flat)),
            out_specs=[
                grad_block,
                grad_block,
                pl.BlockSpec((2, 1, part), lambda i, where: (0, 0, where[0] ^ i)),
                pl.BlockSpec((words, filters), lambda i, where: (0, 0)),
            ],
            scratch_shapes=[
                pltpu.VMEM((2, 2, filters, part), jnp.bfloat16),
                pltpu.VMEM((filters, words), jnp.bfloat16),
                pltpu.SemaphoreType.DMA((2, 4 * (filters // shard.shape[1] // 2))),
            ],
        ),
        out_shape=[
            grad_shape,
            grad_shape,
            jax.ShapeDtypeStruct((2, 1, filters), jnp.float32),
            jax.ShapeDtypeStruct((words, filters), jnp.float32),
        ],
        compiler_params=pltpu.CompilerParams(vmem_limit_bytes=56 << 20),
        cost_estimate=pl.CostEstimate(
            flops=words * filters * filters, bytes_accessed=filters * filters,
            transcendentals=0,
        ),
        name="mix_backward",
    )(where, low, carry, a, g, pull, shard, twin, *flat)


def as_rows(value, lanes):
    count, size = value.shape
    lines = -(-size // lanes)
    return jnp.pad(value, ((0, 0), (0, lines * lanes - size))).reshape(count * lines, lanes)


def from_rows(rows, count, size):
    wide, lines, lanes = rows.shape
    value = rows.reshape(wide, count, lines // count * lanes)[:, :, :size]
    return value.transpose(1, 0, 2).reshape(count, wide * size)


def to_rows(value, wide, lanes):
    count, columns = value.shape
    size = columns // wide
    lines = -(-size // lanes)
    value = value.reshape(count, wide, size).transpose(1, 0, 2)
    return jnp.pad(value, ((0, 0), (0, 0), (0, lines * lanes - size))).reshape(wide, count * lines, lanes)


def split_rows(rows, sizes):
    pieces, start = [], 0
    for size in sizes:
        pieces.append(rows[..., start : start + size, :])
        start += size
    return pieces


def shards(
    narrow,
    wide,
    lengths,
    char_ids,
    char_counts,
    token_types,
    out_grad,
    char_table,
    conv_1,
    conv_2,
    conv_3,
    conv_4,
    conv_5,
    conv_6,
    conv_7,
    conv_bias,
    highway_weight,
    highway_bias,
    projection,
    position_table,
    type_table,
    embed_gain,
    embed_biases,
    qkv_weight,
    out_weight,
    ff_in,
    ff_in_bias,
    ff_out,
    layer_gains,
    layer_biases,
):
    convs = (conv_1, conv_2, conv_3, conv_4, conv_5, conv_6, conv_7)
    index = lax.axis_index("wide")
    place = lax.axis_index("narrow")
    where = jnp.stack([place, index // 2, index % 2]).astype(jnp.int32)
    lanes = conv_bias.shape[0]
    filters = lanes * wide
    model_width = embed_gain.shape[0] * wide
    vocab = char_table.shape[0] * wide // CDIM

    conv_block = jnp.concatenate([jnp.pad(k, ((0, TAP - k.shape[0]), (0, 0))) for k in convs], axis=1)
    model_rows = jnp.concatenate([type_table, embed_gain[None], embed_biases, layer_gains, layer_biases], axis=0)
    small = [
        conv_block,
        conv_bias[None],
        as_rows(highway_bias, lanes),
        as_rows(model_rows, lanes),
        as_rows(ff_in_bias[None], lanes),
        as_rows(char_table[None], lanes),
    ]
    small_sizes = [piece.shape[0] for piece in small]
    padding = -sum(small_sizes) % 16
    small_block = jnp.concatenate(small + [jnp.zeros((padding, lanes), jnp.bfloat16)], axis=0)
    everyone = lax.all_gather(small_block, "wide", axis=0, tiled=False)

    conv_rows, bias_rows, mix_rows, model_rows, inner_rows, table_rows = split_rows(everyone, small_sizes)
    top, start = [], 0
    for kernel in convs:
        size = kernel.shape[1]
        top.append(conv_rows[:, :, start : start + size].transpose(1, 0, 2).reshape(TAP, wide * size))
        start += size
    channels = [kernel.shape[1] * wide for kernel in convs]
    width_of = jnp.concatenate([jnp.full((1, count), k + 1, jnp.int32) for k, count in enumerate(channels)], axis=1)
    mask_rows = (width_of == lax.broadcasted_iota(jnp.int32, (KROWS - TAP - 1, 1), 0) + 1).astype(jnp.bfloat16)
    kern = jnp.concatenate([jnp.concatenate(top, axis=1), from_rows(bias_rows, 1, lanes), mask_rows], axis=0)
    highway_shift = from_rows(mix_rows, 2, highway_bias.shape[1]).astype(jnp.float32)
    vectors = from_rows(model_rows, 13, embed_gain.shape[0]).astype(jnp.float32)
    type_vectors, embed_gain_full, embed_shift = vectors[0:2], vectors[2], vectors[3:5]
    gain_rows, shift_rows = vectors[5:7], vectors[7:13]
    inner_shift = from_rows(inner_rows, 1, ff_in_bias.shape[0])[0].astype(jnp.float32)
    table = from_rows(table_rows, 1, char_table.shape[0]).reshape(vocab, CDIM)

    seq_count, seq_len, char_slots = char_ids.shape
    word_count = seq_count * seq_len
    counts = char_counts.reshape(word_count, 1)
    slots = lax.broadcasted_iota(jnp.int32, (1, char_slots), 1)
    ids = jnp.where(slots < counts, char_ids.reshape(word_count, char_slots), -1)
    row_keep = (
        (lax.broadcasted_iota(jnp.int32, (seq_count, seq_len), 1) < lengths[:, None])
        .astype(jnp.float32)
        .reshape(word_count, 1)
    )
    type_one = (token_types.reshape(word_count, 1) == 1).astype(jnp.float32)

    levels = levels_of(narrow)
    tables = table_turns(table)
    blocks = word_count // CONV_BLOCK

    def stacked_rows(pieces):
        value = jnp.concatenate(pieces, axis=0)
        return jnp.pad(value, ((0, -value.shape[0] % 16), (0, 0)))

    def side_by_side(value):
        return [value[:, i : i + model_width] for i in range(0, value.shape[1], model_width)]

    deep_one = stacked_rows([projection, position_table] + side_by_side(qkv_weight) + [out_weight])
    deep_two = stacked_rows(side_by_side(ff_in) + [ff_out])
    kern, mix_shards, deep_one, deep_two = tie(kern, highway_weight, deep_one, deep_two)
    chips = wide // 2
    stacks = [gather_chips(own_columns(mix_shards[number], place, narrow), wide) for number in range(2)]
    state = []
    for call in range(blocks):
        state = conv_forward(call, ids, counts, tables, kern, state)
    stacks[0], state, deep_one = tie(stacks[0], state, deep_one)
    known = [{0: other_chips(stacks[0], index // 2)}, None]
    spread_level(known[0], narrow, 1)
    windows, totals = state
    places = (jnp.maximum(counts - width_of, 0) + 1).astype(jnp.float32)
    pooled = jnp.log(totals / places)
    carried = gelu_curve(pooled)
    low_state = carried.astype(jnp.bfloat16)
    known[0], stacks[1], mix_shards, low_state, deep_one, deep_two = tie(
        known[0], stacks[1], mix_shards, low_state, deep_one, deep_two
    )
    for level in levels[1:]:
        spread_level(known[0], narrow, level)
    twin = core_swap(mix_shards, wide)
    full_one = lax.all_gather(deep_one, "wide", axis=0, tiled=False)
    full_two = lax.all_gather(deep_two, "wide", axis=0, tiled=False)
    known[0], twin, stacks[1] = tie(known[0], twin, stacks[1])
    other = swap_known(known[0], narrow, wide)
    known[1] = {0: other_chips(stacks[1], index // 2)}
    spread_level(known[1], narrow, 1)
    states, low_states, mixes, mixers = [], [], [], []

    def mix(number, carried, low_state, other):
        mine = [known[number][mask] for mask in range(narrow)]
        mixers.append((mine, other))
        low_states.append(low_state)
        states.append(carried)
        carried, low_state, mix_a, mix_g = mix_forward(
            number, where, low_state, carried, highway_shift[number][None], highway_weight, twin, mine, other
        )
        mixes.append((mix_a, mix_g))
        return carried, low_state

    carried, low_state = mix(0, carried, low_state, other)
    known[1], carried, low_state = tie(known[1], carried, low_state)
    for level in levels[1:]:
        spread_level(known[1], narrow, level)
    known[1], low_state = tie(known[1], low_state)
    carried, low_top = mix(1, carried, low_state, swap_known(known[1], narrow, wide))
    full_one, low_top = tie(full_one, low_top)

    def taken(full, sizes):
        pieces, start = [], 0
        for size in sizes:
            pieces.append(full[:, start : start + size].reshape(wide * size, model_width))
            start += size
        return pieces

    deep_rows = qkv_weight.shape[0]
    projection_full, position_full, *qkv_parts, out_full = taken(
        full_one, [projection.shape[0], position_table.shape[0]] + [deep_rows] * 4
    )
    qkv_full = jnp.concatenate(qkv_parts, axis=1)
    position_rows = jnp.tile(position_full.astype(jnp.float32), (seq_count, 1))
    embed_sum = (
        matmul(low_top, projection_full)
        + embed_shift[0]
        + position_rows
        + type_vectors[0] * (1.0 - type_one)
        + type_vectors[1] * type_one
    )
    embedded = normalize(embed_sum, embed_gain_full, embed_shift[1])
    low_in = embedded.astype(jnp.bfloat16)
    bias_full = jnp.concatenate([shift_rows[0], jnp.zeros_like(shift_rows[0]), shift_rows[1]])
    projected = (matmul(low_in, qkv_full) + bias_full).astype(jnp.bfloat16)
    proj_seqs = projected.reshape(seq_count, seq_len, -1)
    context_seqs, log_totals = lax.map(lambda seq_pair: attend(seq_pair[0], seq_pair[1]), (proj_seqs, lengths))
    context = context_seqs.reshape(word_count, -1)
    full_two, context = tie(full_two, context)
    position_rows = jnp.tile(position_full.astype(jnp.float32), (seq_count, 1))
    embed_sum = (
        matmul(low_top, projection_full)
        + embed_shift[0]
        + position_rows
        + type_vectors[0] * (1.0 - type_one)
        + type_vectors[1] * type_one
    )
    embedded = normalize(embed_sum, embed_gain_full, embed_shift[1])
    low_in = embedded.astype(jnp.bfloat16)
    bias_full = jnp.concatenate([shift_rows[0], jnp.zeros_like(shift_rows[0]), shift_rows[1]])
    projected = (matmul(low_in, qkv_full) + bias_full).astype(jnp.bfloat16)
    proj_seqs = projected.reshape(seq_count, seq_len, -1)
    context_seqs, log_totals = lax.map(lambda seq_pair: attend(seq_pair[0], seq_pair[1]), (proj_seqs, lengths))
    context = context_seqs.reshape(word_count, -1)
    full_two, context = tie(full_two, context)
    *inner_parts, ff_out_full = taken(full_two, [deep_rows] * (ff_in.shape[1] // model_width) + [ff_out.shape[0]])
    ff_in_full = jnp.concatenate(inner_parts, axis=1)
    first_in = embedded + matmul(context, out_full) + shift_rows[2]
    first_out = normalize(first_in, gain_rows[0], shift_rows[3])
    low_first = first_out.astype(jnp.bfloat16)
    inner_pre = matmul(low_first, ff_in_full) + inner_shift
    activated = gelu_curve(inner_pre).astype(jnp.bfloat16)
    second_in = first_out + matmul(activated, ff_out_full) + shift_rows[4]
    final_out = normalize(second_in, gain_rows[1], shift_rows[5])
    hidden_out = (final_out * row_keep).reshape(seq_count, seq_len, -1)

    grad_top = out_grad.reshape(word_count, -1).astype(jnp.float32) * row_keep
    norm_pull = jax.vjp(normalize, second_in, gain_rows[1], shift_rows[5])[1]
    grad_second, grad_gain_two, grad_shift_five = norm_pull(grad_top)
    grad_ffn = grad_second.astype(jnp.bfloat16)
    grad_shift_four = jnp.sum(grad_ffn, axis=0, dtype=jnp.float32)
    weight_ff_out = matmul(activated, grad_ffn, CONTRACT_ROWS)
    grad_inner = (matmul(grad_ffn, ff_out_full, CONTRACT_COLS) * gelu_slope(inner_pre)).astype(jnp.bfloat16)
    grad_ff_bias = jnp.sum(grad_inner, axis=0, dtype=jnp.float32)
    weight_ff_in = matmul(low_first, grad_inner, CONTRACT_ROWS)
    grad_first = grad_second + matmul(grad_inner, ff_in_full, CONTRACT_COLS)
    norm_pull = jax.vjp(normalize, first_in, gain_rows[0], shift_rows[3])[1]
    grad_res, grad_gain_one, grad_shift_three = norm_pull(grad_first)
    grad_attn = grad_res.astype(jnp.bfloat16)
    grad_shift_two = jnp.sum(grad_attn, axis=0, dtype=jnp.float32)
    weight_out = matmul(context, grad_attn, CONTRACT_ROWS)
    grad_context = matmul(grad_attn, out_full, CONTRACT_COLS).astype(jnp.bfloat16)
    grad_seqs = lax.map(
        lambda seq_quad: attend_back(seq_quad[0], seq_quad[1], seq_quad[2], seq_quad[3]),
        (proj_seqs, log_totals, grad_context.reshape(seq_count, seq_len, -1), lengths),
    )
    grad_proj = grad_seqs.reshape(word_count, -1)
    grad_shift_zero = jnp.sum(grad_proj[:, :model_width], axis=0, dtype=jnp.float32)
    grad_shift_one = jnp.sum(grad_proj[:, 2 * model_width :], axis=0, dtype=jnp.float32)
    weight_qkv = matmul(low_in, grad_proj, CONTRACT_ROWS)
    grad_embedded = grad_res + matmul(grad_proj, qkv_full, CONTRACT_COLS)
    norm_pull = jax.vjp(normalize, embed_sum, embed_gain_full, embed_shift[1])[1]
    grad_sum, grad_embed_gain, grad_embed_shift = norm_pull(grad_embedded)
    grad_embed = grad_sum.astype(jnp.bfloat16)
    grad_embed_zero = jnp.sum(grad_embed, axis=0, dtype=jnp.float32)
    grad_position = jnp.sum(grad_embed.reshape(seq_count, seq_len, -1), axis=0, dtype=jnp.float32)
    type_mask = type_one.astype(jnp.bfloat16)
    grad_type_one = jnp.sum(grad_embed * type_mask, axis=0, dtype=jnp.float32)
    grad_type_zero = jnp.sum(grad_embed * (1 - type_mask), axis=0, dtype=jnp.float32)
    weight_proj = matmul(low_top, grad_embed, CONTRACT_ROWS)
    grad_carry = matmul(grad_embed, projection_full, CONTRACT_COLS)

    def deep(value):
        rows = value.shape[0] // wide
        value = value.astype(jnp.bfloat16).reshape(wide, rows, value.shape[1])
        return [value[:, :, i : i + model_width] for i in range(0, value.shape[2], model_width)]

    def reduce_wide(values):
        parts = [deep(value) for value in values]
        total = lax.psum_scatter(jnp.concatenate([p for part in parts for p in part], axis=1), "wide", scatter_dimension=0)
        return total, [[p.shape[1] for p in part] for part in parts]

    def split_deep(total, sizes):
        values, start = [], 0
        for part in sizes:
            pieces = []
            for size in part:
                pieces.append(total[start : start + size])
                start += size
            values.append(jnp.concatenate(pieces, axis=1).astype(jnp.float32))
        return values

    first_sum, first_sizes = reduce_wide([weight_ff_out, weight_ff_in])

    shift_high, weight_high = [None, None], [None, None]

    def unmix(number, pull):
        mix_a, mix_g = mixes[number]
        own_part, other_part, shift_grad, back = mix_backward(
            number, where, low_states[number], states[number], mix_a, mix_g, pull, highway_weight, twin, *mixers[number]
        )
        shift_high[number] = shift_grad.reshape(2 * filters)
        return own_part, other_part, back


    def begun(own_part, got):
        return [(own_part[:, half], got[:, half]) for half in range(2)]

    def send_home(terms):
        blocks = [add_low(parts[0], arrived[0]).reshape(chips, -1, parts.shape[-1]) for parts, arrived in terms]
        return lax.psum_scatter(
            jnp.stack(blocks, axis=1), "wide", scatter_dimension=0, axis_index_groups=chip_groups(wide)
        )

    def laid_out(totals):
        pieces = []
        for half in range(2):
            table = jnp.stack([totals[mask][half] for mask in range(narrow)])
            for block in range(narrow):
                pieces.append(lax.dynamic_index_in_dim(table, place ^ block, 0, keepdims=False))
        return jnp.concatenate(pieces, axis=1).astype(jnp.float32)

    def convolve_back(first, last, state):
        for call in range(first, last):
            state = conv_backward(call, ids.T, windows, scaled, kern, state)
        return state

    rounds = range(narrow.bit_length() - 1)
    rounds = range(narrow.bit_length() - 1)
    own_one, other_one, pull = unmix(1, grad_carry)
    got_one = core_swap(other_one, wide)
    second_parts = [weight_out.astype(jnp.bfloat16), weight_qkv.astype(jnp.bfloat16), weight_proj.astype(jnp.bfloat16)]
    got_one, second_parts, pull = tie(got_one, second_parts, pull)
    second_sum, second_sizes = reduce_wide(second_parts + [grad_position])
    terms_one = collect_round(begun(own_one, got_one), narrow, 0)
    staying = [parts for parts, _ in terms_one]
    staying, pull = tie(staying, pull)
    own_zero, other_zero, pull = unmix(0, pull)
    terms_one, own_zero, other_zero, pull = tie(
        [(parts, sent) for parts, (_, sent) in zip(staying, terms_one)], own_zero, other_zero, pull
    )
    got_zero = core_swap(other_zero, wide)
    for turn in rounds[1:]:
        terms_one = collect_round(terms_one, narrow, turn)
    scaled = pull * gelu_slope(pooled) / totals
    terms_one, got_zero, scaled = tie(terms_one, got_zero, scaled)
    home_one = send_home(terms_one)
    terms_zero = collect_round(begun(own_zero, got_zero), narrow, 0)
    state = [jnp.zeros(kern.shape, jnp.float32), jnp.zeros((VROWS, 128), jnp.float32)]
    state = convolve_back(0, blocks // 2, state)
    state, terms_zero = tie(state, terms_zero)
    for turn in rounds[1:]:
        terms_zero = collect_round(terms_zero, narrow, turn)
    state = convolve_back(blocks // 2, blocks * 3 // 4, state)
    state, terms_zero, first_sum, second_sum = tie(state, terms_zero, first_sum, second_sum)
    home_zero = send_home(terms_zero)
    deep_sum = jnp.concatenate([first_sum, second_sum], axis=0)
    deep_half = deep_sum.shape[0] // 2

    def swap_axis(value, turn):
        return [
            hop(value[half * deep_half : (half + 1) * deep_half], narrow, bits_of(narrow, half)[turn]) for half in range(2)
        ]

    def add_swapped(value, arrived):
        return add_low(value, jnp.concatenate(arrived, axis=0))

    arrived = swap_axis(deep_sum, 0)
    state = convolve_back(blocks * 3 // 4, blocks, state)
    state, home_one, deep_sum, arrived = tie(state, home_one, deep_sum, arrived)
    total_one = {0: home_one}
    spread_level(total_one, narrow, 1)
    deep_sum = add_swapped(deep_sum, arrived)
    arrived = swap_axis(deep_sum, 1)
    kern_grad, table_grad = state
    table_grad = table_grad[:vocab].reshape(vocab, 8, CDIM).sum(axis=1)
    conv_rows, start = [], 0
    for count in channels:
        part = kern_grad[:TAP, start : start + count].reshape(TAP, wide, count // wide)
        conv_rows.append(part.transpose(1, 0, 2))
        start += count
    model_grads = jnp.stack(
        [
            grad_type_zero,
            grad_type_one,
            grad_embed_gain,
            grad_embed_zero,
            grad_embed_shift,
            grad_gain_one,
            grad_gain_two,
            grad_shift_zero,
            grad_shift_one,
            grad_shift_two,
            grad_shift_three,
            grad_shift_four,
            grad_shift_five,
        ]
    )
    small = [
        jnp.concatenate(conv_rows, axis=2),
        to_rows(kern_grad[TAP : TAP + 1], wide, lanes),
        to_rows(jnp.stack(shift_high), wide, lanes),
        to_rows(model_grads, wide, lanes),
        to_rows(grad_ff_bias[None], wide, lanes),
        to_rows(table_grad.reshape(1, -1), wide, lanes),
        jnp.zeros((wide, padding, lanes), jnp.float32),
    ]
    small_part = jnp.concatenate(small, axis=1).astype(jnp.bfloat16).reshape(chips, 2, -1, lanes)

    def exchange(value, at, bit):
        side = (index // bit) % 2
        got = lax.ppermute(
            lax.dynamic_index_in_dim(value, 1 - side, at, keepdims=False), "wide", [(i, i ^ bit) for i in range(wide)]
        )
        return lax.dynamic_index_in_dim(value, side, at, keepdims=False), got

    kept, got = exchange(small_part, 1, 1)
    got, total_one, home_zero, deep_sum, arrived = tie(got, total_one, home_zero, deep_sum, arrived)
    deep_sum = add_swapped(deep_sum, arrived)
    for turn in rounds[2:]:
        deep_sum = add_swapped(deep_sum, swap_axis(deep_sum, turn))
    total_zero = {0: home_zero}
    spread_level(total_zero, narrow, 1)
    for level in levels[1:]:
        spread_level(total_one, narrow, level)
    small_sum = add_low(kept, got)
    bit = wide // 2
    while bit > 1:
        kept, got = exchange(small_sum.reshape(2, -1, *small_sum.shape[1:]), 0, bit)
        small_sum = add_low(kept, got)
        bit //= 2
    total_zero, small_sum = tie(total_zero, small_sum)
    for level in levels[1:]:
        spread_level(total_zero, narrow, level)
    small_sum = small_sum[0].astype(jnp.float32)
    for bit in bits_of(narrow, 0):
        small_sum = small_sum + hop(small_sum.astype(jnp.bfloat16), narrow, bit).astype(jnp.float32)
    weight_high = [laid_out(total_zero), laid_out(total_one)]
    grad_ff_out_sum, grad_ff_in_sum = split_deep(deep_sum[: first_sum.shape[0]], first_sizes)
    grad_out_sum, grad_qkv_sum, grad_projection_sum, grad_position_sum = split_deep(
        deep_sum[first_sum.shape[0] :], second_sizes
    )
    conv_sum, bias_sum, mix_sum, model_sum, inner_sum, table_sum = split_rows(small_sum, small_sizes)
    conv_grads, start = [], 0
    for kernel in convs:
        conv_grads.append(conv_sum[: kernel.shape[0], start : start + kernel.shape[1]])
        start += kernel.shape[1]
    mix_sum = from_rows(mix_sum[None], 2, highway_bias.shape[1])
    model_sum = from_rows(model_sum[None], 13, embed_gain.shape[0])
    return (
        hidden_out,
        from_rows(table_sum[None], 1, char_table.shape[0])[0],
        *conv_grads,
        bias_sum[0],
        jnp.stack(weight_high),
        mix_sum,
        grad_projection_sum,
        grad_position_sum,
        model_sum[0:2],
        model_sum[2],
        model_sum[3:5],
        grad_qkv_sum,
        grad_out_sum,
        grad_ff_in_sum,
        from_rows(inner_sum[None], 1, ff_in_bias.shape[0])[0],
        grad_ff_out_sum,
        model_sum[5:7],
        model_sum[7:13],
    )


def solution(mesh):
    in_specs = (
        P(("narrow", "wide")),
        P(("narrow", "wide"), None, None),
        P(("narrow", "wide"), None),
        P(("narrow", "wide"), None),
        P(("narrow", "wide"), None, None),
        P("wide"),
        P(None, "wide"),
        P(None, "wide"),
        P(None, "wide"),
        P(None, "wide"),
        P(None, "wide"),
        P(None, "wide"),
        P(None, "wide"),
        P("wide"),
        P(None, "wide", None),
        P(None, "wide"),
        P("wide", None),
        P("wide", None),
        P(None, "wide"),
        P("wide"),
        P(None, "wide"),
        P("wide", None),
        P("wide", None),
        P("wide", None),
        P("wide"),
        P("wide", None),
        P(None, "wide"),
        P(None, "wide"),
    )
    out_specs = (
        P(("narrow", "wide"), None, None),
        P("wide"),
        P(None, "wide"),
        P(None, "wide"),
        P(None, "wide"),
        P(None, "wide"),
        P(None, "wide"),
        P(None, "wide"),
        P(None, "wide"),
        P("wide"),
        P(None, "wide", None),
        P(None, "wide"),
        P("wide", None),
        P("wide", None),
        P(None, "wide"),
        P("wide"),
        P(None, "wide"),
        P("wide", None),
        P("wide", None),
        P("wide", None),
        P("wide"),
        P("wide", None),
        P(None, "wide"),
        P(None, "wide"),
    )
    run = functools.partial(shards, mesh.shape["narrow"], mesh.shape["wide"])
    return jax.shard_map(run, mesh=mesh, in_specs=in_specs, out_specs=out_specs, check_vma=False)
```

time: 1630 us -> 827 us (0.51)
  matrix products: 440 us -> 72.3 us
  blocking collectives: 360 us -> 16.6 us
  Pallas kernels: 0 us -> 247 us
  waiting for transfers between devices: 407 us -> 179 us
  other arithmetic: 238 us -> 97.2 us
  starting transfers between devices: 1.51 us -> 36.4 us
    all_gather x15 -> x1, blocking collectives: 274 us -> 16.6 us  [shards(): everyone = lax.all_gather(small_block, 'wide', axis=0, tiled=False)]
    pallas_call x0 -> x12, Pallas kernels: none -> 247 us  [the longest x4 96.8 us: conv_backward(): pl.pallas_call(functools.partial(conv_bwd_body, block, filters), grid=(1,...]
    unnamed x32 -> x8, waiting for transfers between devices: 247 us -> 0.13 us
    dot_general x62 -> x0, matrix products: 230 us -> none  [the longest x28 139 us: convolve(): jnp.einsum('kh,pkw->phw', kernel_flat, stacked, preferred_element_type=jn...]
    dot_general x21 -> x15, matrix products: 185 us -> 49.2 us  [matmul(): lax.dot_general(left, right, dims, preferred_element_type=jnp.float32)]
    ppermute x0 -> x38, waiting for transfers between devices: none -> 127 us  [the longest x30 104 us: hop(): return lax.ppermute(value, 'narrow', [(i, i ^ bit) for i in range(narrow)])]
    psum x1 -> x0, waiting for transfers between devices: 117 us -> none  [sum_embed(): lax.psum(shares[9].astype(jnp.bfloat16), 'narrow').astype(jnp.float32)]
    reduce_sum x15 -> x1, other arithmetic: 111 us -> 0.02 us  [shards(): table_grad = table_grad[:vocab].reshape(vocab, 8, CDIM).sum(axis=1)]
  transfers between devices with their start and end apart: 23 -> 46, of which waited for: 11 -> 21; matrix products, arithmetic and copies ran while one was open for 45% -> 24% of each run, Pallas kernels for 0% -> 30%
where the time goes in v1:
time: 827 us; the launch traced here: 819 us
  Pallas kernels  247 us (30%)
  waiting for transfers between devices  179 us (22%)
  local copies, waits for them, and re-layouts  153 us (19%)
  other arithmetic  97.2 us (12%)
  matrix products  72.3 us (9%)
  starting transfers between devices  36.4 us (4%)
  between operations  17.6 us (2%)
  blocking collectives  16.6 us (2%)
    ppermute x30, waiting for transfers between devices, hop(): return lax.ppermute(value, 'narrow', [(i, i ^ bit) for i in range(narrow)])  104 us
    pallas_call x4, Pallas kernels, conv_backward(): pl.pallas_call(functools.partial(conv_bwd_body, block, filters), grid=(1,...  96.8 us
    unnamed x242, local copies, waits for them, and re-layouts  85.6 us
    pallas_call x2, Pallas kernels, mix_backward(): pl.pallas_call(functools.partial(mix_backward_body, narrow, layer), grid_...  69.3 us
    dot_general x15, matrix products, matmul(): lax.dot_general(left, right, dims, preferred_element_type=jnp.float32)  49.2 us
    pallas_call x4, Pallas kernels, conv_forward(): pl.pallas_call(functools.partial(conv_fwd_body, block, filters, len(state...  43.9 us
    pallas_call x2, Pallas kernels, mix_forward(): pl.pallas_call(functools.partial(mix_forward_body, narrow, layer), grid_s...  37.5 us
    convert_element_type x19, other arithmetic, add_low(): (left.astype(jnp.float32) + right.astype(jnp.float32)).astype(jnp.bfloat16)  36.4 us
  transfers between devices with their start and end apart: 46, of which 21 were waited for; matrix products, arithmetic and copies ran while one was open for 24% of the time, Pallas kernels for 30%

profile of v1, /device:TPU:0, one launch (start us, length us, event | category | flops | bytes accessed | tf_op | source)
XLA Modules:
  0.0 819.0 jit_solution(12517833774886778711)
XLA Ops:
  17.6 16.6 %all-gather = bf16[1152,256]{1,0:T(8,128)(2,1)S(1)} all-gather(bf16[144,256]{1,0:T(8,128)(2,1)S(1)} %concatenate.105), channel_id=2, replica_groups=mesh['narrow'=4,'wide'=8] {'wide'}, dimensions={0}, use_global_device_ids=true | all-gather | bytes 663552 | tf_op jit(solution)/shard_map/all_gather | solution.py:671
  47.5 3.9 fusion.69
  57.7 11.0 %conv_forward.4 = (bf16[25600,128]{1,0:T(8,128)(2,1)S(1)}, f32[512,2048]{1,0:T(8,128)S(1)}) custom-call(s32[512,50]{1,0:T(8,128)S(1)} %copy.270.ids_ref, s32[512,1]{1,0:T(8,128)S(1)} %copy.271.cnt_ref, bf16[8,384,128]{2,1,0:T(8,128)(2,1)S(1)} %constant_dynamic-update-slice_fusion.4.table_ref, bf16[128,2048]{1,0:T(8,128)(2,1)S(1)} %pad_maximum_fusion.19.kern_ref), custom_call_target="tpu_custom_call" | custom-call | flops 419430400 | bytes 262144 | tf_op jit(solution)/shard_map/conv_forward/pallas_call | solution.py:116
  68.7 10.8 %conv_forward.5 = (bf16[25600,128]{1,0:T(8,128)(2,1)S(1)}, f32[512,2048]{1,0:T(8,128)S(1)}) custom-call(s32[512,50]{1,0:T(8,128)S(1)} %copy.270.ids_ref, s32[512,1]{1,0:T(8,128)S(1)} %copy.271.cnt_ref, bf16[8,384,128]{2,1,0:T(8,128)(2,1)S(1)} %constant_dynamic-update-slice_fusion.4.table_ref, ...), custom_call_target="tpu_custom_call", output_to_operand_aliasing={{0}: (4, {}), {1}: (5, {})} | custom-call | flops 419430400 | bytes 262144 | tf_op jit(solution)/shard_map/conv_forward/pallas_call | solution.py:116
  79.5 10.8 %conv_forward.6 = (bf16[25600,128]{1,0:T(8,128)(2,1)S(1)}, f32[512,2048]{1,0:T(8,128)S(1)}) custom-call(s32[512,50]{1,0:T(8,128)S(1)} %copy.270.ids_ref, s32[512,1]{1,0:T(8,128)S(1)} %copy.271.cnt_ref, bf16[8,384,128]{2,1,0:T(8,128)(2,1)S(1)} %constant_dynamic-update-slice_fusion.4.table_ref, ...), custom_call_target="tpu_custom_call", output_to_operand_aliasing={{0}: (4, {}), {1}: (5, {})} | custom-call | flops 419430400 | bytes 262144 | tf_op jit(solution)/shard_map/conv_forward/pallas_call | solution.py:116
  90.4 11.3 %conv_forward.7 = (bf16[25600,128]{1,0:T(8,128)(2,1)S(1)}, f32[512,2048]{1,0:T(8,128)S(1)}) custom-call(s32[512,50]{1,0:T(8,128)S(1)} %copy.270.ids_ref, s32[512,1]{1,0:T(8,128)S(1)} %copy.271.cnt_ref, bf16[8,384,128]{2,1,0:T(8,128)(2,1)S(1)} %constant_dynamic-update-slice_fusion.4.table_ref, ...), custom_call_target="tpu_custom_call", output_to_operand_aliasing={{0}: (4, {}), {1}: (5, {})} | custom-call | flops 419430400 | bytes 262144 | tf_op jit(solution)/shard_map/conv_forward/pallas_call | solution.py:116
  101.6 2.6 copy-done
  111.2 4.2 fusion.66
  115.4 32.9 %all-gather.12.cloned.1.call-done = bf16[8,256,512]{2,1,0:T(8,128)(2,1)} async-done(((bf16[2,256,512]{2,1,0:T(8,128)(2,1)}), bf16[8,256,512]{2,1,0:T(8,128)(2,1)}) %all-gather.12.cloned.1.call-update) | async-done | bytes 2097168 | tf_op jit(solution)/shard_map/all_gather | solution.py:383
  153.8 17.0 %collective-permute-done.3.rest_4_ = bf16[768,512]{1,0:T(8,128)(2,1)S(1)} collective-permute-done((bf16[768,512]{1,0:T(8,128)(2,1)S(1)}, bf16[768,512]{1,0:T(8,128)(2,1)S(1)}, u32[]{:S(2)}, u32[]{:S(2)}) %collective-permute-start.3) | collective-permute-done | bytes 786464 | tf_op jit(solution)/shard_map/ppermute | solution.py:314
  173.0 5.1 pad_maximum_fusion
  183.9 4.7 collective-permute-done.7.rest_5_
  189.7 18.6 %mix_forward.2 = (f32[512,2048]{1,0:T(8,128)}, bf16[512,2048]{1,0:T(8,128)(2,1)}, f32[512,2048]{1,0:T(8,128)}, f32[512,2048]{1,0:T(8,128)}) custom-call(s32[3]{0:T(128)S(1)} %pad_add_fusion.where_ref, bf16[512,2048]{1,0:T(8,128)(2,1)} %get-tuple-element.214.low_ref, f32[512,2048]{1,0:T(8,128)} %get-tuple-element.452.carry_ref, f32[1,4096]{1,0:T(1,128)S(1)} %bitcast.306, ...), custom_call_target="tpu_custom_call" | custom-call | flops 2147483648 | bytes 4194304 | tf_op jit(solution)/shard_map/mix_forward/pallas_call | solution.py:477
  208.3 9.8 %collective-permute-done.6.rest_2_ = bf16[2,768,512]{2,1,0:T(8,128)(2,1)} collective-permute-done((bf16[2,768,512]{2,1,0:T(8,128)(2,1)}, bf16[2,768,512]{2,1,0:T(8,128)(2,1)}, u32[]{:S(2)}, u32[]{:S(2)}) %collective-permute-start.6) | collective-permute-done | bytes 1572896 | tf_op jit(solution)/shard_map/ppermute | solution.py:314
  222.8 17.8 %collective-permute-done.9.rest_4_ = bf16[768,512]{1,0:T(8,128)(2,1)S(1)} collective-permute-done((bf16[768,512]{1,0:T(8,128)(2,1)S(1)}, bf16[768,512]{1,0:T(8,128)(2,1)S(1)}, u32[]{:S(2)}, u32[]{:S(2)}) %collective-permute-start.9) | collective-permute-done | bytes 786464 | tf_op jit(solution)/shard_map/ppermute | solution.py:314
  241.0 6.4 pad_maximum_fusion.1
  250.8 7.0 collective-permute-done.10.rest_5_
  257.9 18.9 %mix_forward.3 = (f32[512,2048]{1,0:T(8,128)}, bf16[512,2048]{1,0:T(8,128)(2,1)}, f32[512,2048]{1,0:T(8,128)}, f32[512,2048]{1,0:T(8,128)}) custom-call(s32[3]{0:T(128)S(1)} %pad_add_fusion.where_ref, bf16[512,2048]{1,0:T(8,128)(2,1)} %get-tuple-element.227.low_ref, f32[512,2048]{1,0:T(8,128)} %get-tuple-element.228.carry_ref, f32[1,4096]{1,0:T(1,128)S(1)} %bitcast.304, ...), custom_call_target="tpu_custom_call" | custom-call | flops 2147483648 | bytes 4194304 | tf_op jit(solution)/shard_map/mix_forward/pallas_call | solution.py:477
  288.6 3.6 fusion.11
  292.2 3.1 copy.272
  295.2 3.0 fusion.81
  300.1 2.7 copy-done.17
  302.8 3.2 fusion.34
  306.0 18.8 %all-gather.16.cloned.1.call-done = bf16[6144,768]{1,0:T(8,128)(2,1)} async-done(((bf16[768,768]{1,0:T(8,128)(2,1)}), bf16[6144,768]{1,0:T(8,128)(2,1)}) %all-gather.16.cloned.1.call-update) | async-done | bytes 9437200 | tf_op jit(solution)/shard_map/all_gather | solution.py:736
  324.8 2.8 slice.672
  334.9 5.6 multiply_convert_fusion.1
  340.5 2.8 fusion.83
  349.6 2.9 convolution_convert_fusion.1
  352.6 6.9 fusion.84
  359.5 3.5 convolution_convert_fusion
  363.1 2.5 constant_dynamic-update-slice_fusion.12
  370.1 7.6 multiply_reduce_fusion.1
  382.3 2.3 copy.274
  384.7 10.9 %multiply_reduce_fusion = (f32[12,512]{1,0:T(8,128)S(1)}, f32[12,512,512]{1,2,0:T(8,128)}) fusion(f32[12,512,512]{1,2,0:T(8,128)} %copy-done.17, f32[12,512]{1,0:T(8,128)S(1)} %log_add_fusion, bf16[512,12,64]{0,2,1:T(8,128)(2,1)} %bitcast.333, bf16[512,3,12,64]{0,3,2,1:T(8,128)(2,1)S(1)} %bitcast.312), kind=kOutput, calls=%fused_computation.1 | convolution fusion | flops 412084224 | bytes 26796032 | tf_op jit(solution)/shard_map/while/body/eval_jaxpr/qhe,khe->hqk/dot_general | solution.py:279
  397.7 7.4 multiply_convert_fusion
  414.3 2.7 multiply_reduce_fusion.2
  419.0 3.9 fusion.85.pull_ref
  422.9 34.7 %mix_backward.2 = (bf16[4,2,1024,512]{3,2,1,0:T(8,128)(2,1)}, bf16[4,2,1024,512]{3,2,1,0:T(8,128)(2,1)}, f32[2,1,2048]{2,1,0:T(1,128)}, f32[512,2048]{1,0:T(8,128)}) custom-call(s32[3]{0:T(128)} %copy-done.16, bf16[512,2048]{1,0:T(8,128)(2,1)} %get-tuple-element.227.low_ref, f32[512,2048]{1,0:T(8,128)} %get-tuple-element.228.carry_ref, ...), custom_call_target="tpu_custom_call" | custom-call | flops 2147483648 | bytes 4194304 | tf_op jit(solution)/shard_map/mix_backward/pallas_call | solution.py:554
  463.4 7.6 collective-permute-done.11
  479.8 2.6 slice_bitcast_fusion.1
  482.4 2.4 copy-done.25
  484.8 3.5 fusion.18
  495.8 34.6 %mix_backward.3 = (bf16[4,2,1024,512]{3,2,1,0:T(8,128)(2,1)}, bf16[4,2,1024,512]{3,2,1,0:T(8,128)(2,1)}, f32[2,1,2048]{2,1,0:T(1,128)}, f32[512,2048]{1,0:T(8,128)}) custom-call(s32[3]{0:T(128)} %copy-done.16, bf16[512,2048]{1,0:T(8,128)(2,1)} %get-tuple-element.214.low_ref, f32[512,2048]{1,0:T(8,128)} %get-tuple-element.452.carry_ref, ...), custom_call_target="tpu_custom_call" | custom-call | flops 2147483648 | bytes 4194304 | tf_op jit(solution)/shard_map/mix_backward/pallas_call | solution.py:554
  530.4 8.2 collective-permute-done.13
  539.8 2.3 add_convert_fusion.20
  549.4 4.7 fusion.16.ginv_ref
  554.1 13.7 %collective-permute-done.14 = bf16[1,1024,512]{2,1,0:T(8,128)(2,1)S(1)} collective-permute-done((bf16[1,1024,512]{2,1,0:T(8,128)(2,1)S(1)}, bf16[1,1024,512]{2,1,0:T(8,128)(2,1)S(1)}, u32[]{:S(2)}, u32[]{:S(2)}) %collective-permute-start.14) | collective-permute-done | bytes 1048608 | tf_op jit(solution)/shard_map/ppermute | solution.py:314
  569.9 2.5 slice_bitcast_fusion.2
  572.4 2.9 add_convert_fusion.2
  576.7 3.5 fusion.20
  584.0 2.9 copy-done.1
  589.1 24.1 %conv_backward.4 = (f32[128,2048]{1,0:T(8,128)S(1)}, f32[272,128]{1,0:T(8,128)S(1)}) custom-call(s32[50,512]{1,0:T(8,128)S(1)} %get-tuple-element.516.idst_ref, bf16[25600,128]{1,0:T(8,128)(2,1)S(1)} %copy-done.1, f32[512,2048]{1,0:T(8,128)S(1)} %copy-done.7, ...), custom_call_target="tpu_custom_call", output_to_operand_aliasing={{0}: (4, {}), {1}: (5, {})} | custom-call | flops 838860800 | bytes 262144 | tf_op jit(solution)/shard_map/conv_backward/pallas_call | solution.py:209
  613.2 24.1 %conv_backward.5 = (f32[128,2048]{1,0:T(8,128)S(1)}, f32[272,128]{1,0:T(8,128)S(1)}) custom-call(s32[50,512]{1,0:T(8,128)S(1)} %get-tuple-element.516.idst_ref, bf16[25600,128]{1,0:T(8,128)(2,1)S(1)} %copy-done.1, f32[512,2048]{1,0:T(8,128)S(1)} %copy-done.7, ...), custom_call_target="tpu_custom_call", output_to_operand_aliasing={{0}: (4, {}), {1}: (5, {})} | custom-call | flops 838860800 | bytes 262144 | tf_op jit(solution)/shard_map/conv_backward/pallas_call | solution.py:209
  637.3 2.8 fusion.19
  640.2 3.2 add_convert_fusion.16
  644.3 3.4 add_convert_fusion.14
  648.4 2.9 copy-done.2
  653.5 24.3 %conv_backward.6 = (f32[128,2048]{1,0:T(8,128)S(1)}, f32[272,128]{1,0:T(8,128)S(1)}) custom-call(s32[50,512]{1,0:T(8,128)S(1)} %get-tuple-element.516.idst_ref, bf16[25600,128]{1,0:T(8,128)(2,1)S(1)} %copy-done.2, f32[512,2048]{1,0:T(8,128)S(1)} %copy-done.8, ...), custom_call_target="tpu_custom_call", output_to_operand_aliasing={{0}: (4, {}), {1}: (5, {})} | custom-call | flops 838860800 | bytes 262144 | tf_op jit(solution)/shard_map/conv_backward/pallas_call | solution.py:209
  692.6 2.9 copy-done.3
  697.7 24.3 %conv_backward.7 = (f32[128,2048]{1,0:T(8,128)S(1)}, f32[272,128]{1,0:T(8,128)S(1)}) custom-call(s32[50,512]{1,0:T(8,128)S(1)} %get-tuple-element.516.idst_ref, bf16[25600,128]{1,0:T(8,128)(2,1)S(1)} %copy-done.3, f32[512,2048]{1,0:T(8,128)S(1)} %copy-done.9, ...), custom_call_target="tpu_custom_call", output_to_operand_aliasing={{0}: (4, {}), {1}: (5, {})} | custom-call | flops 838860800 | bytes 262144 | tf_op jit(solution)/shard_map/conv_backward/pallas_call | solution.py:209
  722.1 2.6 add_convert_fusion.1
  737.1 25.9 %collective-permute-done.25 = bf16[2,256,512]{2,1,0:T(8,128)(2,1)} collective-permute-done((bf16[2,256,512]{2,1,0:T(8,128)(2,1)}, bf16[2,256,512]{2,1,0:T(8,128)(2,1)}, u32[]{:S(2)}, u32[]{:S(2)}) %collective-permute-start.25) | collective-permute-done | bytes 524320 | tf_op jit(solution)/shard_map/ppermute | solution.py:314
  782.9 2.4 collective-permute-done.37
  807.8 3.9 maximum_convert_fusion
  (588 shorter events, 223.1 us)
Async XLA Ops:
  7.2 99.1 %all-gather.10.cloned.1.call-start = ((), (), s32[]{:S(2)}) async-start(), calls=%async_computation.8 | async-start | bytes 2621440 | tf_op jit(solution)/shard_map/all_gather | solution.py:383
  34.2 22.1 %copy-start.22 = (bf16[1152,256]{1,0:T(8,128)(2,1)}, bf16[1152,256]{1,0:T(8,128)(2,1)S(1)}, u32[]{:S(2)}) copy-start(bf16[1152,256]{1,0:T(8,128)(2,1)S(1)} %all-gather) | copy-start | bytes 1769476
  34.9 8.7 %copy-start.61 = (bf16[96,3072]{1,0:T(8,128)(2,1)S(1)}, bf16[96,3072]{1,0:T(8,128)(2,1)}, u32[]{:S(2)}) copy-start(bf16[96,3072]{1,0:T(8,128)(2,1)} %param.51) | copy-start | bytes 1769476
  35.4 9.1 %copy-start.63 = (bf16[96,768]{1,0:T(8,128)(2,1)S(1)}, bf16[96,768]{1,0:T(8,128)(2,1)}, u32[]{:S(2)}) copy-start(bf16[96,768]{1,0:T(8,128)(2,1)} %param.50) | copy-start | bytes 442372
  54.2 94.1 %all-gather.12.cloned.1.call-start = ((), (), s32[]{:S(2)}) async-start(), calls=%async_computation.9 | async-start | bytes 2621440 | tf_op jit(solution)/shard_map/all_gather | solution.py:383
  56.1 220.7 %all-gather.14.cloned.1.call-start = ((), (), s32[]{:S(2)}) async-start(), calls=%async_computation.10 | async-start | bytes 9732096 | tf_op jit(solution)/shard_map/all_gather | solution.py:735
  108.1 80.5 %copy-start.10 = (bf16[2,768,512]{2,1,0:T(8,128)(2,1)}, bf16[2,768,512]{2,1,0:T(8,128)(2,1)S(1)}, u32[]{:S(2)}) copy-start(bf16[2,768,512]{2,1,0:T(8,128)(2,1)S(1)} %pad_maximum_fusion.7.rest_0_) | copy-start | bytes 4718596
  108.1 40.2 %collective-permute-start.1 = (bf16[2,768,512]{2,1,0:T(8,128)(2,1)S(1)}, bf16[2,768,512]{2,1,0:T(8,128)(2,1)}, u32[]{:S(2)}, u32[]{:S(2)}) collective-permute-start(bf16[2,768,512]{2,1,0:T(8,128)(2,1)S(1)} %pad_maximum_fusion.7.rest_0_), channel_id=1, source_target_pairs={{0,16},{8,24},{16,0},{24,8},{1,17},{9,25},{17,1},{25,9},{2,18},{10... | collective-permute-start | bytes 4718600 | tf_op jit(solution)/shard_map/ppermute | solution.py:314
  109.7 38.6 %collective-permute-start = (bf16[2,768,512]{2,1,0:T(8,128)(2,1)S(1)}, bf16[2,768,512]{2,1,0:T(8,128)(2,1)}, u32[]{:S(2)}, u32[]{:S(2)}) collective-permute-start(bf16[2,768,512]{2,1,0:T(8,128)(2,1)S(1)} %pad_maximum_fusion.7.rest_0_), channel_id=1, source_target_pairs={{0,8},{8,0},{16,24},{24,16},{1,9},{9,1},{17,25},{25,17},{2,10},{10... | collective-permute-start | bytes 4718600 | tf_op jit(solution)/shard_map/ppermute | solution.py:314
  148.3 176.5 %all-gather.16.cloned.1.call-start = ((), (), s32[]{:S(2)}) async-start(), calls=%async_computation.11 | async-start | bytes 10616832 | tf_op jit(solution)/shard_map/all_gather | solution.py:736
  148.3 23.7 %collective-permute-start.4 = (bf16[2,256,4096]{2,1,0:T(8,128)(2,1)}, bf16[2,256,4096]{2,1,0:T(8,128)(2,1)}, u32[]{:S(2)}, u32[]{:S(2)}) collective-permute-start(bf16[2,256,4096]{2,1,0:T(8,128)(2,1)} %shard_ref.7), channel_id=1, source_target_pairs={{0,1},{1,0},{2,3},{3,2},{4,5},{5,4},{6,7},{7,6},{8,9},{9,8},{10,11... | collective-permute-start | bytes 12582920 | tf_op jit(solution)/shard_map/ppermute | solution.py:306
  150.8 20.0 %collective-permute-start.3 = (bf16[768,512]{1,0:T(8,128)(2,1)S(1)}, bf16[768,512]{1,0:T(8,128)(2,1)S(1)}, u32[]{:S(2)}, u32[]{:S(2)}) collective-permute-start(bf16[768,512]{1,0:T(8,128)(2,1)S(1)} %slice_bitcast_fusion.9), channel_id=1, source_target_pairs={{0,8},{8,0},{16,24},{24,16},{1,9},{9,1},{17,25},{25,17},{2,10},{10... | collective-permute-start | bytes 2359304 | tf_op jit(solution)/shard_map/ppermute | solution.py:314
  152.3 19.7 %collective-permute-start.2 = (bf16[768,512]{1,0:T(8,128)(2,1)S(1)}, bf16[768,512]{1,0:T(8,128)(2,1)S(1)}, u32[]{:S(2)}, u32[]{:S(2)}) collective-permute-start(bf16[768,512]{1,0:T(8,128)(2,1)S(1)} %slice_bitcast_fusion.10), channel_id=1, source_target_pairs={{0,16},{8,24},{16,0},{24,8},{1,17},{9,25},{17,1},{25,9},{2,18},{10... | collective-permute-start | bytes 2359304 | tf_op jit(solution)/shard_map/ppermute | solution.py:314
  170.8 17.8 %copy-start.11 = (bf16[768,512]{1,0:T(8,128)(2,1)}, bf16[768,512]{1,0:T(8,128)(2,1)S(1)}, u32[]{:S(2)}) copy-start(bf16[768,512]{1,0:T(8,128)(2,1)S(1)} %collective-permute-done.3.rest_4_) | copy-start | bytes 2359300
  178.1 10.5 %collective-permute-start.7 = (bf16[4,2,768,512]{3,2,1,0:T(8,128)(2,1)}, bf16[4,2,768,512]{3,2,1,0:T(8,128)(2,1)}, u32[]{:S(2)}, u32[]{:S(2)}) collective-permute-start(bf16[4,2,768,512]{3,2,1,0:T(8,128)(2,1)} %pad_maximum_fusion), channel_id=1, source_target_pairs={{0,1},{1,0},{2,3},{3,2},{4,5},{5,4},{6,7},{7,6},{8,9},{9,8},{10,11... | collective-permute-start | bytes 18874376 | tf_op jit(solution)/shard_map/ppermute | solution.py:306
  178.1 499.7 %reduce-scatter.5.cloned.1.call-start = ((), (), s32[]{:S(2)}) async-start(), calls=%async_computation.4 | async-start | bytes 10616832 | tf_op jit(solution)/shard_map/reduce_scatter | solution.py:860
  181.0 37.1 %collective-permute-start.6 = (bf16[2,768,512]{2,1,0:T(8,128)(2,1)}, bf16[2,768,512]{2,1,0:T(8,128)(2,1)}, u32[]{:S(2)}, u32[]{:S(2)}) collective-permute-start(bf16[2,768,512]{2,1,0:T(8,128)(2,1)} %pad_maximum_fusion.8.rest_0_), channel_id=1, source_target_pairs={{0,16},{8,24},{16,0},{24,8},{1,17},{9,25},{17,1},{25,9},{2,18},{10... | collective-permute-start | bytes 4718600 | tf_op jit(solution)/shard_map/ppermute | solution.py:314
  182.5 36.8 %collective-permute-start.5 = (bf16[2,768,512]{2,1,0:T(8,128)(2,1)}, bf16[2,768,512]{2,1,0:T(8,128)(2,1)}, u32[]{:S(2)}, u32[]{:S(2)}) collective-permute-start(bf16[2,768,512]{2,1,0:T(8,128)(2,1)} %pad_maximum_fusion.8.rest_0_), channel_id=1, source_target_pairs={{0,8},{8,0},{16,24},{24,16},{1,9},{9,1},{17,25},{25,17},{2,10},{10... | collective-permute-start | bytes 4718600 | tf_op jit(solution)/shard_map/ppermute | solution.py:314
  183.9 74.0 %copy-start.16 = (s32[3]{0:T(128)}, s32[3]{0:T(128)S(1)}, u32[]{:S(2)}) copy-start(s32[3]{0:T(128)S(1)} %pad_add_fusion.where_ref) | copy-start | bytes 40
  221.7 18.9 %collective-permute-start.9 = (bf16[768,512]{1,0:T(8,128)(2,1)S(1)}, bf16[768,512]{1,0:T(8,128)(2,1)S(1)}, u32[]{:S(2)}, u32[]{:S(2)}) collective-permute-start(bf16[768,512]{1,0:T(8,128)(2,1)S(1)} %slice_bitcast_fusion.7), channel_id=1, source_target_pairs={{0,8},{8,0},{16,24},{24,16},{1,9},{9,1},{17,25},{25,17},{2,10},{10... | collective-permute-start | bytes 2359304 | tf_op jit(solution)/shard_map/ppermute | solution.py:314
  222.3 18.6 %collective-permute-start.8 = (bf16[768,512]{1,0:T(8,128)(2,1)S(1)}, bf16[768,512]{1,0:T(8,128)(2,1)S(1)}, u32[]{:S(2)}, u32[]{:S(2)}) collective-permute-start(bf16[768,512]{1,0:T(8,128)(2,1)S(1)} %slice_bitcast_fusion.8), channel_id=1, source_target_pairs={{0,16},{8,24},{16,0},{24,8},{1,17},{9,25},{17,1},{25,9},{2,18},{10... | collective-permute-start | bytes 2359304 | tf_op jit(solution)/shard_map/ppermute | solution.py:314
  240.6 17.3 %copy-start.14 = (bf16[768,512]{1,0:T(8,128)(2,1)}, bf16[768,512]{1,0:T(8,128)(2,1)S(1)}, u32[]{:S(2)}) copy-start(bf16[768,512]{1,0:T(8,128)(2,1)S(1)} %collective-permute-done.9.rest_4_) | copy-start | bytes 2359300
  240.8 17.1 %copy-start.15 = (bf16[768,512]{1,0:T(8,128)(2,1)}, bf16[768,512]{1,0:T(8,128)(2,1)S(1)}, u32[]{:S(2)}) copy-start(bf16[768,512]{1,0:T(8,128)(2,1)S(1)} %collective-permute-done.8.rest_3_) | copy-start | bytes 2359300
  241.0 9.8 %copy-start.76 = (s32[1,512]{1,0:T(1,128)S(1)}, s32[1,512]{1,0:T(1,128)}, u32[]{:S(2)}) copy-start(s32[1,512]{1,0:T(1,128)} %param.31) | copy-start | bytes 6148
  247.4 10.5 %collective-permute-start.10 = (bf16[4,2,768,512]{3,2,1,0:T(8,128)(2,1)}, bf16[4,2,768,512]{3,2,1,0:T(8,128)(2,1)}, u32[]{:S(2)}, u32[]{:S(2)}) collective-permute-start(bf16[4,2,768,512]{3,2,1,0:T(8,128)(2,1)} %pad_maximum_fusion.1), channel_id=1, source_target_pairs={{0,1},{1,0},{2,3},{3,2},{4,5},{5,4},{6,7},{7,6},{8,9},{9,8},{10,11... | collective-permute-start | bytes 18874376 | tf_op jit(solution)/shard_map/ppermute | solution.py:306
  334.6 24.9 %copy-start.32 = (f32[512,768]{1,0:T(8,128)}, f32[512,768]{1,0:T(8,128)S(1)}, u32[]{:S(2)}) copy-start(f32[512,768]{1,0:T(8,128)S(1)} %get-tuple-element.528) | copy-start | bytes 4718596
  370.0 307.8 %reduce-scatter.7.cloned.1.call-start = ((), (), s32[]{:S(2)}) async-start(), calls=%async_computation.5 | async-start | bytes 9732096 | tf_op jit(solution)/shard_map/reduce_scatter | solution.py:860
  370.1 7.6 copy-start.33
  384.6 10.9 %slice-start = ((s8[12582912]{0:T(1024)(128)(4,1)}), s8[4194304]{0:T(1024)(128)(4,1)S(1)}, s32[]{:S(2)}) async-start(s8[12582912]{0:T(1024)(128)(4,1)} %bitcast.308), calls=%async_computation.12 | async-start | bytes 8388608
  384.7 11.9 %slice-start.1 = ((s8[12582912]{0:T(1024)(128)(4,1)}), s8[4194304]{0:T(1024)(128)(4,1)S(1)}, s32[]{:S(2)}) async-start(s8[12582912]{0:T(1024)(128)(4,1)} %bitcast.308), calls=%async_computation.13 | async-start | bytes 8388608
  384.7 13.1 %slice-start.2 = ((s8[12582912]{0:T(1024)(128)(4,1)}), s8[4194304]{0:T(1024)(128)(4,1)S(1)}, s32[]{:S(2)}) async-start(s8[12582912]{0:T(1024)(128)(4,1)} %bitcast.308), calls=%async_computation.14 | async-start | bytes 8388608
  411.5 49.6 %copy-start.28 = (bf16[512,3,12,64]{0,3,2,1:T(8,128)(2,1)}, bf16[512,3,12,64]{0,3,2,1:T(8,128)(2,1)S(1)}, u32[]{:S(2)}) copy-start(bf16[512,3,12,64]{0,3,2,1:T(8,128)(2,1)S(1)} %pad_maximum_fusion.4) | copy-start | bytes 7077892
  422.9 34.9 %copy-start.60 = (bf16[512,768]{1,0:T(8,128)(2,1)S(1)}, bf16[512,768]{1,0:T(8,128)(2,1)}, u32[]{:S(2)}) copy-start(bf16[512,768]{1,0:T(8,128)(2,1)} %copy-done.59) | copy-start | bytes 2359300
  422.9 34.9 %copy-start.80 = (bf16[12,64,512]{2,1,0:T(8,128)(2,1)S(1)}, bf16[12,64,512]{2,1,0:T(8,128)(2,1)}, u32[]{:S(2)}) copy-start(bf16[12,64,512]{2,1,0:T(8,128)(2,1)} %fusion.34) | copy-start | bytes 2359300
  457.6 13.4 %collective-permute-start.11 = (bf16[4,2,1024,512]{3,2,1,0:T(8,128)(2,1)}, bf16[4,2,1024,512]{3,2,1,0:T(8,128)(2,1)S(1)}, u32[]{:S(2)}, u32[]{:S(2)}) collective-permute-start(bf16[4,2,1024,512]{3,2,1,0:T(8,128)(2,1)} %get-tuple-element.245), channel_id=1, source_target_pairs={{0,1},{1,0},{2,3},{3,2},{4,5},{5,4},{6,7},{7,6},{8,9},{9,8},{10,11... | collective-permute-start | bytes 25165832 | tf_op jit(solution)/shard_map/ppermute | solution.py:306
  479.3 242.7 %reduce-scatter.9.cloned.1.call-start = ((), (), s32[]{:S(2)}) async-start(), calls=%async_computation.6 | async-start | bytes 2621440 | tf_op jit(solution)/shard_map/reduce_scatter | solution.py:891
  490.8 47.8 %collective-permute-start.13 = (bf16[2,1024,512]{2,1,0:T(8,128)(2,1)}, bf16[2,1024,512]{2,1,0:T(8,128)(2,1)S(1)}, u32[]{:S(2)}, u32[]{:S(2)}) collective-permute-start(bf16[2,1024,512]{2,1,0:T(8,128)(2,1)} %get-tuple-element.463), channel_id=1, source_target_pairs={{0,8},{8,0},{16,24},{24,16},{1,9},{9,1},{17,25},{25,17},{2,10},{10... | collective-permute-start | bytes 6291464 | tf_op jit(solution)/shard_map/ppermute | solution.py:314
  492.1 47.7 %collective-permute-start.12 = (bf16[2,1024,512]{2,1,0:T(8,128)(2,1)}, bf16[2,1024,512]{2,1,0:T(8,128)(2,1)}, u32[]{:S(2)}, u32[]{:S(2)}) collective-permute-start(bf16[2,1024,512]{2,1,0:T(8,128)(2,1)} %fusion.18), channel_id=1, source_target_pairs={{0,16},{8,24},{16,0},{24,8},{1,17},{9,25},{17,1},{25,9},{2,18},{10... | collective-permute-start | bytes 6291464 | tf_op jit(solution)/shard_map/ppermute | solution.py:314
  539.8 30.1 %collective-permute-start.16 = (bf16[4,2,1024,512]{3,2,1,0:T(8,128)(2,1)}, bf16[4,2,1024,512]{3,2,1,0:T(8,128)(2,1)}, u32[]{:S(2)}, u32[]{:S(2)}) collective-permute-start(bf16[4,2,1024,512]{3,2,1,0:T(8,128)(2,1)} %get-tuple-element.261), channel_id=1, source_target_pairs={{0,1},{1,0},{2,3},{3,2},{4,5},{5,4},{6,7},{7,6},{8,9},{9,8},{10,11... | collective-permute-start | bytes 25165832 | tf_op jit(solution)/shard_map/ppermute | solution.py:306
  542.2 25.6 %collective-permute-start.14 = (bf16[1,1024,512]{2,1,0:T(8,128)(2,1)S(1)}, bf16[1,1024,512]{2,1,0:T(8,128)(2,1)S(1)}, u32[]{:S(2)}, u32[]{:S(2)}) collective-permute-start(bf16[1,1024,512]{2,1,0:T(8,128)(2,1)S(1)} %get-tuple-element.471), channel_id=1, source_target_pairs={{0,8},{8,0},{16,24},{24,16},{1,9},{9,1},{17,25},{25,17},{2,10},{10... | collective-permute-start | bytes 3145736 | tf_op jit(solution)/shard_map/ppermute | solution.py:314
  544.4 25.5 %collective-permute-start.15 = (bf16[1,1024,512]{2,1,0:T(8,128)(2,1)}, bf16[1,1024,512]{2,1,0:T(8,128)(2,1)S(1)}, u32[]{:S(2)}, u32[]{:S(2)}) collective-permute-start(bf16[1,1024,512]{2,1,0:T(8,128)(2,1)} %get-tuple-element.469), channel_id=1, source_target_pairs={{0,16},{8,24},{16,0},{24,8},{1,17},{9,25},{17,1},{25,9},{2,18},{10... | collective-permute-start | bytes 3145736 | tf_op jit(solution)/shard_map/ppermute | solution.py:314
  575.3 64.9 %collective-permute-start.18 = (bf16[2,1024,512]{2,1,0:T(8,128)(2,1)}, bf16[2,1024,512]{2,1,0:T(8,128)(2,1)}, u32[]{:S(2)}, u32[]{:S(2)}) collective-permute-start(bf16[2,1024,512]{2,1,0:T(8,128)(2,1)} %get-tuple-element.461), channel_id=1, source_target_pairs={{0,8},{8,0},{16,24},{24,16},{1,9},{9,1},{17,25},{25,17},{2,10},{10... | collective-permute-start | bytes 6291464 | tf_op jit(solution)/shard_map/ppermute | solution.py:314
  580.2 59.9 %collective-permute-start.17 = (bf16[2,1024,512]{2,1,0:T(8,128)(2,1)}, bf16[2,1024,512]{2,1,0:T(8,128)(2,1)}, u32[]{:S(2)}, u32[]{:S(2)}) collective-permute-start(bf16[2,1024,512]{2,1,0:T(8,128)(2,1)} %fusion.20), channel_id=1, source_target_pairs={{0,16},{8,24},{16,0},{24,8},{1,17},{9,25},{17,1},{25,9},{2,18},{10... | collective-permute-start | bytes 6291464 | tf_op jit(solution)/shard_map/ppermute | solution.py:314
  583.8 179.3 %reduce-scatter.11.cloned.1.call-start = ((), (), s32[]{:S(2)}) async-start(), calls=%async_computation.7 | async-start | bytes 2621440 | tf_op jit(solution)/shard_map/reduce_scatter | solution.py:891
  643.4 34.3 %collective-permute-start.19 = (bf16[1,1024,512]{2,1,0:T(8,128)(2,1)}, bf16[1,1024,512]{2,1,0:T(8,128)(2,1)}, u32[]{:S(2)}, u32[]{:S(2)}) collective-permute-start(bf16[1,1024,512]{2,1,0:T(8,128)(2,1)} %get-tuple-element.467), channel_id=1, source_target_pairs={{0,8},{8,0},{16,24},{24,16},{1,9},{9,1},{17,25},{25,17},{2,10},{10... | collective-permute-start | bytes 3145736 | tf_op jit(solution)/shard_map/ppermute | solution.py:314
  647.8 30.0 %collective-permute-start.20 = (bf16[1,1024,512]{2,1,0:T(8,128)(2,1)}, bf16[1,1024,512]{2,1,0:T(8,128)(2,1)}, u32[]{:S(2)}, u32[]{:S(2)}) collective-permute-start(bf16[1,1024,512]{2,1,0:T(8,128)(2,1)} %get-tuple-element.465), channel_id=1, source_target_pairs={{0,16},{8,24},{16,0},{24,8},{1,17},{9,25},{17,1},{25,9},{2,18},{10... | collective-permute-start | bytes 3145736 | tf_op jit(solution)/shard_map/ppermute | solution.py:314
  688.6 33.5 %collective-permute-start.22 = (bf16[736,768]{1,0:T(8,128)(2,1)}, bf16[736,768]{1,0:T(8,128)(2,1)S(1)}, u32[]{:S(2)}, u32[]{:S(2)}) collective-permute-start(bf16[736,768]{1,0:T(8,128)(2,1)} %slice.825), channel_id=1, source_target_pairs={{0,8},{8,0},{16,24},{24,16},{1,9},{9,1},{17,25},{25,17},{2,10},{10... | collective-permute-start | bytes 3391496 | tf_op jit(solution)/shard_map/ppermute | solution.py:314
  690.3 31.7 %collective-permute-start.21 = (bf16[736,768]{1,0:T(8,128)(2,1)}, bf16[736,768]{1,0:T(8,128)(2,1)}, u32[]{:S(2)}, u32[]{:S(2)}) collective-permute-start(bf16[736,768]{1,0:T(8,128)(2,1)} %slice.719), channel_id=1, source_target_pairs={{0,16},{8,24},{16,0},{24,8},{1,17},{9,25},{17,1},{25,9},{2,18},{10... | collective-permute-start | bytes 3391496 | tf_op jit(solution)/shard_map/ppermute | solution.py:314
  726.8 36.2 %collective-permute-start.27 = (bf16[736,768]{1,0:T(8,128)(2,1)}, bf16[736,768]{1,0:T(8,128)(2,1)}, u32[]{:S(2)}, u32[]{:S(2)}) collective-permute-start(bf16[736,768]{1,0:T(8,128)(2,1)} %get-tuple-element.483), channel_id=1, source_target_pairs={{0,16},{8,24},{16,0},{24,8},{1,17},{9,25},{17,1},{25,9},{2,18},{10... | collective-permute-start | bytes 3391496 | tf_op jit(solution)/shard_map/ppermute | solution.py:314
  727.6 35.5 %collective-permute-start.26 = (bf16[736,768]{1,0:T(8,128)(2,1)}, bf16[736,768]{1,0:T(8,128)(2,1)}, u32[]{:S(2)}, u32[]{:S(2)}) collective-permute-start(bf16[736,768]{1,0:T(8,128)(2,1)} %get-tuple-element.484), channel_id=1, source_target_pairs={{0,8},{8,0},{16,24},{24,16},{1,9},{9,1},{17,25},{25,17},{2,10},{10... | collective-permute-start | bytes 3391496 | tf_op jit(solution)/shard_map/ppermute | solution.py:314
  728.2 34.8 %collective-permute-start.25 = (bf16[2,256,512]{2,1,0:T(8,128)(2,1)}, bf16[2,256,512]{2,1,0:T(8,128)(2,1)}, u32[]{:S(2)}, u32[]{:S(2)}) collective-permute-start(bf16[2,256,512]{2,1,0:T(8,128)(2,1)} %bitcast.109), channel_id=1, source_target_pairs={{0,16},{8,24},{16,0},{24,8},{1,17},{9,25},{17,1},{25,9},{2,18},{10... | collective-permute-start | bytes 1572872 | tf_op jit(solution)/shard_map/ppermute | solution.py:314
  730.1 32.9 %collective-permute-start.24 = (bf16[2,256,512]{2,1,0:T(8,128)(2,1)}, bf16[2,256,512]{2,1,0:T(8,128)(2,1)}, u32[]{:S(2)}, u32[]{:S(2)}) collective-permute-start(bf16[2,256,512]{2,1,0:T(8,128)(2,1)} %bitcast.109), channel_id=1, source_target_pairs={{0,8},{8,0},{16,24},{24,16},{1,9},{9,1},{17,25},{25,17},{2,10},{10... | collective-permute-start | bytes 1572872 | tf_op jit(solution)/shard_map/ppermute | solution.py:314
  734.5 30.8 %copy-start.19 = (bf16[1472,768]{1,0:T(8,128)(2,1)S(1)}, bf16[1472,768]{1,0:T(8,128)(2,1)}, u32[]{:S(2)}) copy-start(bf16[1472,768]{1,0:T(8,128)(2,1)} %copy-done.18) | copy-start | bytes 6782980
  735.4 1.6 collective-permute-start.23
  763.1 22.6 %collective-permute-start.29 = (bf16[2,256,512]{2,1,0:T(8,128)(2,1)}, bf16[2,256,512]{2,1,0:T(8,128)(2,1)S(1)}, u32[]{:S(2)}, u32[]{:S(2)}) collective-permute-start(bf16[2,256,512]{2,1,0:T(8,128)(2,1)} %bitcast.384), channel_id=1, source_target_pairs={{0,16},{8,24},{16,0},{24,8},{1,17},{9,25},{17,1},{25,9},{2,18},{10... | collective-permute-start | bytes 1572872 | tf_op jit(solution)/shard_map/ppermute | solution.py:314
  764.9 20.8 %collective-permute-start.28 = (bf16[2,256,512]{2,1,0:T(8,128)(2,1)}, bf16[2,256,512]{2,1,0:T(8,128)(2,1)S(1)}, u32[]{:S(2)}, u32[]{:S(2)}) collective-permute-start(bf16[2,256,512]{2,1,0:T(8,128)(2,1)} %bitcast.385), channel_id=1, source_target_pairs={{0,8},{8,0},{16,24},{24,16},{1,9},{9,1},{17,25},{25,17},{2,10},{10... | collective-permute-start | bytes 1572872 | tf_op jit(solution)/shard_map/ppermute | solution.py:314
  770.4 7.7 collective-permute-start.30
  773.7 8.9 %collective-permute-start.36 = (bf16[256,512]{1,0:T(8,128)(2,1)S(1)}, bf16[256,512]{1,0:T(8,128)(2,1)S(1)}, u32[]{:S(2)}, u32[]{:S(2)}) collective-permute-start(bf16[256,512]{1,0:T(8,128)(2,1)S(1)} %get-tuple-element.509), channel_id=1, source_target_pairs={{0,16},{8,24},{16,0},{24,8},{1,17},{9,25},{17,1},{25,9},{2,18},{10... | collective-permute-start | bytes 786440 | tf_op jit(solution)/shard_map/ppermute | solution.py:314
  778.2 4.4 collective-permute-start.31
  778.9 6.4 collective-permute-start.37
  787.2 4.4 collective-permute-start.32
  789.3 15.9 %collective-permute-start.34 = (bf16[256,512]{1,0:T(8,128)(2,1)}, bf16[256,512]{1,0:T(8,128)(2,1)}, u32[]{:S(2)}, u32[]{:S(2)}) collective-permute-start(bf16[256,512]{1,0:T(8,128)(2,1)} %get-tuple-element.501), channel_id=1, source_target_pairs={{0,16},{8,24},{16,0},{24,8},{1,17},{9,25},{17,1},{25,9},{2,18},{10... | collective-permute-start | bytes 786440 | tf_op jit(solution)/shard_map/ppermute | solution.py:314
  791.6 4.4 collective-permute-start.33
  793.8 12.8 %collective-permute-start.35 = (bf16[256,512]{1,0:T(8,128)(2,1)}, bf16[256,512]{1,0:T(8,128)(2,1)}, u32[]{:S(2)}, u32[]{:S(2)}) collective-permute-start(bf16[256,512]{1,0:T(8,128)(2,1)} %get-tuple-element.504), channel_id=1, source_target_pairs={{0,8},{8,0},{16,24},{24,16},{1,9},{9,1},{17,25},{25,17},{2,10},{10... | collective-permute-start | bytes 786440 | tf_op jit(solution)/shard_map/ppermute | solution.py:314
  (70 other events, 211.9 us)
Sparse Core Ops, SparseCore 0:
  54.3 47.1 all-gather.9
  103.7 44.5 all-gather.11
  150.5 82.9 all-gather.13
  235.5 89.2 all-gather.15
  370.2 97.9 reduce-scatter.4
  479.4 90.6 reduce-scatter.6
  583.9 41.0 reduce-scatter.8
  682.7 42.7 reduce-scatter.10

commit v2 on v1

--- a/solution.py
+++ b/solution.py
@@ -8,7 +8,6 @@
 from jax.experimental.pallas import tpu as pltpu
 from jax.sharding import PartitionSpec as P
 
-HEADS = 12
 HDIM = 64
 CDIM = 16
 WCH = 50
@@ -110,22 +109,22 @@
     piece(48 * block, 2, 0, 256)
 
 
-def conv_forward(call, ids, counts, tables, kern, state):
+def conv_forward(call, count, ids, counts, tables, kern, state):
     block = CONV_BLOCK
     words, filters = ids.shape[0], kern.shape[1]
     return pl.pallas_call(
         functools.partial(conv_fwd_body, block, filters, len(state)),
-        grid=(1,),
+        grid=(count,),
         in_specs=[
-            pl.BlockSpec((block, ids.shape[1]), lambda i: (call, 0)),
-            pl.BlockSpec((block, 1), lambda i: (call, 0)),
+            pl.BlockSpec((block, ids.shape[1]), lambda i: (call + i, 0)),
+            pl.BlockSpec((block, 1), lambda i: (call + i, 0)),
             pl.BlockSpec(tables.shape, lambda i: (0, 0, 0)),
             pl.BlockSpec(kern.shape, lambda i: (0, 0)),
         ]
         + [pl.BlockSpec(memory_space=pl.ANY)] * len(state),
         out_specs=[
-            pl.BlockSpec((WCH * block, KROWS), lambda i: (call, 0)),
-            pl.BlockSpec((block, filters), lambda i: (call, 0)),
+            pl.BlockSpec((WCH * block, KROWS), lambda i: (call + i, 0)),
+            pl.BlockSpec((block, filters), lambda i: (call + i, 0)),
         ],
         out_shape=[
             jax.ShapeDtypeStruct((words * WCH, KROWS), jnp.bfloat16),
@@ -138,8 +137,8 @@
         ],
         compiler_params=pltpu.CompilerParams(vmem_limit_bytes=40 << 20),
         cost_estimate=pl.CostEstimate(
-            flops=block * WCH * 32 * filters,
-            bytes_accessed=block * filters,
+            flops=count * block * WCH * 32 * filters,
+            bytes_accessed=count * block * filters,
             transcendentals=0,
         ),
         name="conv_forward",
@@ -147,8 +146,11 @@
 
 
 def conv_bwd_body(block, filters, idst_ref, x_ref, ginv_ref, kern_ref, kern_in_ref, table_in_ref, kern_grad_ref, table_grad_ref, gx, flat, hot, part):
-    kern_grad_ref[...] = kern_in_ref[...]
-    table_grad_ref[...] = table_in_ref[...]
+    @pl.when(pl.program_id(0) == 0)
+    def _():
+        kern_grad_ref[...] = kern_in_ref[...]
+        table_grad_ref[...] = table_in_ref[...]
+
 
     tile = 512
     step = 4
@@ -202,17 +204,17 @@
         table_grad_ref[...] += jnp.where((lane_t >= 16 * turn) & (lane_t < 16 * turn + 16), found, 0.0)
 
 
-def conv_backward(call, ids_t, x, ginv, kern, state):
+def conv_backward(call, count, ids_t, x, ginv, kern, state):
     block = CONV_BLOCK
     filters = ginv.shape[1]
     whole = [pl.BlockSpec(kern.shape, lambda i: (0, 0)), pl.BlockSpec((VROWS, 128), lambda i: (0, 0))]
     return pl.pallas_call(
         functools.partial(conv_bwd_body, block, filters),
-        grid=(1,),
+        grid=(count,),
         in_specs=[
-            pl.BlockSpec((ids_t.shape[0], block), lambda i: (0, call)),
-            pl.BlockSpec((WCH * block, KROWS), lambda i: (call, 0)),
-            pl.BlockSpec((block, filters), lambda i: (call, 0)),
+            pl.BlockSpec((ids_t.shape[0], block), lambda i: (0, call + i)),
+            pl.BlockSpec((WCH * block, KROWS), lambda i: (call + i, 0)),
+            pl.BlockSpec((block, filters), lambda i: (call + i, 0)),
             pl.BlockSpec(kern.shape, lambda i: (0, 0)),
         ]
         + whole,
@@ -228,10 +230,10 @@
             pltpu.VMEM((VROWS, FLAT // 128 * block), jnp.bfloat16),
             pltpu.VMEM((FLAT // 128 * block, 128), jnp.bfloat16),
         ],
-        compiler_params=pltpu.CompilerParams(vmem_limit_bytes=40 << 20),
+        compiler_params=pltpu.CompilerParams(vmem_limit_bytes=60 << 20),
         cost_estimate=pl.CostEstimate(
-            flops=block * WCH * 64 * filters,
-            bytes_accessed=block * filters,
+            flops=count * block * WCH * 64 * filters,
+            bytes_accessed=count * block * filters,
             transcendentals=0,
         ),
         name="conv_backward",
@@ -243,63 +245,256 @@
     return jnp.stack([jnp.pad(padded, ((0, 0), (16 * r, 112 - 16 * r))) for r in range(8)])
 
 
-def score_block(heads_all, length):
-    seq_len = heads_all.shape[0]
-    scale_factor = 1.0 / math.sqrt(HDIM)
-    scores = (
-        jnp.einsum(
-            "qhe,khe->hqk", heads_all[:, 0], heads_all[:, 1], preferred_element_type=jnp.float32
-        )
-        * scale_factor
-    )
-    keep_keys = lax.broadcasted_iota(jnp.int32, (1, 1, seq_len), 2) < length
-    return jnp.where(keep_keys, scores, MASKED_SCORE)
-
-
-def attend(proj_seq, length):
-    seq_len = proj_seq.shape[0]
-    heads_all = proj_seq.reshape(seq_len, 3, HEADS, HDIM)
-    scores = score_block(heads_all, length)
-    highest = jnp.max(scores, axis=2, keepdims=True)
-    exponent = jnp.exp(scores - highest)
-    denominator = jnp.sum(exponent, axis=2, keepdims=True)
-    attention = (exponent / denominator).astype(jnp.bfloat16)
-    context = jnp.einsum(
-        "hqk,khe->qhe", attention, heads_all[:, 2], preferred_element_type=jnp.float32
-    )
-    return (context.reshape(seq_len, -1).astype(jnp.bfloat16), highest + jnp.log(denominator))
-
-
-def attend_back(proj_seq, log_total, grad_context, length):
-    seq_len = proj_seq.shape[0]
-    scale_factor = 1.0 / math.sqrt(HDIM)
-    heads_all = proj_seq.reshape(seq_len, 3, HEADS, HDIM)
-    grad_heads = grad_context.reshape(seq_len, HEADS, HDIM)
-    attention = jnp.exp(score_block(heads_all, length) - log_total)
-    grad_attention = jnp.einsum(
-        "qhe,khe->hqk", grad_heads, heads_all[:, 2], preferred_element_type=jnp.float32
-    )
-    grad_values = jnp.einsum(
-        "hqk,qhe->khe",
-        attention.astype(jnp.bfloat16),
-        grad_heads,
-        preferred_element_type=jnp.float32,
-    )
-    row_dot = jnp.sum(attention * grad_attention, axis=2, keepdims=True)
-    grad_scores = (attention * (grad_attention - row_dot)).astype(jnp.bfloat16)
-    grad_queries = (
-        jnp.einsum("hqk,khe->qhe", grad_scores, heads_all[:, 1], preferred_element_type=jnp.float32)
-        * scale_factor
-    )
-    grad_keys = (
-        jnp.einsum("hqk,qhe->khe", grad_scores, heads_all[:, 0], preferred_element_type=jnp.float32)
-        * scale_factor
-    )
-    return (
-        jnp.stack([grad_queries, grad_keys, grad_values], axis=1)
-        .reshape(seq_len, -1)
-        .astype(jnp.bfloat16)
-    )
+def head_scores(length_ref, q, k, head):
+    words, width = q.shape
+    lane = lax.broadcasted_iota(jnp.int32, (words, width), 1)
+    inside = (lane >= head * HDIM) & (lane < (head + 1) * HDIM)
+    own = jnp.where(inside, q.astype(jnp.float32), 0.0).astype(jnp.bfloat16)
+    key = lax.broadcasted_iota(jnp.int32, (words, words), 0)
+    scores = matmul(k, own, CONTRACT_COLS) * (1.0 / math.sqrt(HDIM))
+    return own, inside, key < length_ref[0], scores
+
+
+def attend_body(length_ref, q_ref, k_ref, v_ref, context_ref, total_ref):
+    q, k, v = q_ref[...], k_ref[...], v_ref[...]
+    words, width = q.shape
+    row = lax.broadcasted_iota(jnp.int32, (width, words), 0)
+    context = jnp.zeros((width, words), jnp.float32)
+    for head in range(2):
+        _, _, keep, scores = head_scores(length_ref, q, k, head)
+        scores = jnp.where(keep, scores, MASKED_SCORE)
+        highest = jnp.max(scores, axis=0, keepdims=True)
+        exponent = jnp.exp(scores - highest)
+        denominator = jnp.sum(exponent, axis=0, keepdims=True)
+        weights = (exponent * (1.0 / denominator)).astype(jnp.bfloat16)
+        own = matmul(v, weights, CONTRACT_ROWS)
+        context = jnp.where(row >= head * HDIM, own, context)
+        total_ref[0, head : head + 1, :] = highest + jnp.log(denominator)
+    context_ref[...] = context.T.astype(jnp.bfloat16)
+
+
+def attend_back_body(length_ref, q_ref, k_ref, v_ref, pull_ref, total_ref, grad_ref):
+    q, k, v = q_ref[...], k_ref[...], v_ref[...]
+    pull = pull_ref[...].astype(jnp.float32)
+    words, width = q.shape
+    row = lax.broadcasted_iota(jnp.int32, (width, words), 0)
+    scale = 1.0 / math.sqrt(HDIM)
+    grad_q = jnp.zeros((width, words), jnp.float32)
+    grad_k = jnp.zeros((words, width), jnp.float32)
+    grad_v = jnp.zeros((words, width), jnp.float32)
+    for head in range(2):
+        own, inside, keep, scores = head_scores(length_ref, q, k, head)
+        weights = jnp.where(keep, jnp.exp(scores - total_ref[0, head : head + 1, :]), 0.0)
+        own_pull = jnp.where(inside, pull, 0.0).astype(jnp.bfloat16)
+        grad_weights = matmul(v, own_pull, CONTRACT_COLS)
+        dots = jnp.sum(weights * grad_weights, axis=0, keepdims=True)
+        grad_scores = (weights * (grad_weights - dots)).astype(jnp.bfloat16)
+        grad_v = grad_v + matmul(weights.astype(jnp.bfloat16), own_pull)
+        grad_k = grad_k + matmul(grad_scores, own)
+        grad_q = jnp.where(row >= head * HDIM, matmul(k, grad_scores, CONTRACT_ROWS), grad_q)
+    grad_ref[0] = (grad_q.T * scale).astype(jnp.bfloat16)
+    grad_ref[1] = (grad_k * scale).astype(jnp.bfloat16)
+    grad_ref[2] = grad_v.astype(jnp.bfloat16)
+
+
+def attention_specs(words, columns):
+    return pl.BlockSpec((words, 2 * HDIM), lambda i, length: (0, i)), columns // (2 * HDIM)
+
+
+def attend(length, q, k, v):
+    words, columns = q.shape
+    block, pairs = attention_specs(words, columns)
+    return pl.pallas_call(
+        attend_body,
+        grid_spec=pltpu.PrefetchScalarGridSpec(
+            num_scalar_prefetch=1,
+            grid=(pairs,),
+            in_specs=[block] * 3,
+            out_specs=[block, pl.BlockSpec((1, 8, words), lambda i, length: (i, 0, 0))],
+        ),
+        out_shape=[
+            jax.ShapeDtypeStruct((words, columns), jnp.bfloat16),
+            jax.ShapeDtypeStruct((pairs, 8, words), jnp.float32),
+        ],
+        compiler_params=pltpu.CompilerParams(vmem_limit_bytes=40 << 20),
+        cost_estimate=pl.CostEstimate(flops=words * words * columns, bytes_accessed=words * columns, transcendentals=0),
+        name="attend",
+    )(length, q, k, v)
+
+
+def attend_back(length, q, k, v, pull, totals):
+    words, columns = q.shape
+    block, pairs = attention_specs(words, columns)
+    return pl.pallas_call(
+        attend_back_body,
+        grid_spec=pltpu.PrefetchScalarGridSpec(
+            num_scalar_prefetch=1,
+            grid=(pairs,),
+            in_specs=[block] * 4 + [pl.BlockSpec((1, 8, words), lambda i, length: (i, 0, 0))],
+            out_specs=pl.BlockSpec((3, words, 2 * HDIM), lambda i, length: (0, 0, i)),
+        ),
+        out_shape=jax.ShapeDtypeStruct((3, words, columns), jnp.bfloat16),
+        compiler_params=pltpu.CompilerParams(vmem_limit_bytes=40 << 20),
+        cost_estimate=pl.CostEstimate(flops=words * words * columns, bytes_accessed=words * columns, transcendentals=0),
+        name="attend_back",
+    )(length, q, k, v, pull, totals)
+
+
+def lane_moves(sizes, wide):
+    moves, start, channel = [], 0, 0
+    for size in sizes:
+        for device in range(wide):
+            moves.append((device, start, channel + device * size, size))
+        start += size
+        channel += size * wide
+    return moves
+
+
+def shifted(value, lane_from, lane_to):
+    shift = (lane_to - lane_from) % value.shape[1]
+    return pltpu.roll(value, shift, 1) if shift else value
+
+
+def row_places(row, shape, lanes):
+    count, size = shape
+    places = []
+    for i in range(count):
+        for low in range(0, size, lanes):
+            places.append((row, i, low, min(low + lanes, size)))
+            row += 1
+    return places
+
+
+def share_body(sizes, starts, *refs):
+    others, out_ref, rest = refs[len(sizes) : -2], refs[-2], refs[-1]
+    lanes = out_ref.shape[1]
+    start = 0
+    for ref, size in zip(refs, sizes):
+        rows = ref.shape[1]
+        value = ref[...].astype(jnp.float32).T.astype(out_ref.dtype)
+        out_ref[:rows, start : start + size] = value
+        if rows < TAP:
+            out_ref[rows:TAP, start : start + size] = jnp.zeros((TAP - rows, size), out_ref.dtype)
+        start += size
+    rest[...] = jnp.zeros_like(rest)
+    for ref, row in zip(others, starts):
+        value = ref[...].astype(jnp.float32)
+        for target, i, low, high in row_places(row - TAP, ref.shape, lanes):
+            rest[target : target + 1, : high - low] = value[i : i + 1, low:high]
+    out_ref[TAP:, :] = rest[...].astype(out_ref.dtype)
+
+
+def make_share(kernels, others, starts, rows, lanes):
+    sizes = [kernel.shape[1] for kernel in kernels]
+    return pl.pallas_call(
+        functools.partial(share_body, sizes, starts),
+        out_shape=jax.ShapeDtypeStruct((rows, lanes), jnp.bfloat16),
+        scratch_shapes=[pltpu.VMEM((rows - TAP, lanes), jnp.float32)],
+        name="make_share",
+    )(*[kernel.T for kernel in kernels], *others)
+
+
+def kernel_body(sizes, wide, all_ref, out_ref):
+    filters = out_ref.shape[1]
+    lanes = all_ref.shape[2]
+    width = min(lanes, 128)
+    lane = lax.broadcasted_iota(jnp.int32, (TAP, 128), 1)
+    tiles = [None] * (filters // 128)
+    for device, start, channel, size in lane_moves(sizes, wide):
+        low = start // width * width
+        value = all_ref[device, :TAP, low : low + width].astype(jnp.float32)
+        if width < 128:
+            value = jnp.concatenate([value, jnp.zeros((TAP, 128 - width), jnp.float32)], axis=1)
+        value = shifted(value, start - low, channel % 128)
+        tile = channel // 128
+        inside = (lane >= channel % 128) & (lane < channel % 128 + size)
+        tiles[tile] = jnp.where(inside, value, 0.0 if tiles[tile] is None else tiles[tile])
+    for i, tile in enumerate(tiles):
+        out_ref[:TAP, i * 128 : (i + 1) * 128] = tile.astype(jnp.bfloat16)
+    row = lax.broadcasted_iota(jnp.int32, (KROWS - TAP, filters), 0)
+    channel = lax.broadcasted_iota(jnp.int32, (KROWS - TAP, filters), 1)
+    below = jnp.zeros((KROWS - TAP, filters), jnp.float32)
+    start = 0
+    for i, size in enumerate(sizes):
+        inside = (row == i + 1) & (channel >= start) & (channel < start + size * wide)
+        below = jnp.where(inside, 1.0, below)
+        start += size * wide
+    biases = jnp.concatenate([all_ref[d, TAP : TAP + 16, :].astype(jnp.float32)[:1] for d in range(wide)], axis=1)
+    out_ref[TAP:, :] = jnp.where(row == 0, biases, below).astype(jnp.bfloat16)
+
+
+def make_kernel(everyone, sizes):
+    wide, _, lanes = everyone.shape
+    return pl.pallas_call(
+        functools.partial(kernel_body, sizes, wide),
+        out_shape=jax.ShapeDtypeStruct((KROWS, wide * lanes), jnp.bfloat16),
+        name="make_kernel",
+    )(everyone)
+
+
+def shares_body(sizes, wide, starts, grad_ref, *refs):
+    others, late_ref, out_ref, rest = refs[:-3], refs[-3], refs[-2], refs[-1]
+    lanes = out_ref.shape[2]
+    width = min(lanes, 128)
+    lane = lax.broadcasted_iota(jnp.int32, (TAP, 128), 1)
+    tiles = {}
+    for device, start, channel, size in lane_moves(sizes, wide):
+        source = grad_ref[:TAP, channel // 128 * 128 : channel // 128 * 128 + 128]
+        low = start // width * width
+        value = shifted(source, channel % 128, start - low)
+        inside = (lane >= start - low) & (lane < start - low + size)
+        tiles[device, low] = jnp.where(inside, value, tiles.get((device, low), 0.0))
+    for (device, low), tile in tiles.items():
+        out_ref[device, :TAP, low : low + width] = tile[:, :width].astype(jnp.bfloat16)
+    values = [ref[...] for ref in others]
+    rest[...] = jnp.zeros_like(rest)
+    early = rest.shape[0] - late_ref.shape[1]
+    for device in range(wide):
+        rest[:1, :] = grad_ref[TAP : TAP + 8, device * lanes : (device + 1) * lanes][:1]
+        for value, row in zip(values, starts):
+            count, size = value.shape[0], value.shape[1] // wide
+            for target, i, low, high in row_places(row - TAP, (count, size), lanes):
+                rest[target : target + 1, : high - low] = value[i : i + 1, device * size + low : device * size + high]
+        rest[early:, :] = late_ref[device]
+        out_ref[device, TAP:, :] = rest[...].astype(jnp.bfloat16)
+
+
+def make_shares(grad, others, late, sizes, starts, rows):
+    wide, _, lanes = late.shape
+    return pl.pallas_call(
+        functools.partial(shares_body, sizes, wide, starts),
+        out_shape=jax.ShapeDtypeStruct((wide, rows, lanes), jnp.bfloat16),
+        scratch_shapes=[pltpu.VMEM((rows - TAP, lanes), jnp.float32)],
+        name="make_shares",
+    )(grad, *others, late)
+
+
+def apart_body(sizes, kernel_rows, starts, first, second_ref, *outs):
+    total = first[...] + second_ref[...].astype(jnp.float32)
+    lanes = total.shape[1]
+    width = min(lanes, 128)
+    start = 0
+    for ref, size, rows in zip(outs, sizes, kernel_rows):
+        low = start // width * width
+        tile = total[:128, low : low + width]
+        if width < 128:
+            tile = jnp.concatenate([tile, jnp.zeros((128, 128 - width), jnp.float32)], axis=1)
+        tile = shifted(tile, start - low, 0)
+        ref[...] = tile[:rows, :size] if size == 128 else tile.T[:size, :rows]
+        start += size
+    for ref, row in zip(outs[len(sizes) :], starts):
+        for source, i, low, high in row_places(row, ref.shape, lanes):
+            ref[i : i + 1, low:high] = total[source : source + 1, : high - low]
+
+
+def take_apart(first, second, sizes, kernel_rows, starts, shapes):
+    kernels = [(rows, size) if size == 128 else (size, rows) for rows, size in zip(kernel_rows, sizes)]
+    outs = pl.pallas_call(
+        functools.partial(apart_body, sizes, kernel_rows, starts),
+        out_shape=[jax.ShapeDtypeStruct(shape, jnp.float32) for shape in kernels + shapes],
+        name="take_apart",
+    )(first, second)
+    return [out if i >= len(sizes) or sizes[i] == 128 else out.T for i, out in enumerate(outs)]
 
 
 def core_swap(value, wide):
@@ -367,11 +562,11 @@
     return lax.optimization_barrier(groups)
 
 
-def own_columns(shard, place, narrow):
-    rows, columns = shard.shape
+def own_columns(shards, layer, place, narrow):
+    _, rows, columns = shards.shape
     part = columns // 2 // narrow
-    return jnp.stack(
-        [lax.dynamic_slice(shard, (0, half * (columns // 2) + place * part), (rows, part)) for half in range(2)]
+    return jnp.concatenate(
+        [lax.dynamic_slice(shards, (layer, 0, half * (columns // 2) + place * part), (1, rows, part)) for half in range(2)]
     )
 
 
@@ -391,8 +586,62 @@
     return jnp.concatenate(pieces, axis=1)
 
 
-def swap_known(known, narrow, wide):
-    return core_swap(jnp.stack([jnp.stack(known[m]) if m & (m - 1) else known[m] for m in range(narrow)]), wide)
+def swap_early(known, narrow, wide):
+    return core_swap(jnp.stack([known[mask] for mask in range(narrow) if not mask & (mask - 1)]), wide)
+
+
+def swap_late(known, narrow, wide):
+    far = [jnp.stack(known[mask]) for mask in range(narrow) if mask & (mask - 1)]
+    return [core_swap(jnp.stack(far), wide)] if far else []
+
+
+def own_rows(shard, place, narrow):
+    rows, columns = shard.shape
+    own = lax.dynamic_slice_in_dim(shard, place * (rows // narrow), rows // narrow, 0)
+    return jnp.stack([own[:, : columns // 2], own[:, columns // 2 :]])
+
+
+def assemble_body(chips, narrow, where_ref, *rest):
+    mine, other, (out_ref, sems) = weight_refs(rest, narrow)
+    part = out_ref.shape[1] // narrow
+    columns = out_ref.shape[2] // 2
+    copies = []
+    for side, refs in enumerate((mine, other)):
+        for mask in range(narrow):
+            start = pl.multiple_of((where_ref[0] ^ mask) * part, part)
+            for half in range(2):
+                for chip in range(chips):
+                    source = refs(mask, half).at[chip * part : (chip + 1) * part, :]
+                    target = out_ref.at[
+                        2 * chip + (where_ref[2] ^ side), pl.ds(start, part), half * columns : (half + 1) * columns
+                    ]
+                    copies.append(pltpu.make_async_copy(source, target, sems.at[len(copies)]))
+    for copy in copies:
+        copy.start()
+    for copy in copies:
+        copy.wait()
+
+
+def assemble(where, known, other, wide):
+    narrow = len(known)
+    _, length, columns = known[0].shape
+    chips = wide // 2
+    flat = jax.tree.leaves(([known[mask] for mask in range(narrow)], other))
+    shape = (wide, narrow * length // chips, 2 * columns)
+    return pl.pallas_call(
+        functools.partial(assemble_body, chips, narrow),
+        grid_spec=pltpu.PrefetchScalarGridSpec(
+            num_scalar_prefetch=1,
+            grid=(1,),
+            in_specs=[pl.BlockSpec(memory_space=pl.ANY)] * len(flat),
+            out_specs=pl.BlockSpec(shape, lambda i, where: (0, 0, 0)),
+            scratch_shapes=[pltpu.SemaphoreType.DMA((4 * narrow * chips,))],
+        ),
+        out_shape=jax.ShapeDtypeStruct(shape, known[0].dtype),
+        compiler_params=pltpu.CompilerParams(vmem_limit_bytes=60 << 20),
+        cost_estimate=pl.CostEstimate(flops=0, bytes_accessed=known[0].size, transcendentals=0),
+        name="assemble",
+    )(where, *flat)
 
 
 def weight_copies(narrow, layer, where_ref, mask, shard_ref, twin_ref, mine, other, slot_ref, sems):
@@ -440,39 +689,48 @@
 
 
 def weight_refs(refs, narrow):
-    places, count = {}, 0
+    places, twins, count = {}, {}, 0
+    near = [mask for mask in range(narrow) if not mask & (mask - 1)]
+    far = [mask for mask in range(narrow) if mask & (mask - 1)]
     for mask in range(narrow):
         for half in range(2):
-            if mask & (mask - 1):
+            if mask in far:
                 places[mask, half] = refs[count]
                 count += 1
             else:
                 places[mask, half] = refs[count].at[half]
-        if not mask & (mask - 1):
+        if mask in near:
             count += 1
-    twin = refs[count]
-    return lambda mask, half: places[mask, half], lambda mask, half: twin.at[mask, half], refs[count + 1 :]
+    for group in (near, far):
+        for i, mask in enumerate(group):
+            for half in range(2):
+                twins[mask, half] = refs[count].at[i, half]
+        if group:
+            count += 1
+    return lambda mask, half: places[mask, half], lambda mask, half: twins[mask, half], refs[count:]
 
 
 def mix_forward_body(narrow, layer, where_ref, low_ref, carry_ref, shift_a_ref, shift_g_ref, shard_ref, twin_ref, *rest):
-    mine, other, (next_ref, low_next_ref, a_ref, g_ref, slots, sems) = weight_refs(rest, narrow)
+    mine, other, (next_ref, low_next_ref, a_ref, cdf_ref, gate_ref, slots, sems) = weight_refs(rest, narrow)
     slot = weights_of_step(narrow, layer, where_ref, shard_ref, twin_ref, mine, other, slots, sems)
     low = low_ref[...]
     a = matmul(low, slot[0]) + shift_a_ref[...]
     g = matmul(low, slot[1]) + shift_g_ref[...]
+    gate = jax.nn.sigmoid(g)
+    cdf = 0.5 * (1.0 + lax.erf(a * ROOT_HALF))
     a_ref[...] = a
-    g_ref[...] = g
-    gate = jax.nn.sigmoid(g)
-    following = gate * carry_ref[...] + (1.0 - gate) * gelu_curve(a)
+    cdf_ref[...] = cdf
+    gate_ref[...] = gate
+    following = gate * carry_ref[...] + (1.0 - gate) * (a * cdf)
     next_ref[...] = following
     low_next_ref[...] = following.astype(jnp.bfloat16)
 
 
 def mix_forward(layer, where, low, carry, shift, shard, twin, mine, other):
-    narrow = other.shape[0]
+    narrow = len(mine)
     words, filters = carry.shape
     part = filters // narrow
-    flat = [*jax.tree.leaves(mine), other]
+    flat = jax.tree.leaves((mine, other))
     block = pl.BlockSpec((words, part), lambda i, where: (0, where[0] ^ i))
     return pl.pallas_call(
         functools.partial(mix_forward_body, narrow, layer),
@@ -486,16 +744,16 @@
                 pl.BlockSpec((1, part), lambda i, where: (0, narrow + (where[0] ^ i))),
             ]
             + [pl.BlockSpec(memory_space=pl.ANY)] * (2 + len(flat)),
-            out_specs=[block] * 4,
+            out_specs=[block] * 5,
             scratch_shapes=[
                 pltpu.VMEM((2, 2, filters, part), jnp.bfloat16),
                 pltpu.SemaphoreType.DMA((2, 4 * (filters // shard.shape[1] // 2))),
             ],
         ),
         out_shape=[
-            jax.ShapeDtypeStruct((words, filters), kind) for kind in (jnp.float32, jnp.bfloat16, jnp.float32, jnp.float32)
+            jax.ShapeDtypeStruct((words, filters), kind) for kind in (jnp.float32, jnp.bfloat16, jnp.float32, jnp.float32, jnp.float32)
         ],
-        compiler_params=pltpu.CompilerParams(vmem_limit_bytes=48 << 20),
+        compiler_params=pltpu.CompilerParams(vmem_limit_bytes=60 << 20),
         cost_estimate=pl.CostEstimate(
             flops=words * filters * filters, bytes_accessed=filters * filters,
             transcendentals=0,
@@ -504,8 +762,8 @@
     )(where, low, carry, shift, shift, shard, twin, *flat)
 
 
-def mix_backward_body(narrow, layer, where_ref, low_ref, carry_ref, a_ref, g_ref, pull_ref, shard_ref, twin_ref, *rest):
-    mine, other, (own_ref, oth_ref, shift_ref, back_ref, slots, low_t_ref, sems) = weight_refs(rest, narrow)
+def mix_backward_body(narrow, layer, where_ref, low_ref, carry_ref, a_ref, cdf_ref, gate_ref, pull_ref, shard_ref, twin_ref, *rest):
+    mine, other, (own_a, own_g, oth_a, oth_g, shift_ref, back_ref, slots, low_t_ref, sems) = weight_refs(rest, narrow)
     slot = weights_of_step(narrow, layer, where_ref, shard_ref, twin_ref, mine, other, slots, sems)
 
     @pl.when(pl.program_id(0) == 0)
@@ -514,18 +772,20 @@
             low_t_ref[start : start + 256, :] = low_ref[:, start : start + 256].T
 
     a = a_ref[...]
-    gate = jax.nn.sigmoid(g_ref[...])
+    cdf = cdf_ref[...]
+    gate = gate_ref[...]
     pull = pull_ref[...]
-    pull_a = ((1.0 - gate) * gelu_slope(a) * pull).astype(jnp.bfloat16)
-    pull_g = (gate * (1.0 - gate) * (carry_ref[...] - gelu_curve(a)) * pull).astype(jnp.bfloat16)
-    half_rows = own_ref.shape[2]
+    rest_pull = (1.0 - gate) * pull
+    pull_a = (rest_pull * (cdf + a * NORMAL_PEAK * jnp.exp(-0.5 * a * a))).astype(jnp.bfloat16)
+    pull_g = (rest_pull * gate * (carry_ref[...] - a * cdf)).astype(jnp.bfloat16)
+    half_rows = own_a.shape[1]
     rows = shard_ref.shape[1]
     for half, grad in enumerate((pull_a, pull_g)):
         shift_ref[half, :, :] = jnp.sum(grad.astype(jnp.float32), axis=0, keepdims=True)
-        for side, out_ref in enumerate((own_ref, oth_ref)):
+        for side, out_ref in enumerate(((own_a, own_g)[half], (oth_a, oth_g)[half])):
             for chip in range(half_rows // rows):
                 start = pl.multiple_of((2 * chip + (where_ref[2] ^ side)) * rows, rows)
-                out_ref[0, half, chip * rows : (chip + 1) * rows, :] = matmul(
+                out_ref[0, chip * rows : (chip + 1) * rows, :] = matmul(
                     low_t_ref[pl.ds(start, rows), :], grad
                 ).astype(jnp.bfloat16)
     back = matmul(pull_a, slot[0], CONTRACT_COLS) + matmul(pull_g, slot[1], CONTRACT_COLS)
@@ -543,25 +803,24 @@
     back_ref[:, pl.ds(column, part)] += gate * pull
 
 
-def mix_backward(layer, where, low, carry, a, g, pull, shard, twin, mine, other):
-    narrow = other.shape[0]
+def mix_backward(layer, where, low, carry, a, cdf, gate, pull, shard, twin, mine, other):
+    narrow = len(mine)
     words, filters = carry.shape
     part = filters // narrow
-    flat = [*jax.tree.leaves(mine), other]
+    flat = jax.tree.leaves((mine, other))
     block = pl.BlockSpec((words, part), lambda i, where: (0, where[0] ^ i))
-    grad_block = pl.BlockSpec((1, 2, filters // 2, part), lambda i, where: (i, 0, 0, 0))
-    grad_shape = jax.ShapeDtypeStruct((narrow, 2, filters // 2, part), jnp.bfloat16)
+    grad_block = pl.BlockSpec((1, filters // 2, part), lambda i, where: (i, 0, 0))
+    grad_shape = jax.ShapeDtypeStruct((narrow, filters // 2, part), jnp.bfloat16)
     return pl.pallas_call(
         functools.partial(mix_backward_body, narrow, layer),
         grid_spec=pltpu.PrefetchScalarGridSpec(
             num_scalar_prefetch=1,
             grid=(narrow,),
             in_specs=[pl.BlockSpec((words, filters), lambda i, where: (0, 0))]
-            + [block] * 4
+            + [block] * 5
             + [pl.BlockSpec(memory_space=pl.ANY)] * (2 + len(flat)),
             out_specs=[
-                grad_block,
-                grad_block,
+                *[grad_block] * 4,
                 pl.BlockSpec((2, 1, part), lambda i, where: (0, 0, where[0] ^ i)),
                 pl.BlockSpec((words, filters), lambda i, where: (0, 0)),
             ],
@@ -572,24 +831,17 @@
             ],
         ),
         out_shape=[
-            grad_shape,
-            grad_shape,
+            *[grad_shape] * 4,
             jax.ShapeDtypeStruct((2, 1, filters), jnp.float32),
             jax.ShapeDtypeStruct((words, filters), jnp.float32),
         ],
-        compiler_params=pltpu.CompilerParams(vmem_limit_bytes=56 << 20),
+        compiler_params=pltpu.CompilerParams(vmem_limit_bytes=60 << 20),
         cost_estimate=pl.CostEstimate(
             flops=words * filters * filters, bytes_accessed=filters * filters,
             transcendentals=0,
         ),
         name="mix_backward",
-    )(where, low, carry, a, g, pull, shard, twin, *flat)
-
-
-def as_rows(value, lanes):
-    count, size = value.shape
-    lines = -(-size // lanes)
-    return jnp.pad(value, ((0, 0), (0, lines * lanes - size))).reshape(count * lines, lanes)
+    )(where, low, carry, a, cdf, gate, pull, shard, twin, *flat)
 
 
 def from_rows(rows, count, size):
@@ -604,14 +856,6 @@
     lines = -(-size // lanes)
     value = value.reshape(count, wide, size).transpose(1, 0, 2)
     return jnp.pad(value, ((0, 0), (0, 0), (0, lines * lanes - size))).reshape(wide, count * lines, lanes)
-
-
-def split_rows(rows, sizes):
-    pieces, start = [], 0
-    for size in sizes:
-        pieces.append(rows[..., start : start + size, :])
-        start += size
-    return pieces
 
 
 def shards(
@@ -655,37 +899,38 @@
     model_width = embed_gain.shape[0] * wide
     vocab = char_table.shape[0] * wide // CDIM
 
-    conv_block = jnp.concatenate([jnp.pad(k, ((0, TAP - k.shape[0]), (0, 0))) for k in convs], axis=1)
-    model_rows = jnp.concatenate([type_table, embed_gain[None], embed_biases, layer_gains, layer_biases], axis=0)
-    small = [
-        conv_block,
-        conv_bias[None],
-        as_rows(highway_bias, lanes),
-        as_rows(model_rows, lanes),
-        as_rows(ff_in_bias[None], lanes),
-        as_rows(char_table[None], lanes),
-    ]
-    small_sizes = [piece.shape[0] for piece in small]
-    padding = -sum(small_sizes) % 16
-    small_block = jnp.concatenate(small + [jnp.zeros((padding, lanes), jnp.bfloat16)], axis=0)
+    kernel_sizes = [kernel.shape[1] for kernel in convs]
+    kernel_rows = [kernel.shape[0] for kernel in convs]
+    early = [conv_bias[None], highway_bias, type_table, embed_gain[None], embed_biases, layer_gains, layer_biases, ff_in_bias[None]]
+    late = char_table[None]
+    lines = lambda value: value.shape[0] * -(-value.shape[1] // lanes)
+    early_count = sum(map(lines, early))
+    early_count += -early_count % 8
+    late_count = lines(late)
+    late_count += -late_count % 8
+    late_count += (early_count + late_count) % 16
+    small_rows = TAP + early_count + late_count
+    starts = [TAP + sum(map(lines, early[:i])) for i in range(len(early))] + [TAP + early_count]
+    small_block = make_share(convs, early + [late], starts, small_rows, lanes)
+    columns = [own_columns(highway_weight, number, place, narrow) for number in range(2)]
+    small_block, columns = tie(small_block, columns)
     everyone = lax.all_gather(small_block, "wide", axis=0, tiled=False)
 
-    conv_rows, bias_rows, mix_rows, model_rows, inner_rows, table_rows = split_rows(everyone, small_sizes)
-    top, start = [], 0
-    for kernel in convs:
-        size = kernel.shape[1]
-        top.append(conv_rows[:, :, start : start + size].transpose(1, 0, 2).reshape(TAP, wide * size))
-        start += size
-    channels = [kernel.shape[1] * wide for kernel in convs]
+    kern = make_kernel(everyone, kernel_sizes)
+    channels = [size * wide for size in kernel_sizes]
     width_of = jnp.concatenate([jnp.full((1, count), k + 1, jnp.int32) for k, count in enumerate(channels)], axis=1)
-    mask_rows = (width_of == lax.broadcasted_iota(jnp.int32, (KROWS - TAP - 1, 1), 0) + 1).astype(jnp.bfloat16)
-    kern = jnp.concatenate([jnp.concatenate(top, axis=1), from_rows(bias_rows, 1, lanes), mask_rows], axis=0)
-    highway_shift = from_rows(mix_rows, 2, highway_bias.shape[1]).astype(jnp.float32)
-    vectors = from_rows(model_rows, 13, embed_gain.shape[0]).astype(jnp.float32)
-    type_vectors, embed_gain_full, embed_shift = vectors[0:2], vectors[2], vectors[3:5]
-    gain_rows, shift_rows = vectors[5:7], vectors[7:13]
-    inner_shift = from_rows(inner_rows, 1, ff_in_bias.shape[0])[0].astype(jnp.float32)
-    table = from_rows(table_rows, 1, char_table.shape[0]).reshape(vocab, CDIM)
+    def whole(number, count, size):
+        first = starts[number]
+        return from_rows(everyone[:, first : first + count * -(-size // lanes)], count, size)
+
+    model_size = embed_gain.shape[0]
+    highway_shift = whole(1, 2, highway_bias.shape[1]).astype(jnp.float32)
+    vectors = whole(2, 13, model_size).astype(jnp.float32)
+    inner_shift = whole(7, 1, ff_in_bias.shape[0]).astype(jnp.float32)
+    table = whole(8, 1, char_table.shape[0]).reshape(vocab, CDIM)
+    type_vectors, embed_gain_full, embed_shift = vectors[0:2], vectors[2:3], (vectors[3:4], vectors[4:5])
+    gain_rows = (vectors[5:6], vectors[6:7])
+    shift_rows = [vectors[7 + i : 8 + i] for i in range(6)]
 
     seq_count, seq_len, char_slots = char_ids.shape
     word_count = seq_count * seq_len
@@ -705,37 +950,35 @@
 
     def stacked_rows(pieces):
         value = jnp.concatenate(pieces, axis=0)
-        return jnp.pad(value, ((0, -value.shape[0] % 16), (0, 0)))
+        return jnp.pad(value, ((0, -value.shape[0] % (16 * narrow)), (0, 0)))
 
     def side_by_side(value):
         return [value[:, i : i + model_width] for i in range(0, value.shape[1], model_width)]
 
     deep_one = stacked_rows([projection, position_table] + side_by_side(qkv_weight) + [out_weight])
     deep_two = stacked_rows(side_by_side(ff_in) + [ff_out])
-    kern, mix_shards, deep_one, deep_two = tie(kern, highway_weight, deep_one, deep_two)
     chips = wide // 2
-    stacks = [gather_chips(own_columns(mix_shards[number], place, narrow), wide) for number in range(2)]
+    stacks = [gather_chips(column, wide) for column in columns]
     state = []
-    for call in range(blocks):
-        state = conv_forward(call, ids, counts, tables, kern, state)
-    stacks[0], state, deep_one = tie(stacks[0], state, deep_one)
+    state = conv_forward(0, blocks // 2, ids, counts, tables, kern, state)
+    stacks[0], state, deep_two = tie(stacks[0], state, deep_two)
+    stacks.append(gather_chips(own_rows(deep_two, place, narrow), wide))
     known = [{0: other_chips(stacks[0], index // 2)}, None]
     spread_level(known[0], narrow, 1)
+    state = conv_forward(blocks // 2, blocks - blocks // 2, ids, counts, tables, kern, state)
+    known[0], state, stacks[1], deep_one = tie(known[0], state, stacks[1], deep_one)
+    for level in levels[1:]:
+        spread_level(known[0], narrow, level)
+    twin = core_swap(highway_weight, wide)
+    other = [swap_early(known[0], narrow, wide)]
+    full_one = lax.all_gather(deep_one, "wide", axis=0, tiled=False)
     windows, totals = state
     places = (jnp.maximum(counts - width_of, 0) + 1).astype(jnp.float32)
     pooled = jnp.log(totals / places)
     carried = gelu_curve(pooled)
     low_state = carried.astype(jnp.bfloat16)
-    known[0], stacks[1], mix_shards, low_state, deep_one, deep_two = tie(
-        known[0], stacks[1], mix_shards, low_state, deep_one, deep_two
-    )
-    for level in levels[1:]:
-        spread_level(known[0], narrow, level)
-    twin = core_swap(mix_shards, wide)
-    full_one = lax.all_gather(deep_one, "wide", axis=0, tiled=False)
-    full_two = lax.all_gather(deep_two, "wide", axis=0, tiled=False)
-    known[0], twin, stacks[1] = tie(known[0], twin, stacks[1])
-    other = swap_known(known[0], narrow, wide)
+    known[0], twin, other, stacks[1], low_state = tie(known[0], twin, other, stacks[1], low_state)
+    other += swap_late(known[0], narrow, wide)
     known[1] = {0: other_chips(stacks[1], index // 2)}
     spread_level(known[1], narrow, 1)
     states, low_states, mixes, mixers = [], [], [], []
@@ -745,19 +988,25 @@
         mixers.append((mine, other))
         low_states.append(low_state)
         states.append(carried)
-        carried, low_state, mix_a, mix_g = mix_forward(
-            number, where, low_state, carried, highway_shift[number][None], highway_weight, twin, mine, other
+        carried, low_state, *kept = mix_forward(
+            number, where, low_state, carried, highway_shift[number : number + 1], highway_weight, twin, mine, other
         )
-        mixes.append((mix_a, mix_g))
+        mixes.append(kept)
         return carried, low_state
 
     carried, low_state = mix(0, carried, low_state, other)
     known[1], carried, low_state = tie(known[1], carried, low_state)
     for level in levels[1:]:
         spread_level(known[1], narrow, level)
-    known[1], low_state = tie(known[1], low_state)
-    carried, low_top = mix(1, carried, low_state, swap_known(known[1], narrow, wide))
-    full_one, low_top = tie(full_one, low_top)
+    other = [swap_early(known[1], narrow, wide)]
+    known[1], low_state, other, stacks[2] = tie(known[1], low_state, other, stacks[2])
+    known.append({0: jnp.concatenate([stacks[2][chip] for chip in range(chips)], axis=1)})
+    spread_level(known[2], narrow, 1)
+    carried, low_top = mix(1, carried, low_state, other + swap_late(known[1], narrow, wide))
+    full_one, known[2], low_top = tie(full_one, known[2], low_top)
+    for level in levels[1:]:
+        spread_level(known[2], narrow, level)
+    other = [swap_early(known[2], narrow, wide)]
 
     def taken(full, sizes):
         pieces, start = [], 0
@@ -770,39 +1019,26 @@
     projection_full, position_full, *qkv_parts, out_full = taken(
         full_one, [projection.shape[0], position_table.shape[0]] + [deep_rows] * 4
     )
-    qkv_full = jnp.concatenate(qkv_parts, axis=1)
     position_rows = jnp.tile(position_full.astype(jnp.float32), (seq_count, 1))
     embed_sum = (
         matmul(low_top, projection_full)
         + embed_shift[0]
         + position_rows
-        + type_vectors[0] * (1.0 - type_one)
-        + type_vectors[1] * type_one
+        + type_vectors[0:1] * (1.0 - type_one)
+        + type_vectors[1:2] * type_one
     )
     embedded = normalize(embed_sum, embed_gain_full, embed_shift[1])
     low_in = embedded.astype(jnp.bfloat16)
-    bias_full = jnp.concatenate([shift_rows[0], jnp.zeros_like(shift_rows[0]), shift_rows[1]])
-    projected = (matmul(low_in, qkv_full) + bias_full).astype(jnp.bfloat16)
-    proj_seqs = projected.reshape(seq_count, seq_len, -1)
-    context_seqs, log_totals = lax.map(lambda seq_pair: attend(seq_pair[0], seq_pair[1]), (proj_seqs, lengths))
-    context = context_seqs.reshape(word_count, -1)
-    full_two, context = tie(full_two, context)
-    position_rows = jnp.tile(position_full.astype(jnp.float32), (seq_count, 1))
-    embed_sum = (
-        matmul(low_top, projection_full)
-        + embed_shift[0]
-        + position_rows
-        + type_vectors[0] * (1.0 - type_one)
-        + type_vectors[1] * type_one
-    )
-    embedded = normalize(embed_sum, embed_gain_full, embed_shift[1])
-    low_in = embedded.astype(jnp.bfloat16)
-    bias_full = jnp.concatenate([shift_rows[0], jnp.zeros_like(shift_rows[0]), shift_rows[1]])
-    projected = (matmul(low_in, qkv_full) + bias_full).astype(jnp.bfloat16)
-    proj_seqs = projected.reshape(seq_count, seq_len, -1)
-    context_seqs, log_totals = lax.map(lambda seq_pair: attend(seq_pair[0], seq_pair[1]), (proj_seqs, lengths))
-    context = context_seqs.reshape(word_count, -1)
-    full_two, context = tie(full_two, context)
+    queries = (matmul(low_in, qkv_parts[0]) + shift_rows[0]).astype(jnp.bfloat16)
+    keys = matmul(low_in, qkv_parts[1]).astype(jnp.bfloat16)
+    values = (matmul(low_in, qkv_parts[2]) + shift_rows[1]).astype(jnp.bfloat16)
+    sequences = [slice(i * seq_len, (i + 1) * seq_len) for i in range(seq_count)]
+    attended = [
+        attend(lengths[i : i + 1], queries[rows], keys[rows], values[rows]) for i, rows in enumerate(sequences)
+    ]
+    context = jnp.concatenate([pair[0] for pair in attended], axis=0)
+    known[2], other, context = tie(known[2], other, context)
+    full_two = assemble(where, known[2], other + swap_late(known[2], narrow, wide), wide)
     *inner_parts, ff_out_full = taken(full_two, [deep_rows] * (ff_in.shape[1] // model_width) + [ff_out.shape[0]])
     ff_in_full = jnp.concatenate(inner_parts, axis=1)
     first_in = embedded + matmul(context, out_full) + shift_rows[2]
@@ -818,35 +1054,39 @@
     norm_pull = jax.vjp(normalize, second_in, gain_rows[1], shift_rows[5])[1]
     grad_second, grad_gain_two, grad_shift_five = norm_pull(grad_top)
     grad_ffn = grad_second.astype(jnp.bfloat16)
-    grad_shift_four = jnp.sum(grad_ffn, axis=0, dtype=jnp.float32)
+    grad_shift_four = jnp.sum(grad_ffn, axis=0, keepdims=True, dtype=jnp.float32)
     weight_ff_out = matmul(activated, grad_ffn, CONTRACT_ROWS)
     grad_inner = (matmul(grad_ffn, ff_out_full, CONTRACT_COLS) * gelu_slope(inner_pre)).astype(jnp.bfloat16)
-    grad_ff_bias = jnp.sum(grad_inner, axis=0, dtype=jnp.float32)
+    grad_ff_bias = jnp.sum(grad_inner, axis=0, keepdims=True, dtype=jnp.float32)
     weight_ff_in = matmul(low_first, grad_inner, CONTRACT_ROWS)
     grad_first = grad_second + matmul(grad_inner, ff_in_full, CONTRACT_COLS)
     norm_pull = jax.vjp(normalize, first_in, gain_rows[0], shift_rows[3])[1]
     grad_res, grad_gain_one, grad_shift_three = norm_pull(grad_first)
     grad_attn = grad_res.astype(jnp.bfloat16)
-    grad_shift_two = jnp.sum(grad_attn, axis=0, dtype=jnp.float32)
+    grad_shift_two = jnp.sum(grad_attn, axis=0, keepdims=True, dtype=jnp.float32)
     weight_out = matmul(context, grad_attn, CONTRACT_ROWS)
     grad_context = matmul(grad_attn, out_full, CONTRACT_COLS).astype(jnp.bfloat16)
-    grad_seqs = lax.map(
-        lambda seq_quad: attend_back(seq_quad[0], seq_quad[1], seq_quad[2], seq_quad[3]),
-        (proj_seqs, log_totals, grad_context.reshape(seq_count, seq_len, -1), lengths),
+    grad_proj = jnp.concatenate(
+        [
+            attend_back(lengths[i : i + 1], queries[rows], keys[rows], values[rows], grad_context[rows], attended[i][1])
+            for i, rows in enumerate(sequences)
+        ],
+        axis=1,
     )
-    grad_proj = grad_seqs.reshape(word_count, -1)
-    grad_shift_zero = jnp.sum(grad_proj[:, :model_width], axis=0, dtype=jnp.float32)
-    grad_shift_one = jnp.sum(grad_proj[:, 2 * model_width :], axis=0, dtype=jnp.float32)
-    weight_qkv = matmul(low_in, grad_proj, CONTRACT_ROWS)
-    grad_embedded = grad_res + matmul(grad_proj, qkv_full, CONTRACT_COLS)
+    grad_shift_zero = jnp.sum(grad_proj[0], axis=0, keepdims=True, dtype=jnp.float32)
+    grad_shift_one = jnp.sum(grad_proj[2], axis=0, keepdims=True, dtype=jnp.float32)
+    weight_qkv = [matmul(low_in, grad_proj[i], CONTRACT_ROWS) for i in range(3)]
+    grad_embedded = grad_res
+    for i in range(3):
+        grad_embedded = grad_embedded + matmul(grad_proj[i], qkv_parts[i], CONTRACT_COLS)
     norm_pull = jax.vjp(normalize, embed_sum, embed_gain_full, embed_shift[1])[1]
     grad_sum, grad_embed_gain, grad_embed_shift = norm_pull(grad_embedded)
     grad_embed = grad_sum.astype(jnp.bfloat16)
-    grad_embed_zero = jnp.sum(grad_embed, axis=0, dtype=jnp.float32)
+    grad_embed_zero = jnp.sum(grad_embed, axis=0, keepdims=True, dtype=jnp.float32)
     grad_position = jnp.sum(grad_embed.reshape(seq_count, seq_len, -1), axis=0, dtype=jnp.float32)
     type_mask = type_one.astype(jnp.bfloat16)
-    grad_type_one = jnp.sum(grad_embed * type_mask, axis=0, dtype=jnp.float32)
-    grad_type_zero = jnp.sum(grad_embed * (1 - type_mask), axis=0, dtype=jnp.float32)
+    grad_type_one = jnp.sum(grad_embed * type_mask, axis=0, keepdims=True, dtype=jnp.float32)
+    grad_type_zero = jnp.sum(grad_embed * (1 - type_mask), axis=0, keepdims=True, dtype=jnp.float32)
     weight_proj = matmul(low_top, grad_embed, CONTRACT_ROWS)
     grad_carry = matmul(grad_embed, projection_full, CONTRACT_COLS)
 
@@ -872,19 +1112,19 @@
 
     first_sum, first_sizes = reduce_wide([weight_ff_out, weight_ff_in])
 
-    shift_high, weight_high = [None, None], [None, None]
+    shift_high = [None, None]
+    mix_starts = [starts[1], starts[1] + (starts[2] - starts[1]) // 2]
 
     def unmix(number, pull):
-        mix_a, mix_g = mixes[number]
-        own_part, other_part, shift_grad, back = mix_backward(
-            number, where, low_states[number], states[number], mix_a, mix_g, pull, highway_weight, twin, *mixers[number]
+        *parts, shift_grad, back = mix_backward(
+            number, where, low_states[number], states[number], *mixes[number], pull, highway_weight, twin, *mixers[number]
         )
-        shift_high[number] = shift_grad.reshape(2 * filters)
-        return own_part, other_part, back
+        shift_high[number] = shift_grad.reshape(1, 2 * filters)
+        return parts[:2], parts[2:], back
 
 
     def begun(own_part, got):
-        return [(own_part[:, half], got[:, half]) for half in range(2)]
+        return list(zip(own_part, got))
 
     def send_home(terms):
         blocks = [add_low(parts[0], arrived[0]).reshape(chips, -1, parts.shape[-1]) for parts, arrived in terms]
@@ -901,15 +1141,21 @@
         return jnp.concatenate(pieces, axis=1).astype(jnp.float32)
 
     def convolve_back(first, last, state):
-        for call in range(first, last):
-            state = conv_backward(call, ids.T, windows, scaled, kern, state)
-        return state
+        return conv_backward(first, last - first, ids.T, windows, scaled, kern, state)
 
     rounds = range(narrow.bit_length() - 1)
     rounds = range(narrow.bit_length() - 1)
+
+    def swap_axis(value, turn):
+        split = value.shape[0] // 2
+        return [hop(value[half * split : (half + 1) * split], narrow, bits_of(narrow, half)[turn]) for half in range(2)]
+
+    def add_swapped(value, arrived):
+        return add_low(value, jnp.concatenate(arrived, axis=0))
+
     own_one, other_one, pull = unmix(1, grad_carry)
-    got_one = core_swap(other_one, wide)
-    second_parts = [weight_out.astype(jnp.bfloat16), weight_qkv.astype(jnp.bfloat16), weight_proj.astype(jnp.bfloat16)]
+    got_one = [core_swap(value, wide) for value in other_one]
+    second_parts = [value.astype(jnp.bfloat16) for value in (weight_out, *weight_qkv, weight_proj)]
     got_one, second_parts, pull = tie(got_one, second_parts, pull)
     second_sum, second_sizes = reduce_wide(second_parts + [grad_position])
     terms_one = collect_round(begun(own_one, got_one), narrow, 0)
@@ -919,7 +1165,7 @@
     terms_one, own_zero, other_zero, pull = tie(
         [(parts, sent) for parts, (_, sent) in zip(staying, terms_one)], own_zero, other_zero, pull
     )
-    got_zero = core_swap(other_zero, wide)
+    got_zero = [core_swap(value, wide) for value in other_zero]
     for turn in rounds[1:]:
         terms_one = collect_round(terms_one, narrow, turn)
     scaled = pull * gelu_slope(pooled) / totals
@@ -934,32 +1180,22 @@
     state = convolve_back(blocks // 2, blocks * 3 // 4, state)
     state, terms_zero, first_sum, second_sum = tie(state, terms_zero, first_sum, second_sum)
     home_zero = send_home(terms_zero)
-    deep_sum = jnp.concatenate([first_sum, second_sum], axis=0)
-    deep_half = deep_sum.shape[0] // 2
-
-    def swap_axis(value, turn):
-        return [
-            hop(value[half * deep_half : (half + 1) * deep_half], narrow, bits_of(narrow, half)[turn]) for half in range(2)
-        ]
-
-    def add_swapped(value, arrived):
-        return add_low(value, jnp.concatenate(arrived, axis=0))
-
-    arrived = swap_axis(deep_sum, 0)
+    second_sent = swap_axis(second_sum, 0)
+    first_sent = swap_axis(first_sum, 0)
     state = convolve_back(blocks * 3 // 4, blocks, state)
-    state, home_one, deep_sum, arrived = tie(state, home_one, deep_sum, arrived)
+    state, home_one, second_sum, second_sent, first_sum, first_sent = tie(
+        state, home_one, second_sum, second_sent, first_sum, first_sent
+    )
     total_one = {0: home_one}
     spread_level(total_one, narrow, 1)
-    deep_sum = add_swapped(deep_sum, arrived)
-    arrived = swap_axis(deep_sum, 1)
+    first_sum = add_swapped(first_sum, first_sent)
+    second_sum = add_swapped(second_sum, second_sent)
+    for turn in rounds[1:]:
+        first_sum = add_swapped(first_sum, swap_axis(first_sum, turn))
+        second_sum = add_swapped(second_sum, swap_axis(second_sum, turn))
     kern_grad, table_grad = state
     table_grad = table_grad[:vocab].reshape(vocab, 8, CDIM).sum(axis=1)
-    conv_rows, start = [], 0
-    for count in channels:
-        part = kern_grad[:TAP, start : start + count].reshape(TAP, wide, count // wide)
-        conv_rows.append(part.transpose(1, 0, 2))
-        start += count
-    model_grads = jnp.stack(
+    model_grads = jnp.concatenate(
         [
             grad_type_zero,
             grad_type_one,
@@ -976,16 +1212,11 @@
             grad_shift_five,
         ]
     )
-    small = [
-        jnp.concatenate(conv_rows, axis=2),
-        to_rows(kern_grad[TAP : TAP + 1], wide, lanes),
-        to_rows(jnp.stack(shift_high), wide, lanes),
-        to_rows(model_grads, wide, lanes),
-        to_rows(grad_ff_bias[None], wide, lanes),
-        to_rows(table_grad.reshape(1, -1), wide, lanes),
-        jnp.zeros((wide, padding, lanes), jnp.float32),
-    ]
-    small_part = jnp.concatenate(small, axis=1).astype(jnp.bfloat16).reshape(chips, 2, -1, lanes)
+    late_rows = to_rows(table_grad.reshape(1, -1), wide, lanes)
+    late_rows = jnp.pad(late_rows, ((0, 0), (0, late_count - late_rows.shape[1]), (0, 0)))
+    small_part = make_shares(
+        kern_grad, [*shift_high, model_grads, grad_ff_bias], late_rows, kernel_sizes, [*mix_starts, starts[2], starts[7]], small_rows
+    ).reshape(chips, 2, -1, lanes)
 
     def exchange(value, at, bit):
         side = (index // bit) % 2
@@ -995,10 +1226,7 @@
         return lax.dynamic_index_in_dim(value, side, at, keepdims=False), got
 
     kept, got = exchange(small_part, 1, 1)
-    got, total_one, home_zero, deep_sum, arrived = tie(got, total_one, home_zero, deep_sum, arrived)
-    deep_sum = add_swapped(deep_sum, arrived)
-    for turn in rounds[2:]:
-        deep_sum = add_swapped(deep_sum, swap_axis(deep_sum, turn))
+    got, total_one, home_zero, first_sum, second_sum = tie(got, total_one, home_zero, first_sum, second_sum)
     total_zero = {0: home_zero}
     spread_level(total_zero, narrow, 1)
     for level in levels[1:]:
@@ -1014,38 +1242,35 @@
         spread_level(total_zero, narrow, level)
     small_sum = small_sum[0].astype(jnp.float32)
     for bit in bits_of(narrow, 0):
-        small_sum = small_sum + hop(small_sum.astype(jnp.bfloat16), narrow, bit).astype(jnp.float32)
+        small_got = hop(small_sum.astype(jnp.bfloat16), narrow, bit)
+        if bit > 1:
+            small_sum = small_sum + small_got.astype(jnp.float32)
     weight_high = [laid_out(total_zero), laid_out(total_one)]
-    grad_ff_out_sum, grad_ff_in_sum = split_deep(deep_sum[: first_sum.shape[0]], first_sizes)
-    grad_out_sum, grad_qkv_sum, grad_projection_sum, grad_position_sum = split_deep(
-        deep_sum[first_sum.shape[0] :], second_sizes
+    grad_ff_out_sum, grad_ff_in_sum = split_deep(first_sum, first_sizes)
+    grad_out_sum, *grad_qkv_sums, grad_projection_sum, grad_position_sum = split_deep(second_sum, second_sizes)
+    grad_qkv_sum = jnp.concatenate(grad_qkv_sums, axis=1)
+    *conv_grads, bias_sum, mix_sum, type_sum, gain_sum, norm_sum, gains_sum, biases_sum, inner_sum, table_sum = take_apart(
+        small_sum, small_got, kernel_sizes, kernel_rows, starts, [value.shape for value in early + [late]]
     )
-    conv_sum, bias_sum, mix_sum, model_sum, inner_sum, table_sum = split_rows(small_sum, small_sizes)
-    conv_grads, start = [], 0
-    for kernel in convs:
-        conv_grads.append(conv_sum[: kernel.shape[0], start : start + kernel.shape[1]])
-        start += kernel.shape[1]
-    mix_sum = from_rows(mix_sum[None], 2, highway_bias.shape[1])
-    model_sum = from_rows(model_sum[None], 13, embed_gain.shape[0])
     return (
         hidden_out,
-        from_rows(table_sum[None], 1, char_table.shape[0])[0],
+        table_sum[0],
         *conv_grads,
         bias_sum[0],
         jnp.stack(weight_high),
         mix_sum,
         grad_projection_sum,
         grad_position_sum,
-        model_sum[0:2],
-        model_sum[2],
-        model_sum[3:5],
+        type_sum,
+        gain_sum[0],
+        norm_sum,
         grad_qkv_sum,
         grad_out_sum,
         grad_ff_in_sum,
-        from_rows(inner_sum[None], 1, ff_in_bias.shape[0])[0],
+        inner_sum[0],
         grad_ff_out_sum,
-        model_sum[5:7],
-        model_sum[7:13],
+        gains_sum,
+        biases_sum,
     )
 
 

time: 827 us -> 749 us (0.906)
  waiting for transfers between devices: 179 us -> 106 us
  Pallas kernels: 247 us -> 306 us
  local copies, waits for them, and re-layouts: 153 us -> 111 us
  matrix products: 72.3 us -> 46.9 us
    pallas_call x4 -> x10, Pallas kernels: 96.8 us -> 153 us  [the longest x3 106 us: conv_backward(): pl.pallas_call(functools.partial(conv_bwd_body, block, filters), grid=(co...]
    unnamed x242 -> x249, local copies, waits for them, and re-layouts: 85.6 us -> 54.1 us
    all_gather x2 -> x3, waiting for transfers between devices: 32.9 us -> 5.33 us  [gather_chips(): lax.all_gather(own, 'wide', axis=0, tiled=False, axis_index_groups=chip_g...]
    dot_general x6 -> x0, matrix products: 23.1 us -> none  [the longest x1 10.9 us: attend_back(): jnp.einsum('qhe,khe->hqk', grad_heads, heads_all[:, 2], preferred_element...]
    all_gather x1 -> x0, waiting for transfers between devices: 18.8 us -> none  [shards(): full_two = lax.all_gather(deep_two, 'wide', axis=0, tiled=False)]
    ppermute x30 -> x38, waiting for transfers between devices: 104 us -> 89.2 us  [hop(): return lax.ppermute(value, 'narrow', [(i, i ^ bit) for i in range(narrow)])]
    ppermute x5 -> x11, waiting for transfers between devices: 19.3 us -> 9.09 us  [core_swap(): return lax.ppermute(value, 'wide', [(i, i ^ 1) for i in range(wide)])]
    ppermute x30 -> x38, starting transfers between devices: 34.1 us -> 40.6 us  [hop(): return lax.ppermute(value, 'narrow', [(i, i ^ bit) for i in range(narrow)])]
  transfers between devices with their start and end apart: 46 -> 60, of which waited for: 21 -> 20; matrix products, arithmetic and copies ran while one was open for 24% -> 22% of each run, Pallas kernels for 30% -> 40%
where the time goes in v2:
time: 749 us; the launch traced here: 739 us
  Pallas kernels  306 us (41%)
  local copies, waits for them, and re-layouts  111 us (15%)
  waiting for transfers between devices  106 us (14%)
  other arithmetic  89.4 us (12%)
  matrix products  46.9 us (6%)
  starting transfers between devices  44.3 us (6%)
  blocking collectives  17.8 us (2%)
  between operations  17.2 us (2%)
    pallas_call x3, Pallas kernels, conv_backward(): pl.pallas_call(functools.partial(conv_bwd_body, block, filters), grid=(co...  106 us
    ppermute x38, waiting for transfers between devices, hop(): return lax.ppermute(value, 'narrow', [(i, i ^ bit) for i in range(narrow)])  89.2 us
    pallas_call x2, Pallas kernels, mix_backward(): pl.pallas_call(functools.partial(mix_backward_body, narrow, layer), grid_...  68.8 us
    unnamed x249, local copies, waits for them, and re-layouts  54.1 us
    dot_general x21, matrix products, matmul(): lax.dot_general(left, right, dims, preferred_element_type=jnp.float32)  46.9 us
    pallas_call x2, Pallas kernels, conv_forward(): pl.pallas_call(functools.partial(conv_fwd_body, block, filters, len(state...  43.3 us
    pallas_call x2, Pallas kernels, mix_forward(): pl.pallas_call(functools.partial(mix_forward_body, narrow, layer), grid_s...  41.1 us
    ppermute x38, starting transfers between devices, hop(): return lax.ppermute(value, 'narrow', [(i, i ^ bit) for i in range(narrow)])  40.6 us
  transfers between devices with their start and end apart: 60, of which 20 were waited for; matrix products, arithmetic and copies ran while one was open for 22% of the time, Pallas kernels for 40%

profile of v2, /device:TPU:0, one launch (start us, length us, event | category | flops | bytes accessed | tf_op | source)
XLA Modules:
  0.0 738.7 jit_solution(13927382298842595742)
XLA Ops:
  17.4 17.8 %all-gather.1 = bf16[1152,256]{1,0:T(8,128)(2,1)S(1)} all-gather(bf16[144,256]{1,0:T(8,128)(2,1)} %make_share.1), channel_id=3, replica_groups=mesh['narrow'=4,'wide'=8] {'wide'}, dimensions={0}, use_global_device_ids=true | all-gather | bytes 663552 | tf_op jit(solution)/shard_map/all_gather | solution.py:917
  36.1 2.3 make_kernel.1.kern_ref
  40.5 21.6 %conv_forward.2 = (bf16[25600,128]{1,0:T(8,128)(2,1)S(1)}, f32[512,2048]{1,0:T(8,128)S(1)}) custom-call(s32[512,50]{1,0:T(8,128)S(1)} %copy.82.ids_ref, s32[512,1]{1,0:T(8,128)S(1)} %copy.83.cnt_ref, bf16[8,384,128]{2,1,0:T(8,128)(2,1)S(1)} %bitcast_dynamic-update-slice_fusion.table_ref, bf16[128,2048]{1,0:T(8,128)(2,1)S(1)} %copy-done.8), custom_call_target="tpu_custom_call" | custom-call | flops 838860800 | bytes 524288 | tf_op jit(solution)/shard_map/conv_forward/pallas_call | solution.py:115
  62.1 2.8 copy-done
  64.9 2.0 copy-done.3
  76.9 2.9 copy-done.1
  79.8 2.2 copy-done.4
  82.0 21.6 %conv_forward.3 = (bf16[25600,128]{1,0:T(8,128)(2,1)S(1)}, f32[512,2048]{1,0:T(8,128)S(1)}) custom-call(s32[512,50]{1,0:T(8,128)S(1)} %copy.82.ids_ref, s32[512,1]{1,0:T(8,128)S(1)} %copy.83.cnt_ref, bf16[8,384,128]{2,1,0:T(8,128)(2,1)S(1)} %bitcast_dynamic-update-slice_fusion.table_ref, ...), custom_call_target="tpu_custom_call", output_to_operand_aliasing={{0}: (4, {}), {1}: (5, {})} | custom-call | flops 838860800 | bytes 524288 | tf_op jit(solution)/shard_map/conv_forward/pallas_call | solution.py:115
  103.6 2.8 copy-done.2
  106.4 2.0 copy-done.5
  108.4 5.3 all-gather.12.cloned.1.call-done
  114.1 2.3 pad_maximum_fusion
  122.9 4.2 fusion.41
  127.2 3.2 collective-permute-done.4.twin_ref
  130.4 8.1 %collective-permute-done.3.rest_4_ = bf16[768,512]{1,0:T(8,128)(2,1)S(1)} collective-permute-done((bf16[768,512]{1,0:T(8,128)(2,1)S(1)}, bf16[768,512]{1,0:T(8,128)(2,1)S(1)}, u32[]{:S(2)}, u32[]{:S(2)}) %collective-permute-start.3) | collective-permute-done | bytes 786464 | tf_op jit(solution)/shard_map/ppermute | solution.py:509
  138.4 2.4 collective-permute-done.2.rest_3_
  147.9 20.7 %mix_forward.2 = (f32[512,2048]{1,0:T(8,128)}, bf16[512,2048]{1,0:T(8,128)(2,1)}, f32[512,2048]{1,0:T(8,128)}, f32[512,2048]{1,0:T(8,128)}, f32[512,2048]{1,0:T(8,128)}) custom-call(s32[3]{0:T(128)} %pad_add_fusion.where_ref, bf16[512,2048]{1,0:T(8,128)(2,1)} %get-tuple-element.199.low_ref, f32[512,2048]{1,0:T(8,128)} %get-tuple-element.383.carry_ref, ...), custom_call_target="tpu_custom_call" | custom-call | flops 2147483648 | bytes 4194304 | tf_op jit(solution)/shard_map/mix_forward/pallas_call | solution.py:735
  168.6 10.8 %collective-permute-done.7.rest_2_ = bf16[2,768,512]{2,1,0:T(8,128)(2,1)S(1)} collective-permute-done((bf16[2,768,512]{2,1,0:T(8,128)(2,1)S(1)}, bf16[2,768,512]{2,1,0:T(8,128)(2,1)S(1)}, u32[]{:S(2)}, u32[]{:S(2)}) %collective-permute-start.7) | collective-permute-done | bytes 1572896 | tf_op jit(solution)/shard_map/ppermute | solution.py:509
  180.7 3.6 pad_maximum_fusion.1
  186.9 18.7 %collective-permute-done.10.rest_4_ = bf16[768,512]{1,0:T(8,128)(2,1)S(1)} collective-permute-done((bf16[768,512]{1,0:T(8,128)(2,1)S(1)}, bf16[768,512]{1,0:T(8,128)(2,1)S(1)}, u32[]{:S(2)}, u32[]{:S(2)}) %collective-permute-start.10) | collective-permute-done | bytes 786464 | tf_op jit(solution)/shard_map/ppermute | solution.py:509
  222.9 20.4 %mix_forward.3 = (f32[512,2048]{1,0:T(8,128)}, bf16[512,2048]{1,0:T(8,128)(2,1)}, f32[512,2048]{1,0:T(8,128)}, f32[512,2048]{1,0:T(8,128)}, f32[512,2048]{1,0:T(8,128)}) custom-call(s32[3]{0:T(128)} %pad_add_fusion.where_ref, bf16[512,2048]{1,0:T(8,128)(2,1)} %get-tuple-element.215.low_ref, f32[512,2048]{1,0:T(8,128)} %get-tuple-element.216.carry_ref, ...), custom_call_target="tpu_custom_call" | custom-call | flops 2147483648 | bytes 4194304 | tf_op jit(solution)/shard_map/mix_forward/pallas_call | solution.py:735
  244.1 2.3 slice.434
  250.9 2.1 fusion.39
  259.1 17.1 %attend.1 = (bf16[512,768]{1,0:T(8,128)(2,1)S(1)}, f32[6,8,512]{2,1,0:T(8,128)S(1)}) custom-call(s32[1]{0:T(128)} %copy.150.length_ref, bf16[512,768]{1,0:T(8,128)(2,1)S(1)} %add_convert_fusion.26.q_ref, bf16[512,768]{1,0:T(8,128)(2,1)S(1)} %convolution_convert_fusion.8.k_ref, bf16[512,768]{1,0:T(8,128)(2,1)S(1)} %add_convert_fusion.25.v_ref), custom_call_target="tpu_custom_call" | custom-call | flops 201326592 | bytes 393216 | tf_op jit(solution)/shard_map/attend/pallas_call | solution.py:307
  279.2 2.7 fusion.55
  282.3 8.5 %assemble.1 = bf16[8,768,768]{2,1,0:T(8,128)(2,1)} custom-call(s32[3]{0:T(128)} %pad_add_fusion.where_ref, bf16[2,768,384]{2,1,0:T(8,128)(2,1)} %copy-done.24, bf16[2,768,384]{2,1,0:T(8,128)(2,1)} %copy-done.31, bf16[2,768,384]{2,1,0:T(8,128)(2,1)} %copy-done.30, bf16[768,384]{1,0:T(8,128)(2,1)} %copy-done.59, bf16[768,384]{1,0:T(8,128)(2,1)} %copy-done.58, ...), custom_call_target="tpu_custom_call" | custom-call | bytes 589824 | tf_op jit(solution)/shard_map/assemble/pallas_call | solution.py:631
  290.8 2.8 slice.553
  293.6 2.3 copy-done.17
  296.3 3.0 multiply_convert_fusion
  299.3 2.8 fusion.56
  304.0 1.9 fusion.38
  307.9 2.9 convolution_convert_fusion.1
  310.8 5.2 convert_reduce_fusion
  316.1 3.5 convolution_convert_fusion
  319.6 2.5 constant_dynamic-update-slice_fusion.4
  326.8 7.8 %multiply_reduce_fusion = (f32[768]{0:T(1024)}, f32[512]{0:T(512)S(1)}, f32[768]{0:T(1024)}, f32[512,768]{1,0:T(8,128)S(1)}) fusion(f32[512,768]{1,0:T(8,128)S(1)} %get-tuple-element.464, f32[512]{0:T(512)S(1)} %fusion.28, f32[512]{0:T(512)S(1)} %broadcast_multiply_fusion.1, f32[768]{0:T(1024)S(1)} %mul.339, bf16[512,3072]{1,0:T(8,128)(2,1)} %copy-done.102, ...), kind=kOutput, calls=%fused_computation.74 | convolution fusion | flops 2438723584 | bytes 12600320 | tf_op jit(solution)/shard_map/dot_general | solution.py:49
  337.9 13.2 %attend_back.1 = bf16[3,512,768]{2,1,0:T(8,128)(2,1)S(1)} custom-call(s32[1]{0:T(128)} %copy.150.length_ref, bf16[512,768]{1,0:T(8,128)(2,1)S(1)} %copy-done.12, bf16[512,768]{1,0:T(8,128)(2,1)S(1)} %copy-done.10, bf16[512,768]{1,0:T(8,128)(2,1)S(1)} %add_convert_fusion.25.v_ref, bf16[512,768]{1,0:T(8,128)(2,1)S(1)} %convolution_convert_fusion.7.pull_ref, ...), custom_call_target="tpu_custom_call" | custom-call | flops 201326592 | bytes 393216 | tf_op jit(solution)/shard_map/attend_back/pallas_call | solution.py:328
  354.2 2.0 multiply_reduce_fusion.1
  358.1 3.8 fusion.57.pull_ref
  361.9 34.7 %mix_backward.2 = (bf16[4,1024,512]{2,1,0:T(8,128)(2,1)}, bf16[4,1024,512]{2,1,0:T(8,128)(2,1)}, bf16[4,1024,512]{2,1,0:T(8,128)(2,1)}, bf16[4,1024,512]{2,1,0:T...) custom-call(s32[3]{0:T(128)} %pad_add_fusion.where_ref, bf16[512,2048]{1,0:T(8,128)(2,1)} %get-tuple-element.215.low_ref, ...), custom_call_target="tpu_custom_call" | custom-call | flops 2147483648 | bytes 4194304 | tf_op jit(solution)/shard_map/mix_backward/pallas_call | solution.py:814
  404.6 5.9 collective-permute-done.20
  418.4 5.7 add_convert_fusion.4
  425.9 2.7 add_convert_fusion.5
  430.0 34.1 %mix_backward.3 = (bf16[4,1024,512]{2,1,0:T(8,128)(2,1)}, bf16[4,1024,512]{2,1,0:T(8,128)(2,1)}, bf16[4,1024,512]{2,1,0:T(8,128)(2,1)}, bf16[4,1024,512]{2,1,0:T...) custom-call(s32[3]{0:T(128)} %pad_add_fusion.where_ref, bf16[512,2048]{1,0:T(8,128)(2,1)} %get-tuple-element.199.low_ref, ...), custom_call_target="tpu_custom_call" | custom-call | flops 2147483648 | bytes 4194304 | tf_op jit(solution)/shard_map/mix_backward/pallas_call | solution.py:814
  464.1 8.1 %collective-permute-done.22 = bf16[2,1024,512]{2,1,0:T(8,128)(2,1)} collective-permute-done((bf16[2,1024,512]{2,1,0:T(8,128)(2,1)}, bf16[2,1024,512]{2,1,0:T(8,128)(2,1)}, u32[]{:S(2)}, u32[]{:S(2)}) %collective-permute-start.22) | collective-permute-done | bytes 2097184 | tf_op jit(solution)/shard_map/ppermute | solution.py:509
  472.2 4.5 collective-permute-done.21
  477.2 3.0 add_convert_fusion.22
  481.2 2.5 add_convert_fusion.20
  484.8 4.7 fusion.9.ginv_ref
  489.5 15.8 %collective-permute-done.23 = bf16[1,1024,512]{2,1,0:T(8,128)(2,1)S(1)} collective-permute-done((bf16[1,1024,512]{2,1,0:T(8,128)(2,1)S(1)}, bf16[1,1024,512]{2,1,0:T(8,128)(2,1)S(1)}, u32[]{:S(2)}, u32[]{:S(2)}) %collective-permute-start.23) | collective-permute-done | bytes 1048608 | tf_op jit(solution)/shard_map/ppermute | solution.py:509
  505.3 3.3 collective-permute-done.24
  508.7 2.8 add_convert_fusion
  512.6 2.7 add_convert_fusion.2
  520.3 51.6 %conv_backward.3 = (f32[128,2048]{1,0:T(8,128)}, f32[272,128]{1,0:T(8,128)}) custom-call(s32[50,512]{1,0:T(8,128)} %get-tuple-element.459.idst_ref, bf16[25600,128]{1,0:T(8,128)(2,1)} %copy-done.2, f32[512,2048]{1,0:T(8,128)} %fusion.9.ginv_ref, bf16[128,2048]{1,0:T(8,128)(2,1)} %make_kernel.1.kern_ref, ...), custom_call_target="tpu_custom_call", output_to_operand_aliasing={{0}: (4, {}), {1}: (5, {})} | custom-call | flops 1677721600 | bytes 524288 | tf_op jit(solution)/shard_map/conv_backward/pallas_call | solution.py:211
  571.9 3.9 add_convert_fusion.18
  576.5 3.5 add_convert_fusion.16
  581.2 26.9 %conv_backward.4 = (f32[128,2048]{1,0:T(8,128)}, f32[272,128]{1,0:T(8,128)}) custom-call(s32[50,512]{1,0:T(8,128)} %get-tuple-element.459.idst_ref, bf16[25600,128]{1,0:T(8,128)(2,1)} %copy-done.2, f32[512,2048]{1,0:T(8,128)} %fusion.9.ginv_ref, bf16[128,2048]{1,0:T(8,128)(2,1)} %make_kernel.1.kern_ref, ...), custom_call_target="tpu_custom_call", output_to_operand_aliasing={{0}: (4, {}), {1}: (5, {})} | custom-call | flops 838860800 | bytes 262144 | tf_op jit(solution)/shard_map/conv_backward/pallas_call | solution.py:211
  620.3 27.1 %conv_backward.5 = (f32[128,2048]{1,0:T(8,128)}, f32[272,128]{1,0:T(8,128)}) custom-call(s32[50,512]{1,0:T(8,128)} %get-tuple-element.459.idst_ref, bf16[25600,128]{1,0:T(8,128)(2,1)} %copy-done.2, f32[512,2048]{1,0:T(8,128)} %fusion.9.ginv_ref, bf16[128,2048]{1,0:T(8,128)(2,1)} %make_kernel.1.kern_ref, ...), custom_call_target="tpu_custom_call", output_to_operand_aliasing={{0}: (4, {}), {1}: (5, {})} | custom-call | flops 838860800 | bytes 262144 | tf_op jit(solution)/shard_map/conv_backward/pallas_call | solution.py:211
  664.5 2.7 concatenate.84.refs_2_
  669.9 2.7 make_shares.1
  676.9 2.6 collective-permute-done.39
  681.0 6.0 collective-permute-done.37
  705.1 3.6 collective-permute-done.51
  727.4 3.9 maximum_convert_fusion
  (522 shorter events, 192.4 us)
Async XLA Ops:
  7.2 59.9 %all-gather.10.cloned.1.call-start = ((), (), s32[]{:S(2)}) async-start(), calls=%async_computation.8 | async-start | bytes 2621440 | tf_op jit(solution)/shard_map/all_gather | solution.py:578
  16.6 97.1 %all-gather.12.cloned.1.call-start = ((), (), s32[]{:S(2)}) async-start(), calls=%async_computation.9 | async-start | bytes 2621440 | tf_op jit(solution)/shard_map/all_gather | solution.py:578
  17.3 169.6 %all-gather.16.cloned.1.call-start = ((), (), s32[]{:S(2)}) async-start(), calls=%async_computation.11 | async-start | bytes 1474560 | tf_op jit(solution)/shard_map/all_gather | solution.py:578
  67.9 175.5 %all-gather.14.cloned.1.call-start = ((), (), s32[]{:S(2)}) async-start(), calls=%async_computation.10 | async-start | bytes 9732096 | tf_op jit(solution)/shard_map/all_gather | solution.py:974
  69.7 44.4 %copy-start.18 = (bf16[2,768,512]{2,1,0:T(8,128)(2,1)}, bf16[2,768,512]{2,1,0:T(8,128)(2,1)S(1)}, u32[]{:S(2)}) copy-start(bf16[2,768,512]{2,1,0:T(8,128)(2,1)S(1)} %pad_maximum_fusion.6.rest_0_) | copy-start | bytes 4718596
  69.7 44.0 %collective-permute-start.1 = (bf16[2,768,512]{2,1,0:T(8,128)(2,1)S(1)}, bf16[2,768,512]{2,1,0:T(8,128)(2,1)}, u32[]{:S(2)}, u32[]{:S(2)}) collective-permute-start(bf16[2,768,512]{2,1,0:T(8,128)(2,1)S(1)} %pad_maximum_fusion.6.rest_0_), channel_id=1, source_target_pairs={{0,16},{8,24},{16,0},{24,8},{1,17},{9,25},{17,1},{25,9},{2,18},{10... | collective-permute-start | bytes 4718600 | tf_op jit(solution)/shard_map/ppermute | solution.py:509
  71.4 42.4 %collective-permute-start = (bf16[2,768,512]{2,1,0:T(8,128)(2,1)S(1)}, bf16[2,768,512]{2,1,0:T(8,128)(2,1)}, u32[]{:S(2)}, u32[]{:S(2)}) collective-permute-start(bf16[2,768,512]{2,1,0:T(8,128)(2,1)S(1)} %pad_maximum_fusion.6.rest_0_), channel_id=1, source_target_pairs={{0,8},{8,0},{16,24},{24,16},{1,9},{9,1},{17,25},{25,17},{2,10},{10... | collective-permute-start | bytes 4718600 | tf_op jit(solution)/shard_map/ppermute | solution.py:509
  113.8 494.3 %reduce-scatter.5.cloned.1.call-start = ((), (), s32[]{:S(2)}) async-start(), calls=%async_computation.4 | async-start | bytes 10616832 | tf_op jit(solution)/shard_map/reduce_scatter | solution.py:1100
  116.4 24.5 %collective-permute-start.5 = (bf16[3,2,768,512]{3,2,1,0:T(8,128)(2,1)S(1)}, bf16[3,2,768,512]{3,2,1,0:T(8,128)(2,1)S(1)}, u32[]{:S(2)}, u32[]{:S(2)}) collective-permute-start(bf16[3,2,768,512]{3,2,1,0:T(8,128)(2,1)S(1)} %pad_maximum_fusion), channel_id=1, source_target_pairs={{0,1},{1,0},{2,3},{3,2},{4,5},{5,4},{6,7},{7,6},{8,9},{9,8},{10,11... | collective-permute-start | bytes 14155784 | tf_op jit(solution)/shard_map/ppermute | solution.py:501
  117.2 13.2 %collective-permute-start.4 = (bf16[2,256,4096]{2,1,0:T(8,128)(2,1)S(1)}, bf16[2,256,4096]{2,1,0:T(8,128)(2,1)S(1)}, u32[]{:S(2)}, u32[]{:S(2)}) collective-permute-start(bf16[2,256,4096]{2,1,0:T(8,128)(2,1)S(1)} %copy-done.15), channel_id=1, source_target_pairs={{0,1},{1,0},{2,3},{3,2},{4,5},{5,4},{6,7},{7,6},{8,9},{9,8},{10,11... | collective-permute-start | bytes 12582920 | tf_op jit(solution)/shard_map/ppermute | solution.py:501
  118.7 19.7 %collective-permute-start.3 = (bf16[768,512]{1,0:T(8,128)(2,1)S(1)}, bf16[768,512]{1,0:T(8,128)(2,1)S(1)}, u32[]{:S(2)}, u32[]{:S(2)}) collective-permute-start(bf16[768,512]{1,0:T(8,128)(2,1)S(1)} %slice_bitcast_fusion.5), channel_id=1, source_target_pairs={{0,8},{8,0},{16,24},{24,16},{1,9},{9,1},{17,25},{25,17},{2,10},{10... | collective-permute-start | bytes 2359304 | tf_op jit(solution)/shard_map/ppermute | solution.py:509
  121.4 19.4 %collective-permute-start.2 = (bf16[768,512]{1,0:T(8,128)(2,1)S(1)}, bf16[768,512]{1,0:T(8,128)(2,1)S(1)}, u32[]{:S(2)}, u32[]{:S(2)}) collective-permute-start(bf16[768,512]{1,0:T(8,128)(2,1)S(1)} %slice_bitcast_fusion.6), channel_id=1, source_target_pairs={{0,16},{8,24},{16,0},{24,8},{1,17},{9,25},{17,1},{25,9},{2,18},{10... | collective-permute-start | bytes 2359304 | tf_op jit(solution)/shard_map/ppermute | solution.py:509
  142.3 5.6 collective-permute-start.8
  143.8 36.9 %copy-start.19 = (bf16[2,768,512]{2,1,0:T(8,128)(2,1)}, bf16[2,768,512]{2,1,0:T(8,128)(2,1)S(1)}, u32[]{:S(2)}) copy-start(bf16[2,768,512]{2,1,0:T(8,128)(2,1)S(1)} %pad_maximum_fusion.7.rest_0_) | copy-start | bytes 4718596
  143.8 35.6 %collective-permute-start.7 = (bf16[2,768,512]{2,1,0:T(8,128)(2,1)S(1)}, bf16[2,768,512]{2,1,0:T(8,128)(2,1)S(1)}, u32[]{:S(2)}, u32[]{:S(2)}) collective-permute-start(bf16[2,768,512]{2,1,0:T(8,128)(2,1)S(1)} %pad_maximum_fusion.7.rest_0_), channel_id=1, source_target_pairs={{0,16},{8,24},{16,0},{24,8},{1,17},{9,25},{17,1},{25,9},{2,18},{10... | collective-permute-start | bytes 4718600 | tf_op jit(solution)/shard_map/ppermute | solution.py:509
  145.2 35.5 %collective-permute-start.6 = (bf16[2,768,512]{2,1,0:T(8,128)(2,1)S(1)}, bf16[2,768,512]{2,1,0:T(8,128)(2,1)}, u32[]{:S(2)}, u32[]{:S(2)}) collective-permute-start(bf16[2,768,512]{2,1,0:T(8,128)(2,1)S(1)} %pad_maximum_fusion.7.rest_0_), channel_id=1, source_target_pairs={{0,8},{8,0},{16,24},{24,16},{1,9},{9,1},{17,25},{25,17},{2,10},{10... | collective-permute-start | bytes 4718600 | tf_op jit(solution)/shard_map/ppermute | solution.py:509
  184.3 21.6 %collective-permute-start.11 = (bf16[3,2,768,512]{3,2,1,0:T(8,128)(2,1)}, bf16[3,2,768,512]{3,2,1,0:T(8,128)(2,1)}, u32[]{:S(2)}, u32[]{:S(2)}) collective-permute-start(bf16[3,2,768,512]{3,2,1,0:T(8,128)(2,1)} %pad_maximum_fusion.1), channel_id=1, source_target_pairs={{0,1},{1,0},{2,3},{3,2},{4,5},{5,4},{6,7},{7,6},{8,9},{9,8},{10,11... | collective-permute-start | bytes 14155784 | tf_op jit(solution)/shard_map/ppermute | solution.py:501
  185.6 20.0 %collective-permute-start.10 = (bf16[768,512]{1,0:T(8,128)(2,1)S(1)}, bf16[768,512]{1,0:T(8,128)(2,1)S(1)}, u32[]{:S(2)}, u32[]{:S(2)}) collective-permute-start(bf16[768,512]{1,0:T(8,128)(2,1)S(1)} %slice_bitcast_fusion.3), channel_id=1, source_target_pairs={{0,8},{8,0},{16,24},{24,16},{1,9},{9,1},{17,25},{25,17},{2,10},{10... | collective-permute-start | bytes 2359304 | tf_op jit(solution)/shard_map/ppermute | solution.py:509
  186.2 19.7 %collective-permute-start.9 = (bf16[768,512]{1,0:T(8,128)(2,1)S(1)}, bf16[768,512]{1,0:T(8,128)(2,1)S(1)}, u32[]{:S(2)}, u32[]{:S(2)}) collective-permute-start(bf16[768,512]{1,0:T(8,128)(2,1)S(1)} %slice_bitcast_fusion.4), channel_id=1, source_target_pairs={{0,16},{8,24},{16,0},{24,8},{1,17},{9,25},{17,1},{25,9},{2,18},{10... | collective-permute-start | bytes 2359304 | tf_op jit(solution)/shard_map/ppermute | solution.py:509
  207.3 15.6 %collective-permute-start.14 = (bf16[1,2,768,512]{3,2,1,0:T(8,128)(2,1)}, bf16[1,2,768,512]{3,2,1,0:T(8,128)(2,1)}, u32[]{:S(2)}, u32[]{:S(2)}) collective-permute-start(bf16[1,2,768,512]{3,2,1,0:T(8,128)(2,1)} %maximum_bitcast_fusion.1), channel_id=1, source_target_pairs={{0,1},{1,0},{2,3},{3,2},{4,5},{5,4},{6,7},{7,6},{8,9},{9,8},{10,11... | collective-permute-start | bytes 4718600 | tf_op jit(solution)/shard_map/ppermute | solution.py:501
  207.6 35.8 %copy-start.24 = (bf16[2,768,384]{2,1,0:T(8,128)(2,1)}, bf16[2,768,384]{2,1,0:T(8,128)(2,1)S(1)}, u32[]{:S(2)}) copy-start(bf16[2,768,384]{2,1,0:T(8,128)(2,1)S(1)} %pad_maximum_fusion.8.rest_0_) | copy-start | bytes 3538948
  207.6 35.7 %collective-permute-start.13 = (bf16[2,768,384]{2,1,0:T(8,128)(2,1)S(1)}, bf16[2,768,384]{2,1,0:T(8,128)(2,1)S(1)}, u32[]{:S(2)}, u32[]{:S(2)}) collective-permute-start(bf16[2,768,384]{2,1,0:T(8,128)(2,1)S(1)} %pad_maximum_fusion.8.rest_0_), channel_id=1, source_target_pairs={{0,16},{8,24},{16,0},{24,8},{1,17},{9,25},{17,1},{25,9},{2,18},{10... | collective-permute-start | bytes 3538952 | tf_op jit(solution)/shard_map/ppermute | solution.py:509
  208.4 35.0 %collective-permute-start.12 = (bf16[2,768,384]{2,1,0:T(8,128)(2,1)S(1)}, bf16[2,768,384]{2,1,0:T(8,128)(2,1)S(1)}, u32[]{:S(2)}, u32[]{:S(2)}) collective-permute-start(bf16[2,768,384]{2,1,0:T(8,128)(2,1)S(1)} %pad_maximum_fusion.8.rest_0_), channel_id=1, source_target_pairs={{0,8},{8,0},{16,24},{24,16},{1,9},{9,1},{17,25},{25,17},{2,10},{10... | collective-permute-start | bytes 3538952 | tf_op jit(solution)/shard_map/ppermute | solution.py:509
  244.0 32.3 %collective-permute-start.17 = (bf16[3,2,768,384]{3,2,1,0:T(8,128)(2,1)S(1)}, bf16[3,2,768,384]{3,2,1,0:T(8,128)(2,1)S(1)}, u32[]{:S(2)}, u32[]{:S(2)}) collective-permute-start(bf16[3,2,768,384]{3,2,1,0:T(8,128)(2,1)S(1)} %pad_maximum_fusion.3), channel_id=1, source_target_pairs={{0,1},{1,0},{2,3},{3,2},{4,5},{5,4},{6,7},{7,6},{8,9},{9,8},{10,11... | collective-permute-start | bytes 10616840 | tf_op jit(solution)/shard_map/ppermute | solution.py:501
  248.3 27.9 %collective-permute-start.16 = (bf16[768,384]{1,0:T(8,128)(2,1)S(1)}, bf16[768,384]{1,0:T(8,128)(2,1)S(1)}, u32[]{:S(2)}, u32[]{:S(2)}) collective-permute-start(bf16[768,384]{1,0:T(8,128)(2,1)S(1)} %slice_bitcast_fusion.13), channel_id=1, source_target_pairs={{0,8},{8,0},{16,24},{24,16},{1,9},{9,1},{17,25},{25,17},{2,10},{10... | collective-permute-start | bytes 1769480 | tf_op jit(solution)/shard_map/ppermute | solution.py:509
  248.9 27.3 %collective-permute-start.15 = (bf16[768,384]{1,0:T(8,128)(2,1)S(1)}, bf16[768,384]{1,0:T(8,128)(2,1)S(1)}, u32[]{:S(2)}, u32[]{:S(2)}) collective-permute-start(bf16[768,384]{1,0:T(8,128)(2,1)S(1)} %slice_bitcast_fusion.14), channel_id=1, source_target_pairs={{0,16},{8,24},{16,0},{24,8},{1,17},{9,25},{17,1},{25,9},{2,18},{10... | collective-permute-start | bytes 1769480 | tf_op jit(solution)/shard_map/ppermute | solution.py:509
  277.7 4.6 collective-permute-start.18
  326.7 281.4 %reduce-scatter.7.cloned.1.call-start = ((), (), s32[]{:S(2)}) async-start(), calls=%async_computation.5 | async-start | bytes 9732096 | tf_op jit(solution)/shard_map/reduce_scatter | solution.py:1100
  361.9 35.3 %copy-start.14 = (bf16[512,768]{1,0:T(8,128)(2,1)S(1)}, bf16[512,768]{1,0:T(8,128)(2,1)}, u32[]{:S(2)}) copy-start(bf16[512,768]{1,0:T(8,128)(2,1)} %copy-done.13) | copy-start | bytes 2359300
  396.6 8.0 %collective-permute-start.19 = (bf16[4,1024,512]{2,1,0:T(8,128)(2,1)}, bf16[4,1024,512]{2,1,0:T(8,128)(2,1)S(1)}, u32[]{:S(2)}, u32[]{:S(2)}) collective-permute-start(bf16[4,1024,512]{2,1,0:T(8,128)(2,1)} %get-tuple-element.243), channel_id=1, source_target_pairs={{0,1},{1,0},{2,3},{3,2},{4,5},{5,4},{6,7},{7,6},{8,9},{9,8},{10,11... | collective-permute-start | bytes 12582920 | tf_op jit(solution)/shard_map/ppermute | solution.py:501
  396.7 13.8 %collective-permute-start.20 = (bf16[4,1024,512]{2,1,0:T(8,128)(2,1)}, bf16[4,1024,512]{2,1,0:T(8,128)(2,1)S(1)}, u32[]{:S(2)}, u32[]{:S(2)}) collective-permute-start(bf16[4,1024,512]{2,1,0:T(8,128)(2,1)} %get-tuple-element.244), channel_id=1, source_target_pairs={{0,1},{1,0},{2,3},{3,2},{4,5},{5,4},{6,7},{7,6},{8,9},{9,8},{10,11... | collective-permute-start | bytes 12582920 | tf_op jit(solution)/shard_map/ppermute | solution.py:501
  418.3 229.1 %reduce-scatter.9.cloned.1.call-start = ((), (), s32[]{:S(2)}) async-start(), calls=%async_computation.6 | async-start | bytes 2621440 | tf_op jit(solution)/shard_map/reduce_scatter | solution.py:1131
  424.1 48.0 %collective-permute-start.22 = (bf16[2,1024,512]{2,1,0:T(8,128)(2,1)}, bf16[2,1024,512]{2,1,0:T(8,128)(2,1)}, u32[]{:S(2)}, u32[]{:S(2)}) collective-permute-start(bf16[2,1024,512]{2,1,0:T(8,128)(2,1)} %get-tuple-element.396), channel_id=1, source_target_pairs={{0,8},{8,0},{16,24},{24,16},{1,9},{9,1},{17,25},{25,17},{2,10},{10... | collective-permute-start | bytes 6291464 | tf_op jit(solution)/shard_map/ppermute | solution.py:509
  428.7 48.0 %collective-permute-start.21 = (bf16[2,1024,512]{2,1,0:T(8,128)(2,1)}, bf16[2,1024,512]{2,1,0:T(8,128)(2,1)}, u32[]{:S(2)}, u32[]{:S(2)}) collective-permute-start(bf16[2,1024,512]{2,1,0:T(8,128)(2,1)} %get-tuple-element.398), channel_id=1, source_target_pairs={{0,16},{8,24},{16,0},{24,8},{1,17},{9,25},{17,1},{25,9},{2,18},{10... | collective-permute-start | bytes 6291464 | tf_op jit(solution)/shard_map/ppermute | solution.py:509
  476.7 32.0 %collective-permute-start.25 = (bf16[4,1024,512]{2,1,0:T(8,128)(2,1)}, bf16[4,1024,512]{2,1,0:T(8,128)(2,1)S(1)}, u32[]{:S(2)}, u32[]{:S(2)}) collective-permute-start(bf16[4,1024,512]{2,1,0:T(8,128)(2,1)} %get-tuple-element.265), channel_id=1, source_target_pairs={{0,1},{1,0},{2,3},{3,2},{4,5},{5,4},{6,7},{7,6},{8,9},{9,8},{10,11... | collective-permute-start | bytes 12582920 | tf_op jit(solution)/shard_map/ppermute | solution.py:501
  476.7 32.0 %collective-permute-start.26 = (bf16[4,1024,512]{2,1,0:T(8,128)(2,1)}, bf16[4,1024,512]{2,1,0:T(8,128)(2,1)S(1)}, u32[]{:S(2)}, u32[]{:S(2)}) collective-permute-start(bf16[4,1024,512]{2,1,0:T(8,128)(2,1)} %get-tuple-element.266), channel_id=1, source_target_pairs={{0,1},{1,0},{2,3},{3,2},{4,5},{5,4},{6,7},{7,6},{8,9},{9,8},{10,11... | collective-permute-start | bytes 12582920 | tf_op jit(solution)/shard_map/ppermute | solution.py:501
  480.2 25.1 %collective-permute-start.23 = (bf16[1,1024,512]{2,1,0:T(8,128)(2,1)S(1)}, bf16[1,1024,512]{2,1,0:T(8,128)(2,1)S(1)}, u32[]{:S(2)}, u32[]{:S(2)}) collective-permute-start(bf16[1,1024,512]{2,1,0:T(8,128)(2,1)S(1)} %get-tuple-element.406), channel_id=1, source_target_pairs={{0,8},{8,0},{16,24},{24,16},{1,9},{9,1},{17,25},{25,17},{2,10},{10... | collective-permute-start | bytes 3145736 | tf_op jit(solution)/shard_map/ppermute | solution.py:509
  483.7 25.0 %collective-permute-start.24 = (bf16[1,1024,512]{2,1,0:T(8,128)(2,1)S(1)}, bf16[1,1024,512]{2,1,0:T(8,128)(2,1)S(1)}, u32[]{:S(2)}, u32[]{:S(2)}) collective-permute-start(bf16[1,1024,512]{2,1,0:T(8,128)(2,1)S(1)} %get-tuple-element.404), channel_id=1, source_target_pairs={{0,16},{8,24},{16,0},{24,8},{1,17},{9,25},{17,1},{25,9},{2,18},{10... | collective-permute-start | bytes 3145736 | tf_op jit(solution)/shard_map/ppermute | solution.py:509
  511.5 60.4 %collective-permute-start.28 = (bf16[2,1024,512]{2,1,0:T(8,128)(2,1)}, bf16[2,1024,512]{2,1,0:T(8,128)(2,1)}, u32[]{:S(2)}, u32[]{:S(2)}) collective-permute-start(bf16[2,1024,512]{2,1,0:T(8,128)(2,1)} %get-tuple-element.392), channel_id=1, source_target_pairs={{0,8},{8,0},{16,24},{24,16},{1,9},{9,1},{17,25},{25,17},{2,10},{10... | collective-permute-start | bytes 6291464 | tf_op jit(solution)/shard_map/ppermute | solution.py:509
  515.2 56.6 %collective-permute-start.27 = (bf16[2,1024,512]{2,1,0:T(8,128)(2,1)}, bf16[2,1024,512]{2,1,0:T(8,128)(2,1)}, u32[]{:S(2)}, u32[]{:S(2)}) collective-permute-start(bf16[2,1024,512]{2,1,0:T(8,128)(2,1)} %get-tuple-element.394), channel_id=1, source_target_pairs={{0,16},{8,24},{16,0},{24,8},{1,17},{9,25},{17,1},{25,9},{2,18},{10... | collective-permute-start | bytes 6291464 | tf_op jit(solution)/shard_map/ppermute | solution.py:509
  518.5 168.5 %reduce-scatter.11.cloned.1.call-start = ((), (), s32[]{:S(2)}) async-start(), calls=%async_computation.7 | async-start | bytes 2621440 | tf_op jit(solution)/shard_map/reduce_scatter | solution.py:1131
  575.7 32.3 %collective-permute-start.29 = (bf16[1,1024,512]{2,1,0:T(8,128)(2,1)}, bf16[1,1024,512]{2,1,0:T(8,128)(2,1)}, u32[]{:S(2)}, u32[]{:S(2)}) collective-permute-start(bf16[1,1024,512]{2,1,0:T(8,128)(2,1)} %get-tuple-element.402), channel_id=1, source_target_pairs={{0,8},{8,0},{16,24},{24,16},{1,9},{9,1},{17,25},{25,17},{2,10},{10... | collective-permute-start | bytes 3145736 | tf_op jit(solution)/shard_map/ppermute | solution.py:509
  580.0 28.1 %collective-permute-start.30 = (bf16[1,1024,512]{2,1,0:T(8,128)(2,1)}, bf16[1,1024,512]{2,1,0:T(8,128)(2,1)}, u32[]{:S(2)}, u32[]{:S(2)}) collective-permute-start(bf16[1,1024,512]{2,1,0:T(8,128)(2,1)} %get-tuple-element.400), channel_id=1, source_target_pairs={{0,16},{8,24},{16,0},{24,8},{1,17},{9,25},{17,1},{25,9},{2,18},{10... | collective-permute-start | bytes 3145736 | tf_op jit(solution)/shard_map/ppermute | solution.py:509
  615.2 32.2 %collective-permute-start.34 = (bf16[384,768]{1,0:T(8,128)(2,1)}, bf16[384,768]{1,0:T(8,128)(2,1)}, u32[]{:S(2)}, u32[]{:S(2)}) collective-permute-start(bf16[384,768]{1,0:T(8,128)(2,1)} %get-tuple-element.425), channel_id=1, source_target_pairs={{0,8},{8,0},{16,24},{24,16},{1,9},{9,1},{17,25},{25,17},{2,10},{10... | collective-permute-start | bytes 1769480 | tf_op jit(solution)/shard_map/ppermute | solution.py:509
  616.3 31.2 %collective-permute-start.33 = (bf16[384,768]{1,0:T(8,128)(2,1)}, bf16[384,768]{1,0:T(8,128)(2,1)}, u32[]{:S(2)}, u32[]{:S(2)}) collective-permute-start(bf16[384,768]{1,0:T(8,128)(2,1)} %get-tuple-element.426), channel_id=1, source_target_pairs={{0,16},{8,24},{16,0},{24,8},{1,17},{9,25},{17,1},{25,9},{2,18},{10... | collective-permute-start | bytes 1769480 | tf_op jit(solution)/shard_map/ppermute | solution.py:509
  618.3 29.1 %collective-permute-start.32 = (bf16[352,768]{1,0:T(8,128)(2,1)}, bf16[352,768]{1,0:T(8,128)(2,1)}, u32[]{:S(2)}, u32[]{:S(2)}) collective-permute-start(bf16[352,768]{1,0:T(8,128)(2,1)} %get-tuple-element.439), channel_id=1, source_target_pairs={{0,8},{8,0},{16,24},{24,16},{1,9},{9,1},{17,25},{25,17},{2,10},{10... | collective-permute-start | bytes 1622024 | tf_op jit(solution)/shard_map/ppermute | solution.py:509
  619.1 28.3 %collective-permute-start.31 = (bf16[352,768]{1,0:T(8,128)(2,1)}, bf16[352,768]{1,0:T(8,128)(2,1)}, u32[]{:S(2)}, u32[]{:S(2)}) collective-permute-start(bf16[352,768]{1,0:T(8,128)(2,1)} %get-tuple-element.440), channel_id=1, source_target_pairs={{0,16},{8,24},{16,0},{24,8},{1,17},{9,25},{17,1},{25,9},{2,18},{10... | collective-permute-start | bytes 1622024 | tf_op jit(solution)/shard_map/ppermute | solution.py:509
  650.2 23.4 %collective-permute-start.40 = (bf16[352,768]{1,0:T(8,128)(2,1)}, bf16[352,768]{1,0:T(8,128)(2,1)}, u32[]{:S(2)}, u32[]{:S(2)}) collective-permute-start(bf16[352,768]{1,0:T(8,128)(2,1)} %get-tuple-element.437), channel_id=1, source_target_pairs={{0,8},{8,0},{16,24},{24,16},{1,9},{9,1},{17,25},{25,17},{2,10},{10... | collective-permute-start | bytes 1622024 | tf_op jit(solution)/shard_map/ppermute | solution.py:509
  651.3 23.6 %collective-permute-start.41 = (bf16[352,768]{1,0:T(8,128)(2,1)}, bf16[352,768]{1,0:T(8,128)(2,1)}, u32[]{:S(2)}, u32[]{:S(2)}) collective-permute-start(bf16[352,768]{1,0:T(8,128)(2,1)} %get-tuple-element.438), channel_id=1, source_target_pairs={{0,16},{8,24},{16,0},{24,8},{1,17},{9,25},{17,1},{25,9},{2,18},{10... | collective-permute-start | bytes 1622024 | tf_op jit(solution)/shard_map/ppermute | solution.py:509
  655.0 21.9 %collective-permute-start.38 = (bf16[384,768]{1,0:T(8,128)(2,1)}, bf16[384,768]{1,0:T(8,128)(2,1)}, u32[]{:S(2)}, u32[]{:S(2)}) collective-permute-start(bf16[384,768]{1,0:T(8,128)(2,1)} %get-tuple-element.423), channel_id=1, source_target_pairs={{0,8},{8,0},{16,24},{24,16},{1,9},{9,1},{17,25},{25,17},{2,10},{10... | collective-permute-start | bytes 1769480 | tf_op jit(solution)/shard_map/ppermute | solution.py:509
  655.8 23.7 %collective-permute-start.39 = (bf16[384,768]{1,0:T(8,128)(2,1)}, bf16[384,768]{1,0:T(8,128)(2,1)}, u32[]{:S(2)}, u32[]{:S(2)}) collective-permute-start(bf16[384,768]{1,0:T(8,128)(2,1)} %get-tuple-element.424), channel_id=1, source_target_pairs={{0,16},{8,24},{16,0},{24,8},{1,17},{9,25},{17,1},{25,9},{2,18},{10... | collective-permute-start | bytes 1769480 | tf_op jit(solution)/shard_map/ppermute | solution.py:509
  669.1 17.8 %collective-permute-start.37 = (bf16[2,256,512]{2,1,0:T(8,128)(2,1)}, bf16[2,256,512]{2,1,0:T(8,128)(2,1)}, u32[]{:S(2)}, u32[]{:S(2)}) collective-permute-start(bf16[2,256,512]{2,1,0:T(8,128)(2,1)} %bitcast.97), channel_id=1, source_target_pairs={{0,16},{8,24},{16,0},{24,8},{1,17},{9,25},{17,1},{25,9},{2,18},{10... | collective-permute-start | bytes 1572872 | tf_op jit(solution)/shard_map/ppermute | solution.py:509
  673.6 13.4 %collective-permute-start.36 = (bf16[2,256,512]{2,1,0:T(8,128)(2,1)}, bf16[2,256,512]{2,1,0:T(8,128)(2,1)}, u32[]{:S(2)}, u32[]{:S(2)}) collective-permute-start(bf16[2,256,512]{2,1,0:T(8,128)(2,1)} %bitcast.97), channel_id=1, source_target_pairs={{0,8},{8,0},{16,24},{24,16},{1,9},{9,1},{17,25},{25,17},{2,10},{10... | collective-permute-start | bytes 1572872 | tf_op jit(solution)/shard_map/ppermute | solution.py:509
  674.9 6.1 collective-permute-start.35
  687.0 22.1 %collective-permute-start.43 = (bf16[2,256,512]{2,1,0:T(8,128)(2,1)}, bf16[2,256,512]{2,1,0:T(8,128)(2,1)S(1)}, u32[]{:S(2)}, u32[]{:S(2)}) collective-permute-start(bf16[2,256,512]{2,1,0:T(8,128)(2,1)} %bitcast.323), channel_id=1, source_target_pairs={{0,16},{8,24},{16,0},{24,8},{1,17},{9,25},{17,1},{25,9},{2,18},{10... | collective-permute-start | bytes 1572872 | tf_op jit(solution)/shard_map/ppermute | solution.py:509
  688.1 20.9 %collective-permute-start.42 = (bf16[2,256,512]{2,1,0:T(8,128)(2,1)}, bf16[2,256,512]{2,1,0:T(8,128)(2,1)S(1)}, u32[]{:S(2)}, u32[]{:S(2)}) collective-permute-start(bf16[2,256,512]{2,1,0:T(8,128)(2,1)} %bitcast.324), channel_id=1, source_target_pairs={{0,8},{8,0},{16,24},{24,16},{1,9},{9,1},{17,25},{25,17},{2,10},{10... | collective-permute-start | bytes 1572872 | tf_op jit(solution)/shard_map/ppermute | solution.py:509
  693.3 7.0 collective-permute-start.44
  696.5 8.3 %collective-permute-start.50 = (bf16[256,512]{1,0:T(8,128)(2,1)S(1)}, bf16[256,512]{1,0:T(8,128)(2,1)S(1)}, u32[]{:S(2)}, u32[]{:S(2)}) collective-permute-start(bf16[256,512]{1,0:T(8,128)(2,1)S(1)} %get-tuple-element.452), channel_id=1, source_target_pairs={{0,16},{8,24},{16,0},{24,8},{1,17},{9,25},{17,1},{25,9},{2,18},{10... | collective-permute-start | bytes 786440 | tf_op jit(solution)/shard_map/ppermute | solution.py:509
  700.4 4.4 collective-permute-start.45
  702.3 6.4 collective-permute-start.51
  710.5 4.4 collective-permute-start.46
  712.3 12.6 %collective-permute-start.48 = (bf16[256,512]{1,0:T(8,128)(2,1)}, bf16[256,512]{1,0:T(8,128)(2,1)}, u32[]{:S(2)}, u32[]{:S(2)}) collective-permute-start(bf16[256,512]{1,0:T(8,128)(2,1)} %get-tuple-element.444), channel_id=1, source_target_pairs={{0,16},{8,24},{16,0},{24,8},{1,17},{9,25},{17,1},{25,9},{2,18},{10... | collective-permute-start | bytes 786440 | tf_op jit(solution)/shard_map/ppermute | solution.py:509
  715.5 4.4 collective-permute-start.47
  717.0 9.2 %collective-permute-start.49 = (bf16[256,512]{1,0:T(8,128)(2,1)}, bf16[256,512]{1,0:T(8,128)(2,1)}, u32[]{:S(2)}, u32[]{:S(2)}) collective-permute-start(bf16[256,512]{1,0:T(8,128)(2,1)} %get-tuple-element.447), channel_id=1, source_target_pairs={{0,8},{8,0},{16,24},{24,16},{1,9},{9,1},{17,25},{25,17},{2,10},{10... | collective-permute-start | bytes 786440 | tf_op jit(solution)/shard_map/ppermute | solution.py:509
  (99 other events, 635.4 us)
Sparse Core Ops, SparseCore 0:
  16.7 50.0 all-gather.9
  69.0 44.7 all-gather.11
  115.9 29.1 all-gather.15
  146.6 83.3 all-gather.13
  326.9 97.1 reduce-scatter.4
  426.3 90.4 reduce-scatter.6
  519.0 42.2 reduce-scatter.8
  613.0 41.6 reduce-scatter.10

commit v3 on v2

--- a/solution.py
+++ b/solution.py
@@ -43,6 +43,17 @@
     centred = value - average
     spread = jnp.mean(centred * centred, axis=-1, keepdims=True)
     return centred * lax.rsqrt(spread + EPSILON) * gain + shift
+
+
+def normalize_back(value, gain, pull):
+    centred = value - jnp.mean(value, axis=-1, keepdims=True)
+    scale = lax.rsqrt(jnp.mean(centred * centred, axis=-1, keepdims=True) + EPSILON)
+    unit = centred * scale
+    inner = pull * gain
+    grad = scale * (
+        inner - jnp.mean(inner, axis=-1, keepdims=True) - unit * jnp.mean(inner * unit, axis=-1, keepdims=True)
+    )
+    return grad, jnp.sum(pull * unit, axis=0, keepdims=True), jnp.sum(pull, axis=0, keepdims=True)
 
 
 def matmul(left, right, dims=INNER_FIRST):
@@ -135,7 +146,7 @@
             pltpu.VMEM((block, FLAT + 128), jnp.float32),
             pltpu.VMEM((FLAT // 128 * block, VPAD), jnp.bfloat16),
         ],
-        compiler_params=pltpu.CompilerParams(vmem_limit_bytes=40 << 20),
+        compiler_params=pltpu.CompilerParams(vmem_limit_bytes=60 << 20),
         cost_estimate=pl.CostEstimate(
             flops=count * block * WCH * 32 * filters,
             bytes_accessed=count * block * filters,
@@ -549,13 +560,19 @@
     return slice(count // 2, count), slice(0, count // 2)
 
 
-def collect_round(terms, narrow, turn):
-    following = []
+def round_sums(terms):
+    sums = []
     for half, (parts, arrived) in enumerate(terms):
         leaving, staying = sides(half, parts.shape[0])
-        sent = hop(add_low(parts[leaving], arrived[leaving]), narrow, bits_of(narrow, half)[turn])
-        following.append((add_low(parts[staying], arrived[staying]), sent))
-    return following
+        sums.append((add_low(parts[leaving], arrived[leaving]), add_low(parts[staying], arrived[staying])))
+    return sums
+
+
+def collect_round(terms, narrow, turn):
+    return [
+        (staying, hop(leaving, narrow, bits_of(narrow, half)[turn]))
+        for half, (leaving, staying) in enumerate(round_sums(terms))
+    ]
 
 
 def tie(*groups):
@@ -762,9 +779,8 @@
     )(where, low, carry, shift, shift, shard, twin, *flat)
 
 
-def mix_backward_body(narrow, layer, where_ref, low_ref, carry_ref, a_ref, cdf_ref, gate_ref, pull_ref, shard_ref, twin_ref, *rest):
-    mine, other, (own_a, own_g, oth_a, oth_g, shift_ref, back_ref, slots, low_t_ref, sems) = weight_refs(rest, narrow)
-    slot = weights_of_step(narrow, layer, where_ref, shard_ref, twin_ref, mine, other, slots, sems)
+def mix_grad_body(rows, where_ref, low_ref, carry_ref, a_ref, cdf_ref, gate_ref, pull_ref, *rest):
+    own_a, own_g, oth_a, oth_g, shift_ref, grads_ref, low_t_ref = rest
 
     @pl.when(pl.program_id(0) == 0)
     def _():
@@ -774,13 +790,12 @@
     a = a_ref[...]
     cdf = cdf_ref[...]
     gate = gate_ref[...]
-    pull = pull_ref[...]
-    rest_pull = (1.0 - gate) * pull
+    rest_pull = (1.0 - gate) * pull_ref[...]
     pull_a = (rest_pull * (cdf + a * NORMAL_PEAK * jnp.exp(-0.5 * a * a))).astype(jnp.bfloat16)
     pull_g = (rest_pull * gate * (carry_ref[...] - a * cdf)).astype(jnp.bfloat16)
     half_rows = own_a.shape[1]
-    rows = shard_ref.shape[1]
     for half, grad in enumerate((pull_a, pull_g)):
+        grads_ref[half] = grad
         shift_ref[half, :, :] = jnp.sum(grad.astype(jnp.float32), axis=0, keepdims=True)
         for side, out_ref in enumerate(((own_a, own_g)[half], (oth_a, oth_g)[half])):
             for chip in range(half_rows // rows):
@@ -788,7 +803,41 @@
                 out_ref[0, chip * rows : (chip + 1) * rows, :] = matmul(
                     low_t_ref[pl.ds(start, rows), :], grad
                 ).astype(jnp.bfloat16)
-    back = matmul(pull_a, slot[0], CONTRACT_COLS) + matmul(pull_g, slot[1], CONTRACT_COLS)
+
+
+def mix_grad(where, narrow, rows, low, carry, a, cdf, gate, pull):
+    words, filters = carry.shape
+    part = filters // narrow
+    block = pl.BlockSpec((words, part), lambda i, where: (0, where[0] ^ i))
+    grad_block = pl.BlockSpec((1, filters // 2, part), lambda i, where: (i, 0, 0))
+    return pl.pallas_call(
+        functools.partial(mix_grad_body, rows),
+        grid_spec=pltpu.PrefetchScalarGridSpec(
+            num_scalar_prefetch=1,
+            grid=(narrow,),
+            in_specs=[pl.BlockSpec((words, filters), lambda i, where: (0, 0))] + [block] * 5,
+            out_specs=[
+                *[grad_block] * 4,
+                pl.BlockSpec((2, 1, part), lambda i, where: (0, 0, where[0] ^ i)),
+                pl.BlockSpec((2, words, part), lambda i, where: (0, 0, where[0] ^ i)),
+            ],
+            scratch_shapes=[pltpu.VMEM((filters, words), jnp.bfloat16)],
+        ),
+        out_shape=[
+            *[jax.ShapeDtypeStruct((narrow, filters // 2, part), jnp.bfloat16)] * 4,
+            jax.ShapeDtypeStruct((2, 1, filters), jnp.float32),
+            jax.ShapeDtypeStruct((2, words, filters), jnp.bfloat16),
+        ],
+        compiler_params=pltpu.CompilerParams(vmem_limit_bytes=60 << 20),
+        cost_estimate=pl.CostEstimate(flops=words * filters * part, bytes_accessed=words * filters, transcendentals=0),
+        name="mix_grad",
+    )(where, low, carry, a, cdf, gate, pull)
+
+
+def mix_pull_body(narrow, layer, where_ref, grads_ref, gate_ref, pull_ref, shard_ref, twin_ref, *rest):
+    mine, other, (back_ref, slots, sems) = weight_refs(rest, narrow)
+    slot = weights_of_step(narrow, layer, where_ref, shard_ref, twin_ref, mine, other, slots, sems)
+    back = matmul(grads_ref[0], slot[0], CONTRACT_COLS) + matmul(grads_ref[1], slot[1], CONTRACT_COLS)
 
     @pl.when(pl.program_id(0) == 0)
     def _():
@@ -798,50 +847,82 @@
     def _():
         back_ref[...] += back
 
-    part = gate.shape[1]
+    part = gate_ref.shape[1]
     column = pl.multiple_of((where_ref[0] ^ pl.program_id(0)) * part, part)
-    back_ref[:, pl.ds(column, part)] += gate * pull
-
-
-def mix_backward(layer, where, low, carry, a, cdf, gate, pull, shard, twin, mine, other):
+    back_ref[:, pl.ds(column, part)] += gate_ref[...] * pull_ref[...]
+
+
+def mix_pull(layer, where, grads, gate, pull, shard, twin, mine, other):
     narrow = len(mine)
-    words, filters = carry.shape
+    words, filters = gate.shape
     part = filters // narrow
     flat = jax.tree.leaves((mine, other))
     block = pl.BlockSpec((words, part), lambda i, where: (0, where[0] ^ i))
-    grad_block = pl.BlockSpec((1, filters // 2, part), lambda i, where: (i, 0, 0))
-    grad_shape = jax.ShapeDtypeStruct((narrow, filters // 2, part), jnp.bfloat16)
     return pl.pallas_call(
-        functools.partial(mix_backward_body, narrow, layer),
+        functools.partial(mix_pull_body, narrow, layer),
         grid_spec=pltpu.PrefetchScalarGridSpec(
             num_scalar_prefetch=1,
             grid=(narrow,),
-            in_specs=[pl.BlockSpec((words, filters), lambda i, where: (0, 0))]
-            + [block] * 5
+            in_specs=[pl.BlockSpec((2, words, part), lambda i, where: (0, 0, where[0] ^ i))]
+            + [block] * 2
             + [pl.BlockSpec(memory_space=pl.ANY)] * (2 + len(flat)),
-            out_specs=[
-                *[grad_block] * 4,
-                pl.BlockSpec((2, 1, part), lambda i, where: (0, 0, where[0] ^ i)),
-                pl.BlockSpec((words, filters), lambda i, where: (0, 0)),
-            ],
+            out_specs=pl.BlockSpec((words, filters), lambda i, where: (0, 0)),
             scratch_shapes=[
                 pltpu.VMEM((2, 2, filters, part), jnp.bfloat16),
-                pltpu.VMEM((filters, words), jnp.bfloat16),
                 pltpu.SemaphoreType.DMA((2, 4 * (filters // shard.shape[1] // 2))),
             ],
         ),
-        out_shape=[
-            *[grad_shape] * 4,
-            jax.ShapeDtypeStruct((2, 1, filters), jnp.float32),
-            jax.ShapeDtypeStruct((words, filters), jnp.float32),
-        ],
+        out_shape=jax.ShapeDtypeStruct((words, filters), jnp.float32),
         compiler_params=pltpu.CompilerParams(vmem_limit_bytes=60 << 20),
-        cost_estimate=pl.CostEstimate(
-            flops=words * filters * filters, bytes_accessed=filters * filters,
-            transcendentals=0,
-        ),
-        name="mix_backward",
-    )(where, low, carry, a, cdf, gate, pull, shard, twin, *flat)
+        cost_estimate=pl.CostEstimate(flops=words * filters * part, bytes_accessed=words * filters, transcendentals=0),
+        name="mix_pull",
+    )(where, grads, gate, pull, shard, twin, *flat)
+
+
+def spread_rows(out_ref, value, row):
+    wide = out_ref.shape[0]
+    rows = value.shape[0] // wide
+    for device in range(wide):
+        out_ref[device, row : row + rows, :] = value[device * rows : (device + 1) * rows].astype(jnp.bfloat16)
+    return row + rows
+
+
+def first_body(inner_ref, ffn_ref, first_ref, grad_ref, out_ref):
+    columns = out_ref.shape[2]
+    row = spread_rows(out_ref, matmul(inner_ref[...], ffn_ref[...], CONTRACT_ROWS), 0)
+    for start in range(0, grad_ref.shape[1], columns):
+        row = spread_rows(out_ref, matmul(first_ref[...], grad_ref[:, start : start + columns], CONTRACT_ROWS), row)
+
+
+def first_parts(wide, activated, grad_ffn, low_first, grad_inner):
+    words, columns = grad_ffn.shape
+    return pl.pallas_call(
+        first_body,
+        out_shape=jax.ShapeDtypeStruct((wide, 2 * activated.shape[1] // wide, columns), jnp.bfloat16),
+        compiler_params=pltpu.CompilerParams(vmem_limit_bytes=60 << 20),
+        cost_estimate=pl.CostEstimate(flops=words * columns * columns, bytes_accessed=words * columns, transcendentals=0),
+        name="first_parts",
+    )(activated, grad_ffn, low_first, grad_inner)
+
+
+def second_body(context_ref, attn_ref, in_ref, proj_ref, top_ref, embed_ref, position_ref, out_ref):
+    row = spread_rows(out_ref, matmul(context_ref[...], attn_ref[...], CONTRACT_ROWS), 0)
+    for part in range(3):
+        row = spread_rows(out_ref, matmul(in_ref[...], proj_ref[part], CONTRACT_ROWS), row)
+    row = spread_rows(out_ref, matmul(top_ref[...], embed_ref[...], CONTRACT_ROWS), row)
+    spread_rows(out_ref, position_ref[...], row)
+
+
+def second_parts(wide, context, grad_attn, low_in, grad_proj, low_top, grad_embed, grad_position):
+    words, columns = context.shape
+    rows = (4 * columns + low_top.shape[1] + grad_position.shape[0]) // wide
+    return pl.pallas_call(
+        second_body,
+        out_shape=jax.ShapeDtypeStruct((wide, rows, columns), jnp.bfloat16),
+        compiler_params=pltpu.CompilerParams(vmem_limit_bytes=60 << 20),
+        cost_estimate=pl.CostEstimate(flops=words * columns * columns, bytes_accessed=words * columns, transcendentals=0),
+        name="second_parts",
+    )(context, grad_attn, low_in, grad_proj, low_top, grad_embed, grad_position)
 
 
 def from_rows(rows, count, size):
@@ -926,11 +1007,9 @@
     model_size = embed_gain.shape[0]
     highway_shift = whole(1, 2, highway_bias.shape[1]).astype(jnp.float32)
     vectors = whole(2, 13, model_size).astype(jnp.float32)
-    inner_shift = whole(7, 1, ff_in_bias.shape[0]).astype(jnp.float32)
+    vectors = [vectors[i] for i in range(13)]
+    inner_shift = whole(7, 1, ff_in_bias.shape[0])[0].astype(jnp.float32)
     table = whole(8, 1, char_table.shape[0]).reshape(vocab, CDIM)
-    type_vectors, embed_gain_full, embed_shift = vectors[0:2], vectors[2:3], (vectors[3:4], vectors[4:5])
-    gain_rows = (vectors[5:6], vectors[6:7])
-    shift_rows = [vectors[7 + i : 8 + i] for i in range(6)]
 
     seq_count, seq_len, char_slots = char_ids.shape
     word_count = seq_count * seq_len
@@ -995,7 +1074,9 @@
         return carried, low_state
 
     carried, low_state = mix(0, carried, low_state, other)
-    known[1], carried, low_state = tie(known[1], carried, low_state)
+    known[1], carried, low_state, vectors, inner_shift = tie(known[1], carried, low_state, vectors, inner_shift)
+    type_zero, type_other, embed_gain_full, *embed_shift = vectors[:5]
+    gain_rows, shift_rows = vectors[5:7], vectors[7:13]
     for level in levels[1:]:
         spread_level(known[1], narrow, level)
     other = [swap_early(known[1], narrow, wide)]
@@ -1024,8 +1105,8 @@
         matmul(low_top, projection_full)
         + embed_shift[0]
         + position_rows
-        + type_vectors[0:1] * (1.0 - type_one)
-        + type_vectors[1:2] * type_one
+        + type_zero * (1.0 - type_one)
+        + type_other * type_one
     )
     embedded = normalize(embed_sum, embed_gain_full, embed_shift[1])
     low_in = embedded.astype(jnp.bfloat16)
@@ -1050,22 +1131,24 @@
     final_out = normalize(second_in, gain_rows[1], shift_rows[5])
     hidden_out = (final_out * row_keep).reshape(seq_count, seq_len, -1)
 
+    def reduce_wide(value):
+        return lax.psum_scatter(value, "wide", scatter_dimension=0)
+
     grad_top = out_grad.reshape(word_count, -1).astype(jnp.float32) * row_keep
-    norm_pull = jax.vjp(normalize, second_in, gain_rows[1], shift_rows[5])[1]
-    grad_second, grad_gain_two, grad_shift_five = norm_pull(grad_top)
+    grad_second, grad_gain_two, grad_shift_five = normalize_back(second_in, gain_rows[1], grad_top)
     grad_ffn = grad_second.astype(jnp.bfloat16)
     grad_shift_four = jnp.sum(grad_ffn, axis=0, keepdims=True, dtype=jnp.float32)
-    weight_ff_out = matmul(activated, grad_ffn, CONTRACT_ROWS)
     grad_inner = (matmul(grad_ffn, ff_out_full, CONTRACT_COLS) * gelu_slope(inner_pre)).astype(jnp.bfloat16)
     grad_ff_bias = jnp.sum(grad_inner, axis=0, keepdims=True, dtype=jnp.float32)
-    weight_ff_in = matmul(low_first, grad_inner, CONTRACT_ROWS)
     grad_first = grad_second + matmul(grad_inner, ff_in_full, CONTRACT_COLS)
-    norm_pull = jax.vjp(normalize, first_in, gain_rows[0], shift_rows[3])[1]
-    grad_res, grad_gain_one, grad_shift_three = norm_pull(grad_first)
+    grad_res, grad_gain_one, grad_shift_three = normalize_back(first_in, gain_rows[0], grad_first)
     grad_attn = grad_res.astype(jnp.bfloat16)
     grad_shift_two = jnp.sum(grad_attn, axis=0, keepdims=True, dtype=jnp.float32)
-    weight_out = matmul(context, grad_attn, CONTRACT_ROWS)
     grad_context = matmul(grad_attn, out_full, CONTRACT_COLS).astype(jnp.bfloat16)
+    first_packed = first_parts(wide, activated, grad_ffn, low_first, grad_inner)
+    first_sizes = [[ff_out.shape[0]], [ff_in.shape[0]] * (ff_in.shape[1] // model_width)]
+    first_packed, grad_context = tie(first_packed, grad_context)
+    first_sum = reduce_wide(first_packed)
     grad_proj = jnp.concatenate(
         [
             attend_back(lengths[i : i + 1], queries[rows], keys[rows], values[rows], grad_context[rows], attended[i][1])
@@ -1075,30 +1158,17 @@
     )
     grad_shift_zero = jnp.sum(grad_proj[0], axis=0, keepdims=True, dtype=jnp.float32)
     grad_shift_one = jnp.sum(grad_proj[2], axis=0, keepdims=True, dtype=jnp.float32)
-    weight_qkv = [matmul(low_in, grad_proj[i], CONTRACT_ROWS) for i in range(3)]
     grad_embedded = grad_res
     for i in range(3):
         grad_embedded = grad_embedded + matmul(grad_proj[i], qkv_parts[i], CONTRACT_COLS)
-    norm_pull = jax.vjp(normalize, embed_sum, embed_gain_full, embed_shift[1])[1]
-    grad_sum, grad_embed_gain, grad_embed_shift = norm_pull(grad_embedded)
+    grad_sum, grad_embed_gain, grad_embed_shift = normalize_back(embed_sum, embed_gain_full, grad_embedded)
     grad_embed = grad_sum.astype(jnp.bfloat16)
     grad_embed_zero = jnp.sum(grad_embed, axis=0, keepdims=True, dtype=jnp.float32)
     grad_position = jnp.sum(grad_embed.reshape(seq_count, seq_len, -1), axis=0, dtype=jnp.float32)
     type_mask = type_one.astype(jnp.bfloat16)
     grad_type_one = jnp.sum(grad_embed * type_mask, axis=0, keepdims=True, dtype=jnp.float32)
     grad_type_zero = jnp.sum(grad_embed * (1 - type_mask), axis=0, keepdims=True, dtype=jnp.float32)
-    weight_proj = matmul(low_top, grad_embed, CONTRACT_ROWS)
     grad_carry = matmul(grad_embed, projection_full, CONTRACT_COLS)
-
-    def deep(value):
-        rows = value.shape[0] // wide
-        value = value.astype(jnp.bfloat16).reshape(wide, rows, value.shape[1])
-        return [value[:, :, i : i + model_width] for i in range(0, value.shape[2], model_width)]
-
-    def reduce_wide(values):
-        parts = [deep(value) for value in values]
-        total = lax.psum_scatter(jnp.concatenate([p for part in parts for p in part], axis=1), "wide", scatter_dimension=0)
-        return total, [[p.shape[1] for p in part] for part in parts]
 
     def split_deep(total, sizes):
         values, start = [], 0
@@ -1110,27 +1180,28 @@
             values.append(jnp.concatenate(pieces, axis=1).astype(jnp.float32))
         return values
 
-    first_sum, first_sizes = reduce_wide([weight_ff_out, weight_ff_in])
-
     shift_high = [None, None]
     mix_starts = [starts[1], starts[1] + (starts[2] - starts[1]) // 2]
 
     def unmix(number, pull):
-        *parts, shift_grad, back = mix_backward(
-            number, where, low_states[number], states[number], *mixes[number], pull, highway_weight, twin, *mixers[number]
+        *parts, shift_grad, grads = mix_grad(
+            where, narrow, highway_weight.shape[1], low_states[number], states[number], *mixes[number], pull
         )
         shift_high[number] = shift_grad.reshape(1, 2 * filters)
-        return parts[:2], parts[2:], back
-
+        return parts[:2], parts[2:], grads
+
+    def pull_back(number, grads, pull):
+        return mix_pull(number, where, grads, mixes[number][2], pull, highway_weight, twin, *mixers[number])
 
     def begun(own_part, got):
         return list(zip(own_part, got))
 
-    def send_home(terms):
+    def home_blocks(terms):
         blocks = [add_low(parts[0], arrived[0]).reshape(chips, -1, parts.shape[-1]) for parts, arrived in terms]
-        return lax.psum_scatter(
-            jnp.stack(blocks, axis=1), "wide", scatter_dimension=0, axis_index_groups=chip_groups(wide)
-        )
+        return jnp.stack(blocks, axis=1)
+
+    def send_home(blocks):
+        return lax.psum_scatter(blocks, "wide", scatter_dimension=0, axis_index_groups=chip_groups(wide))
 
     def laid_out(totals):
         pieces = []
@@ -1140,10 +1211,28 @@
                 pieces.append(lax.dynamic_index_in_dim(table, place ^ block, 0, keepdims=False))
         return jnp.concatenate(pieces, axis=1).astype(jnp.float32)
 
-    def convolve_back(first, last, state):
-        return conv_backward(first, last - first, ids.T, windows, scaled, kern, state)
-
-    rounds = range(narrow.bit_length() - 1)
+    def convolve_back(first, count, state):
+        return conv_backward(first, count, ids.T, windows, scaled, kern, state)
+
+    def model_rows():
+        return jnp.concatenate(
+            [
+                grad_type_zero,
+                grad_type_one,
+                grad_embed_gain,
+                grad_embed_zero,
+                grad_embed_shift,
+                grad_gain_one,
+                grad_gain_two,
+                grad_shift_zero,
+                grad_shift_one,
+                grad_shift_two,
+                grad_shift_three,
+                grad_shift_four,
+                grad_shift_five,
+            ]
+        )
+
     rounds = range(narrow.bit_length() - 1)
 
     def swap_axis(value, turn):
@@ -1153,65 +1242,53 @@
     def add_swapped(value, arrived):
         return add_low(value, jnp.concatenate(arrived, axis=0))
 
-    own_one, other_one, pull = unmix(1, grad_carry)
+    own_one, other_one, grads = unmix(1, grad_carry)
     got_one = [core_swap(value, wide) for value in other_one]
-    second_parts = [value.astype(jnp.bfloat16) for value in (weight_out, *weight_qkv, weight_proj)]
-    got_one, second_parts, pull = tie(got_one, second_parts, pull)
-    second_sum, second_sizes = reduce_wide(second_parts + [grad_position])
+    pull = pull_back(1, grads, grad_carry)
+    got_one, pull = tie(got_one, pull)
     terms_one = collect_round(begun(own_one, got_one), narrow, 0)
     staying = [parts for parts, _ in terms_one]
-    staying, pull = tie(staying, pull)
-    own_zero, other_zero, pull = unmix(0, pull)
-    terms_one, own_zero, other_zero, pull = tie(
-        [(parts, sent) for parts, (_, sent) in zip(staying, terms_one)], own_zero, other_zero, pull
+    staying, pull, context = tie(staying, pull, context)
+    second_packed = second_parts(wide, context, grad_attn, low_in, grad_proj, low_top, grad_embed, grad_position)
+    second_sizes = [[value.shape[0] // wide] for value in (out_full, *qkv_parts, projection_full, position_full)]
+    own_zero, other_zero, grads = unmix(0, pull)
+    terms_one, own_zero, other_zero, grads, second_packed = tie(
+        [(parts, sent) for parts, (_, sent) in zip(staying, terms_one)], own_zero, other_zero, grads, second_packed
     )
+    second_sum = reduce_wide(second_packed)
     got_zero = [core_swap(value, wide) for value in other_zero]
-    for turn in rounds[1:]:
+    for turn in rounds[1:-1]:
         terms_one = collect_round(terms_one, narrow, turn)
-    scaled = pull * gelu_slope(pooled) / totals
-    terms_one, got_zero, scaled = tie(terms_one, got_zero, scaled)
-    home_one = send_home(terms_one)
+    sums, grads = tie(round_sums(terms_one), grads)
+    sent = [hop(leaving, narrow, bits_of(narrow, half)[rounds[-1]]) for half, (leaving, _) in enumerate(sums)]
+    scaled = pull_back(0, grads, pull) * gelu_slope(pooled) / totals
+    model_grads = model_rows()
+    terms_one = [(staying, arrived) for (_, staying), arrived in zip(sums, sent)]
+    terms_one, got_zero, scaled, model_grads = tie(terms_one, got_zero, scaled, model_grads)
+    blocks_one = home_blocks(terms_one)
     terms_zero = collect_round(begun(own_zero, got_zero), narrow, 0)
     state = [jnp.zeros(kern.shape, jnp.float32), jnp.zeros((VROWS, 128), jnp.float32)]
     state = convolve_back(0, blocks // 2, state)
-    state, terms_zero = tie(state, terms_zero)
+    state, terms_zero, blocks_one, first_sum, second_sum = tie(state, terms_zero, blocks_one, first_sum, second_sum)
+    home_one = send_home(blocks_one)
     for turn in rounds[1:]:
         terms_zero = collect_round(terms_zero, narrow, turn)
-    state = convolve_back(blocks // 2, blocks * 3 // 4, state)
-    state, terms_zero, first_sum, second_sum = tie(state, terms_zero, first_sum, second_sum)
-    home_zero = send_home(terms_zero)
     second_sent = swap_axis(second_sum, 0)
-    first_sent = swap_axis(first_sum, 0)
-    state = convolve_back(blocks * 3 // 4, blocks, state)
-    state, home_one, second_sum, second_sent, first_sum, first_sent = tie(
-        state, home_one, second_sum, second_sent, first_sum, first_sent
-    )
+    state = convolve_back(blocks // 2, blocks // 4, state)
+    state, terms_zero, second_sum, second_sent = tie(state, terms_zero, second_sum, second_sent)
+    second_sum = add_swapped(second_sum, second_sent)
+    blocks_zero, state = tie(home_blocks(terms_zero), state)
+    home_zero = send_home(blocks_zero)
     total_one = {0: home_one}
     spread_level(total_one, narrow, 1)
-    first_sum = add_swapped(first_sum, first_sent)
+    for turn in rounds[1:-1]:
+        second_sum = add_swapped(second_sum, swap_axis(second_sum, turn))
+    second_sent = swap_axis(second_sum, rounds[-1])
+    state = convolve_back(blocks * 3 // 4, blocks // 4, state)
+    state, total_one, second_sum, second_sent = tie(state, total_one, second_sum, second_sent)
     second_sum = add_swapped(second_sum, second_sent)
-    for turn in rounds[1:]:
-        first_sum = add_swapped(first_sum, swap_axis(first_sum, turn))
-        second_sum = add_swapped(second_sum, swap_axis(second_sum, turn))
     kern_grad, table_grad = state
     table_grad = table_grad[:vocab].reshape(vocab, 8, CDIM).sum(axis=1)
-    model_grads = jnp.concatenate(
-        [
-            grad_type_zero,
-            grad_type_one,
-            grad_embed_gain,
-            grad_embed_zero,
-            grad_embed_shift,
-            grad_gain_one,
-            grad_gain_two,
-            grad_shift_zero,
-            grad_shift_one,
-            grad_shift_two,
-            grad_shift_three,
-            grad_shift_four,
-            grad_shift_five,
-        ]
-    )
     late_rows = to_rows(table_grad.reshape(1, -1), wide, lanes)
     late_rows = jnp.pad(late_rows, ((0, 0), (0, late_count - late_rows.shape[1]), (0, 0)))
     small_part = make_shares(
@@ -1225,26 +1302,35 @@
         )
         return lax.dynamic_index_in_dim(value, side, at, keepdims=False), got
 
+    def halves(value):
+        return value.reshape(2, -1, *value.shape[1:])
+
+    chip_bits = [wide >> i for i in range(1, wide.bit_length() - 1)]
+    place_bits = bits_of(narrow, 1)
     kept, got = exchange(small_part, 1, 1)
-    got, total_one, home_zero, first_sum, second_sum = tie(got, total_one, home_zero, first_sum, second_sum)
+    first_sent = swap_axis(first_sum, 0)
+    for level in levels[1:]:
+        spread_level(total_one, narrow, level)
+    kept, got, first_sum, first_sent, total_one = tie(kept, got, first_sum, first_sent, total_one)
+    small_sum = add_low(kept, got)
+    for bit in chip_bits:
+        kept, got = exchange(halves(small_sum), 0, bit)
+        small_sum = add_low(kept, got)
+    first_sum = add_swapped(first_sum, first_sent)
+    for turn in rounds[1:-1]:
+        first_sum = add_swapped(first_sum, swap_axis(first_sum, turn))
+    first_sent = swap_axis(first_sum, rounds[-1])
+    small_sum, first_sum, first_sent, home_zero = tie(small_sum, first_sum, first_sent, home_zero)
+    first_sum = add_swapped(first_sum, first_sent)
     total_zero = {0: home_zero}
     spread_level(total_zero, narrow, 1)
-    for level in levels[1:]:
-        spread_level(total_one, narrow, level)
-    small_sum = add_low(kept, got)
-    bit = wide // 2
-    while bit > 1:
-        kept, got = exchange(small_sum.reshape(2, -1, *small_sum.shape[1:]), 0, bit)
-        small_sum = add_low(kept, got)
-        bit //= 2
-    total_zero, small_sum = tie(total_zero, small_sum)
+    small_sum = small_sum[0].astype(jnp.float32)
+    for bit in place_bits[:-1]:
+        small_sum = small_sum + hop(small_sum.astype(jnp.bfloat16), narrow, bit).astype(jnp.float32)
+    small_sum, total_zero = tie(small_sum, total_zero)
+    small_got = hop(small_sum.astype(jnp.bfloat16), narrow, place_bits[-1])
     for level in levels[1:]:
         spread_level(total_zero, narrow, level)
-    small_sum = small_sum[0].astype(jnp.float32)
-    for bit in bits_of(narrow, 0):
-        small_got = hop(small_sum.astype(jnp.bfloat16), narrow, bit)
-        if bit > 1:
-            small_sum = small_sum + small_got.astype(jnp.float32)
     weight_high = [laid_out(total_zero), laid_out(total_one)]
     grad_ff_out_sum, grad_ff_in_sum = split_deep(first_sum, first_sizes)
     grad_out_sum, *grad_qkv_sums, grad_projection_sum, grad_position_sum = split_deep(second_sum, second_sizes)

time: 749 us -> 725 us (0.968)
  local copies, waits for them, and re-layouts: 111 us -> 77.7 us
  Pallas kernels: 306 us -> 339 us
  waiting for transfers between devices: 106 us -> 85.2 us
  matrix products: 46.9 us -> 29.3 us
  other arithmetic: 89.4 us -> 103 us
    pallas_call x2 -> x6, Pallas kernels: 68.8 us -> 104 us  [the longest x2 42.5 us: mix_grad(): pl.pallas_call(functools.partial(mix_grad_body, rows), grid_spec=pltpu.Pr...]
    ppermute x38, waiting for transfers between devices: 89.2 us -> 63.9 us  [hop(): return lax.ppermute(value, 'narrow', [(i, i ^ bit) for i in range(narrow)])]
    unnamed x249 -> x230, local copies, waits for them, and re-layouts: 54.1 us -> 33.2 us
    dot_general x21 -> x14, matrix products: 46.9 us -> 29.3 us  [matmul(): lax.dot_general(left, right, dims, preferred_element_type=jnp.float32)]
    pallas_call x1, Pallas kernels: 17.1 us -> 8.9 us  [attend(): pl.pallas_call(attend_body, grid_spec=pltpu.PrefetchScalarGridSpec(num_sc...]
    convert_element_type x19, other arithmetic: 37.7 us -> 45.8 us  [add_low(): (left.astype(jnp.float32) + right.astype(jnp.float32)).astype(jnp.bfloat16)]
  transfers between devices with their start and end apart: 60 -> 60, of which waited for: 20 -> 20; matrix products, arithmetic and copies ran while one was open for 22% -> 20% of each run, Pallas kernels for 40% -> 44%
where the time goes in v3:
time: 725 us; the launch traced here: 716 us
  Pallas kernels  339 us (47%)
  other arithmetic  103 us (14%)
  waiting for transfers between devices  85.2 us (12%)
  local copies, waits for them, and re-layouts  77.7 us (11%)
  starting transfers between devices  46.9 us (6%)
  matrix products  29.3 us (4%)
  blocking collectives  17.8 us (2%)
  between operations  16.8 us (2%)
    pallas_call x3, Pallas kernels, conv_backward(): pl.pallas_call(functools.partial(conv_bwd_body, block, filters), grid=(co...  105 us
    ppermute x38, waiting for transfers between devices, hop(): return lax.ppermute(value, 'narrow', [(i, i ^ bit) for i in range(narrow)])  63.9 us
    pallas_call x2, Pallas kernels, conv_forward(): pl.pallas_call(functools.partial(conv_fwd_body, block, filters, len(state...  48.6 us
    convert_element_type x19, other arithmetic, add_low(): (left.astype(jnp.float32) + right.astype(jnp.float32)).astype(jnp.bfloat16)  45.8 us
    pallas_call x2, Pallas kernels, mix_grad(): pl.pallas_call(functools.partial(mix_grad_body, rows), grid_spec=pltpu.Pr...  42.5 us
    ppermute x38, starting transfers between devices, hop(): return lax.ppermute(value, 'narrow', [(i, i ^ bit) for i in range(narrow)])  41.6 us
    pallas_call x2, Pallas kernels, mix_forward(): pl.pallas_call(functools.partial(mix_forward_body, narrow, layer), grid_s...  40.8 us
    pallas_call x2, Pallas kernels, mix_pull(): pl.pallas_call(functools.partial(mix_pull_body, narrow, layer), grid_spec...  38.7 us
  transfers between devices with their start and end apart: 60, of which 20 were waited for; matrix products, arithmetic and copies ran while one was open for 20% of the time, Pallas kernels for 44%

profile of v3, /device:TPU:0, one launch (start us, length us, event | category | flops | bytes accessed | tf_op | source)
XLA Modules:
  0.0 715.5 jit_solution(4900414322508731651)
XLA Ops:
  14.8 1.8 make_share.1
  17.4 17.8 %all-gather.1 = bf16[1152,256]{1,0:T(8,128)(2,1)S(1)} all-gather(bf16[144,256]{1,0:T(8,128)(2,1)} %make_share.1), channel_id=3, replica_groups=mesh['narrow'=4,'wide'=8] {'wide'}, dimensions={0}, use_global_device_ids=true | all-gather | bytes 663552 | tf_op jit(solution)/shard_map/all_gather | solution.py:998
  36.1 2.3 make_kernel.1.kern_ref
  42.7 24.1 %conv_forward.2 = (bf16[25600,128]{1,0:T(8,128)(2,1)}, f32[512,2048]{1,0:T(8,128)}) custom-call(s32[512,50]{1,0:T(8,128)} %copy.80.ids_ref, s32[512,1]{1,0:T(8,128)} %copy.81.cnt_ref, bf16[8,384,128]{2,1,0:T(8,128)(2,1)} %copy-done.68, bf16[128,2048]{1,0:T(8,128)(2,1)} %make_kernel.1.kern_ref), custom_call_target="tpu_custom_call" | custom-call | flops 838860800 | bytes 524288 | tf_op jit(solution)/shard_map/conv_forward/pallas_call | solution.py:126
  69.6 1.6 collective-permute-start.1
  76.9 24.4 %conv_forward.3 = (bf16[25600,128]{1,0:T(8,128)(2,1)}, f32[512,2048]{1,0:T(8,128)}) custom-call(s32[512,50]{1,0:T(8,128)} %copy.80.ids_ref, s32[512,1]{1,0:T(8,128)} %copy.81.cnt_ref, bf16[8,384,128]{2,1,0:T(8,128)(2,1)} %copy-done.68, bf16[128,2048]{1,0:T(8,128)(2,1)} %make_kernel.1.kern_ref, ...), custom_call_target="tpu_custom_call", output_to_operand_aliasing={{0}: (4, {}), {1}: (5, {})} | custom-call | flops 838860800 | bytes 524288 | tf_op jit(solution)/shard_map/conv_forward/pallas_call | solution.py:126
  101.3 12.4 %all-gather.12.cloned.1.call-done = bf16[8,256,512]{2,1,0:T(8,128)(2,1)} async-done(((bf16[2,256,512]{2,1,0:T(8,128)(2,1)}), bf16[8,256,512]{2,1,0:T(8,128)(2,1)}) %all-gather.12.cloned.1.call-update) | async-done | bytes 2097168 | tf_op jit(solution)/shard_map/all_gather | solution.py:595
  114.3 1.8 pad_maximum_fusion
  121.3 4.2 fusion.38
  125.5 4.6 collective-permute-done.4.twin_ref
  130.1 6.9 collective-permute-done.3.rest_4_
  137.0 2.4 collective-permute-done.2.rest_3_
  156.1 20.4 %mix_forward.2 = (f32[512,2048]{1,0:T(8,128)}, bf16[512,2048]{1,0:T(8,128)(2,1)}, f32[512,2048]{1,0:T(8,128)}, f32[512,2048]{1,0:T(8,128)}, f32[512,2048]{1,0:T(8,128)}) custom-call(s32[3]{0:T(128)} %pad_add_fusion.where_ref, bf16[512,2048]{1,0:T(8,128)(2,1)} %get-tuple-element.232.low_ref, f32[512,2048]{1,0:T(8,128)} %get-tuple-element.451.carry_ref, ...), custom_call_target="tpu_custom_call" | custom-call | flops 2147483648 | bytes 4194304 | tf_op jit(solution)/shard_map/mix_forward/pallas_call | solution.py:752
  179.3 3.8 pad_maximum_fusion.1
  186.7 18.8 %collective-permute-done.10.rest_4_ = bf16[768,512]{1,0:T(8,128)(2,1)S(1)} collective-permute-done((bf16[768,512]{1,0:T(8,128)(2,1)S(1)}, bf16[768,512]{1,0:T(8,128)(2,1)S(1)}, u32[]{:S(2)}, u32[]{:S(2)}) %collective-permute-start.10) | collective-permute-done | bytes 786464 | tf_op jit(solution)/shard_map/ppermute | solution.py:520
  210.8 20.4 %mix_forward.3 = (f32[512,2048]{1,0:T(8,128)}, bf16[512,2048]{1,0:T(8,128)(2,1)}, f32[512,2048]{1,0:T(8,128)}, f32[512,2048]{1,0:T(8,128)}, f32[512,2048]{1,0:T(8,128)}) custom-call(s32[3]{0:T(128)} %pad_add_fusion.where_ref, bf16[512,2048]{1,0:T(8,128)(2,1)} %get-tuple-element.248.low_ref, f32[512,2048]{1,0:T(8,128)} %get-tuple-element.249.carry_ref, ...), custom_call_target="tpu_custom_call" | custom-call | flops 2147483648 | bytes 4194304 | tf_op jit(solution)/shard_map/mix_forward/pallas_call | solution.py:752
  231.2 3.6 collective-permute-done.13.rest_2_
  242.7 2.1 fusion.36
  249.0 8.9 %attend.1 = (bf16[512,768]{1,0:T(8,128)(2,1)S(1)}, f32[6,8,512]{2,1,0:T(8,128)S(1)}) custom-call(s32[1]{0:T(128)} %copy.137.length_ref, bf16[512,768]{1,0:T(8,128)(2,1)S(1)} %add_convert_fusion.25.q_ref, bf16[512,768]{1,0:T(8,128)(2,1)S(1)} %convolution_convert_fusion.1.k_ref, bf16[512,768]{1,0:T(8,128)(2,1)S(1)} %add_convert_fusion.24.v_ref), custom_call_target="tpu_custom_call" | custom-call | flops 201326592 | bytes 393216 | tf_op jit(solution)/shard_map/attend/pallas_call | solution.py:318
  261.8 8.5 %assemble.1 = bf16[8,768,768]{2,1,0:T(8,128)(2,1)} custom-call(s32[3]{0:T(128)} %pad_add_fusion.where_ref, bf16[2,768,384]{2,1,0:T(8,128)(2,1)} %copy-done.18, bf16[2,768,384]{2,1,0:T(8,128)(2,1)} %copy-done.22, bf16[2,768,384]{2,1,0:T(8,128)(2,1)} %copy-done.21, bf16[768,384]{1,0:T(8,128)(2,1)} %copy-done.52, bf16[768,384]{1,0:T(8,128)(2,1)} %copy-done.51, ...), custom_call_target="tpu_custom_call" | custom-call | bytes 589824 | tf_op jit(solution)/shard_map/assemble/pallas_call | solution.py:648
  270.4 2.8 slice.540
  273.2 2.3 copy-done.11
  276.2 2.8 multiply_convert_fusion
  279.0 1.6 copy-done.48
  280.6 2.8 fusion.34
  285.5 1.9 convert_reduce_fusion.1
  287.4 5.3 convert_reduce_fusion
  294.3 4.4 multiply_reduce_fusion
  298.7 12.0 %first_parts.1 = bf16[8,768,768]{2,1,0:T(8,128)(2,1)} custom-call(bf16[512,3072]{1,0:T(8,128)(2,1)} %copy-done.48, bf16[512,768]{1,0:T(8,128)(2,1)} %copy-done.41, bf16[512,768]{1,0:T(8,128)(2,1)} %copy-done.43, bf16[512,3072]{1,0:T(8,128)(2,1)} %copy-done.49), custom_call_target="tpu_custom_call" | custom-call | flops 301989888 | bytes 393216 | tf_op jit(solution)/shard_map/first_parts/pallas_call | solution.py:899
  310.7 3.7 convert_reduce_fusion.2
  314.4 1.7 convolution_convert_fusion.pull_ref
  320.2 13.7 %attend_back.1.proj_ref = bf16[3,512,768]{2,1,0:T(8,128)(2,1)S(1)} custom-call(s32[1]{0:T(128)} %copy.137.length_ref, bf16[512,768]{1,0:T(8,128)(2,1)S(1)} %copy-done.5, bf16[512,768]{1,0:T(8,128)(2,1)S(1)} %copy-done.3, bf16[512,768]{1,0:T(8,128)(2,1)S(1)} %add_convert_fusion.24.v_ref, bf16[512,768]{1,0:T(8,128)(2,1)S(1)} %copy-done.7, ...), custom_call_target="tpu_custom_call" | custom-call | flops 201326592 | bytes 393216 | tf_op jit(solution)/shard_map/attend_back/pallas_call | solution.py:339
  341.1 3.8 fusion.52.pull_ref
  344.9 21.3 %mix_grad.2 = (bf16[4,1024,512]{2,1,0:T(8,128)(2,1)}, bf16[4,1024,512]{2,1,0:T(8,128)(2,1)}, bf16[4,1024,512]{2,1,0:T(8,128)(2,1)}, bf16[4,1024,512]{2,1,0:T(8,1...) custom-call(s32[3]{0:T(128)} %pad_add_fusion.where_ref, bf16[512,2048]{1,0:T(8,128)(2,1)} %get-tuple-element.248.low_ref, ...), custom_call_target="tpu_custom_call" | custom-call | flops 536870912 | bytes 1048576 | tf_op jit(solution)/shard_map/mix_grad/pallas_call | solution.py:813
  366.7 19.5 %mix_pull.2.pull_ref = f32[512,2048]{1,0:T(8,128)} custom-call(s32[3]{0:T(128)} %pad_add_fusion.where_ref, bf16[2,512,2048]{2,1,0:T(8,128)(2,1)} %get-tuple-element.293.grads_ref, f32[512,2048]{1,0:T(8,128)} %get-tuple-element.287.gate_ref, f32[512,2048]{1,0:T(8,128)} %fusion.52.pull_ref, bf16[2,256,4096]{2,1,0:T(8,128)(2,1)} %shard_ref.7, ...), custom_call_target="tpu_custom_call" | custom-call | flops 536870912 | bytes 1048576 | tf_op jit(solution)/shard_map/mix_pull/pallas_call | solution.py:861
  386.3 5.7 add_convert_fusion.4
  393.1 4.2 add_convert_fusion.5
  399.8 11.3 %second_parts.1 = bf16[8,704,768]{2,1,0:T(8,128)(2,1)} custom-call(bf16[512,768]{1,0:T(8,128)(2,1)} %copy-done.6, bf16[512,768]{1,0:T(8,128)(2,1)} %copy-done.44, bf16[512,768]{1,0:T(8,128)(2,1)} %copy-done.42, bf16[3,512,768]{2,1,0:T(8,128)(2,1)} %copy-done, bf16[512,2048]{1,0:T(8,128)(2,1)} %get-tuple-element.257.top_ref, bf16[512,768]{1,0:T(8,128)(2,1)} %copy-done.23, ...), custom_call_target="tpu_custom_call" | custom-call | flops 301989888 | bytes 393216 | tf_op jit(solution)/shard_map/second_parts/pallas_call | solution.py:919
  411.1 21.2 %mix_grad.3 = (bf16[4,1024,512]{2,1,0:T(8,128)(2,1)}, bf16[4,1024,512]{2,1,0:T(8,128)(2,1)}, bf16[4,1024,512]{2,1,0:T(8,128)(2,1)}, bf16[4,1024,512]{2,1,0:T(8,1...) custom-call(s32[3]{0:T(128)} %pad_add_fusion.where_ref, bf16[512,2048]{1,0:T(8,128)(2,1)} %get-tuple-element.232.low_ref, ...), custom_call_target="tpu_custom_call" | custom-call | flops 536870912 | bytes 1048576 | tf_op jit(solution)/shard_map/mix_grad/pallas_call | solution.py:813
  432.3 7.5 %collective-permute-done.22 = bf16[2,1024,512]{2,1,0:T(8,128)(2,1)} collective-permute-done((bf16[2,1024,512]{2,1,0:T(8,128)(2,1)}, bf16[2,1024,512]{2,1,0:T(8,128)(2,1)}, u32[]{:S(2)}, u32[]{:S(2)}) %collective-permute-start.22) | collective-permute-done | bytes 2097184 | tf_op jit(solution)/shard_map/ppermute | solution.py:520
  439.9 5.2 collective-permute-done.21
  448.3 4.7 add_convert_fusion.22
  453.0 3.5 add_convert_fusion.20
  457.9 19.1 %mix_pull.3 = f32[512,2048]{1,0:T(8,128)} custom-call(s32[3]{0:T(128)} %pad_add_fusion.where_ref, bf16[2,512,2048]{2,1,0:T(8,128)(2,1)} %get-tuple-element.321.grads_ref, f32[512,2048]{1,0:T(8,128)} %get-tuple-element.302.gate_ref, f32[512,2048]{1,0:T(8,128)} %mix_pull.2.pull_ref, bf16[2,256,4096]{2,1,0:T(8,128)(2,1)} %shard_ref.7, ...), custom_call_target="tpu_custom_call" | custom-call | flops 536870912 | bytes 1048576 | tf_op jit(solution)/shard_map/mix_pull/pallas_call | solution.py:861
  477.0 8.0 %fusion.9.ginv_ref = f32[512,2048]{1,0:T(8,128)} fusion(f32[512,2048]{1,0:T(8,128)} %get-tuple-element.230, f32[512,2048]{1,0:T(8,128)} %mix_pull.3, s32[2048]{0:T(1024)S(1)} %copy-done.81, s32[512]{0:T(512)S(1)} %bitcast.307), kind=kLoop, calls=%fused_computation.17 | loop fusion | flops 15728640 | bytes 12593152 | tf_op jit(solution)/shard_map/div | solution.py:1264
  486.4 4.0 add_convert_fusion
  492.0 4.2 add_convert_fusion.2
  499.0 51.4 %conv_backward.3 = (f32[128,2048]{1,0:T(8,128)}, f32[272,128]{1,0:T(8,128)}) custom-call(s32[50,512]{1,0:T(8,128)} %get-tuple-element.525.idst_ref, bf16[25600,128]{1,0:T(8,128)(2,1)} %get-tuple-element.284.x_ref, f32[512,2048]{1,0:T(8,128)} %fusion.9.ginv_ref, bf16[128,2048]{1,0:T(8,128)(2,1)} %make_kernel.1.kern_ref, ...), custom_call_target="tpu_custom_call", output_to_operand_aliasing={{0}: (4, {}), {1}: (5, {})} | custom-call | flops 1677721600 | bytes 524288 | tf_op jit(solution)/shard_map/conv_backward/pallas_call | solution.py:222
  550.5 1.7 add_convert_fusion.19
  554.6 4.1 add_convert_fusion.16
  559.0 3.5 add_convert_fusion.14
  568.7 26.9 %conv_backward.4 = (f32[128,2048]{1,0:T(8,128)}, f32[272,128]{1,0:T(8,128)}) custom-call(s32[50,512]{1,0:T(8,128)} %get-tuple-element.525.idst_ref, bf16[25600,128]{1,0:T(8,128)(2,1)} %get-tuple-element.284.x_ref, f32[512,2048]{1,0:T(8,128)} %fusion.9.ginv_ref, bf16[128,2048]{1,0:T(8,128)(2,1)} %make_kernel.1.kern_ref, ...), custom_call_target="tpu_custom_call", output_to_operand_aliasing={{0}: (4, {}), {1}: (5, {})} | custom-call | flops 838860800 | bytes 262144 | tf_op jit(solution)/shard_map/conv_backward/pallas_call | solution.py:222
  603.2 2.5 add_convert_fusion.13
  610.5 27.0 %conv_backward.5 = (f32[128,2048]{1,0:T(8,128)}, f32[272,128]{1,0:T(8,128)}) custom-call(s32[50,512]{1,0:T(8,128)} %get-tuple-element.525.idst_ref, bf16[25600,128]{1,0:T(8,128)(2,1)} %get-tuple-element.284.x_ref, f32[512,2048]{1,0:T(8,128)} %fusion.9.ginv_ref, bf16[128,2048]{1,0:T(8,128)(2,1)} %make_kernel.1.kern_ref, ...), custom_call_target="tpu_custom_call", output_to_operand_aliasing={{0}: (4, {}), {1}: (5, {})} | custom-call | flops 838860800 | bytes 262144 | tf_op jit(solution)/shard_map/conv_backward/pallas_call | solution.py:222
  641.6 1.7 slice_bitcast_fusion.16
  645.6 2.7 make_shares.1
  658.5 1.7 collective-permute-start.45
  666.9 3.4 collective-permute-done.43
  670.3 3.1 collective-permute-done.45
  681.0 7.7 %collective-permute-done.46 = bf16[144,256]{1,0:T(8,128)(2,1)S(1)} collective-permute-done((bf16[144,256]{1,0:T(8,128)(2,1)S(1)}, bf16[144,256]{1,0:T(8,128)(2,1)S(1)}, u32[]{:S(2)}, u32[]{:S(2)}) %collective-permute-start.46) | collective-permute-done | bytes 73760 | tf_op jit(solution)/shard_map/ppermute | solution.py:520
  693.2 1.6 collective-permute-start.51
  694.8 2.0 collective-permute-done.49.second_ref
  697.5 1.9 take_apart.1
  704.6 3.9 maximum_convert_fusion
  (500 shorter events, 162.8 us)
Async XLA Ops:
  7.2 59.9 %all-gather.10.cloned.1.call-start = ((), (), s32[]{:S(2)}) async-start(), calls=%async_computation.8 | async-start | bytes 2621440 | tf_op jit(solution)/shard_map/all_gather | solution.py:595
  16.6 97.1 %all-gather.12.cloned.1.call-start = ((), (), s32[]{:S(2)}) async-start(), calls=%async_computation.9 | async-start | bytes 2621440 | tf_op jit(solution)/shard_map/all_gather | solution.py:595
  17.3 169.4 %all-gather.16.cloned.1.call-start = ((), (), s32[]{:S(2)}) async-start(), calls=%async_computation.11 | async-start | bytes 1474560 | tf_op jit(solution)/shard_map/all_gather | solution.py:595
  67.9 167.2 %all-gather.14.cloned.1.call-start = ((), (), s32[]{:S(2)}) async-start(), calls=%async_computation.10 | async-start | bytes 9732096 | tf_op jit(solution)/shard_map/all_gather | solution.py:1053
  69.6 44.6 %copy-start.12 = (bf16[2,768,512]{2,1,0:T(8,128)(2,1)}, bf16[2,768,512]{2,1,0:T(8,128)(2,1)S(1)}, u32[]{:S(2)}) copy-start(bf16[2,768,512]{2,1,0:T(8,128)(2,1)S(1)} %pad_maximum_fusion.6.rest_0_) | copy-start | bytes 4718596
  69.6 44.1 %collective-permute-start.1 = (bf16[2,768,512]{2,1,0:T(8,128)(2,1)S(1)}, bf16[2,768,512]{2,1,0:T(8,128)(2,1)S(1)}, u32[]{:S(2)}, u32[]{:S(2)}) collective-permute-start(bf16[2,768,512]{2,1,0:T(8,128)(2,1)S(1)} %pad_maximum_fusion.6.rest_0_), channel_id=1, source_target_pairs={{0,16},{8,24},{16,0},{24,8},{1,17},{9,25},{17,1},{25,9},{2,18},{10... | collective-permute-start | bytes 4718600 | tf_op jit(solution)/shard_map/ppermute | solution.py:520
  71.3 42.5 %collective-permute-start = (bf16[2,768,512]{2,1,0:T(8,128)(2,1)S(1)}, bf16[2,768,512]{2,1,0:T(8,128)(2,1)}, u32[]{:S(2)}, u32[]{:S(2)}) collective-permute-start(bf16[2,768,512]{2,1,0:T(8,128)(2,1)S(1)} %pad_maximum_fusion.6.rest_0_), channel_id=1, source_target_pairs={{0,8},{8,0},{16,24},{24,16},{1,9},{9,1},{17,25},{25,17},{2,10},{10... | collective-permute-start | bytes 4718600 | tf_op jit(solution)/shard_map/ppermute | solution.py:520
  113.8 440.4 %reduce-scatter.5.cloned.1.call-start = ((), (), s32[]{:S(2)}) async-start(), calls=%async_computation.4 | async-start | bytes 10616832 | tf_op jit(solution)/shard_map/reduce_scatter | solution.py:1135
  116.2 23.3 %collective-permute-start.5 = (bf16[3,2,768,512]{3,2,1,0:T(8,128)(2,1)S(1)}, bf16[3,2,768,512]{3,2,1,0:T(8,128)(2,1)S(1)}, u32[]{:S(2)}, u32[]{:S(2)}) collective-permute-start(bf16[3,2,768,512]{3,2,1,0:T(8,128)(2,1)S(1)} %pad_maximum_fusion), channel_id=1, source_target_pairs={{0,1},{1,0},{2,3},{3,2},{4,5},{5,4},{6,7},{7,6},{8,9},{9,8},{10,11... | collective-permute-start | bytes 14155784 | tf_op jit(solution)/shard_map/ppermute | solution.py:512
  116.9 13.2 %collective-permute-start.4 = (bf16[2,256,4096]{2,1,0:T(8,128)(2,1)S(1)}, bf16[2,256,4096]{2,1,0:T(8,128)(2,1)S(1)}, u32[]{:S(2)}, u32[]{:S(2)}) collective-permute-start(bf16[2,256,4096]{2,1,0:T(8,128)(2,1)S(1)} %copy-done.8), channel_id=1, source_target_pairs={{0,1},{1,0},{2,3},{3,2},{4,5},{5,4},{6,7},{7,6},{8,9},{9,8},{10,11... | collective-permute-start | bytes 12582920 | tf_op jit(solution)/shard_map/ppermute | solution.py:512
  117.0 20.0 %collective-permute-start.3 = (bf16[768,512]{1,0:T(8,128)(2,1)S(1)}, bf16[768,512]{1,0:T(8,128)(2,1)S(1)}, u32[]{:S(2)}, u32[]{:S(2)}) collective-permute-start(bf16[768,512]{1,0:T(8,128)(2,1)S(1)} %slice_bitcast_fusion.6), channel_id=1, source_target_pairs={{0,8},{8,0},{16,24},{24,16},{1,9},{9,1},{17,25},{25,17},{2,10},{10... | collective-permute-start | bytes 2359304 | tf_op jit(solution)/shard_map/ppermute | solution.py:520
  119.7 19.7 %collective-permute-start.2 = (bf16[768,512]{1,0:T(8,128)(2,1)S(1)}, bf16[768,512]{1,0:T(8,128)(2,1)S(1)}, u32[]{:S(2)}, u32[]{:S(2)}) collective-permute-start(bf16[768,512]{1,0:T(8,128)(2,1)S(1)} %slice_bitcast_fusion.7), channel_id=1, source_target_pairs={{0,16},{8,24},{16,0},{24,8},{1,17},{9,25},{17,1},{25,9},{2,18},{10... | collective-permute-start | bytes 2359304 | tf_op jit(solution)/shard_map/ppermute | solution.py:520
  140.9 15.2 %collective-permute-start.8 = (bf16[1,2,768,512]{3,2,1,0:T(8,128)(2,1)}, bf16[1,2,768,512]{3,2,1,0:T(8,128)(2,1)}, u32[]{:S(2)}, u32[]{:S(2)}) collective-permute-start(bf16[1,2,768,512]{3,2,1,0:T(8,128)(2,1)} %maximum_bitcast_fusion), channel_id=1, source_target_pairs={{0,1},{1,0},{2,3},{3,2},{4,5},{5,4},{6,7},{7,6},{8,9},{9,8},{10,11... | collective-permute-start | bytes 4718600 | tf_op jit(solution)/shard_map/ppermute | solution.py:512
  142.1 37.1 %copy-start.13 = (bf16[2,768,512]{2,1,0:T(8,128)(2,1)}, bf16[2,768,512]{2,1,0:T(8,128)(2,1)S(1)}, u32[]{:S(2)}) copy-start(bf16[2,768,512]{2,1,0:T(8,128)(2,1)S(1)} %pad_maximum_fusion.7.rest_0_) | copy-start | bytes 4718596
  142.1 35.9 %collective-permute-start.7 = (bf16[2,768,512]{2,1,0:T(8,128)(2,1)S(1)}, bf16[2,768,512]{2,1,0:T(8,128)(2,1)}, u32[]{:S(2)}, u32[]{:S(2)}) collective-permute-start(bf16[2,768,512]{2,1,0:T(8,128)(2,1)S(1)} %pad_maximum_fusion.7.rest_0_), channel_id=1, source_target_pairs={{0,16},{8,24},{16,0},{24,8},{1,17},{9,25},{17,1},{25,9},{2,18},{10... | collective-permute-start | bytes 4718600 | tf_op jit(solution)/shard_map/ppermute | solution.py:520
  143.6 35.7 %collective-permute-start.6 = (bf16[2,768,512]{2,1,0:T(8,128)(2,1)S(1)}, bf16[2,768,512]{2,1,0:T(8,128)(2,1)}, u32[]{:S(2)}, u32[]{:S(2)}) collective-permute-start(bf16[2,768,512]{2,1,0:T(8,128)(2,1)S(1)} %pad_maximum_fusion.7.rest_0_), channel_id=1, source_target_pairs={{0,8},{8,0},{16,24},{24,16},{1,9},{9,1},{17,25},{25,17},{2,10},{10... | collective-permute-start | bytes 4718600 | tf_op jit(solution)/shard_map/ppermute | solution.py:520
  183.1 22.7 %collective-permute-start.11 = (bf16[3,2,768,512]{3,2,1,0:T(8,128)(2,1)}, bf16[3,2,768,512]{3,2,1,0:T(8,128)(2,1)}, u32[]{:S(2)}, u32[]{:S(2)}) collective-permute-start(bf16[3,2,768,512]{3,2,1,0:T(8,128)(2,1)} %pad_maximum_fusion.1), channel_id=1, source_target_pairs={{0,1},{1,0},{2,3},{3,2},{4,5},{5,4},{6,7},{7,6},{8,9},{9,8},{10,11... | collective-permute-start | bytes 14155784 | tf_op jit(solution)/shard_map/ppermute | solution.py:512
  185.5 20.0 %collective-permute-start.10 = (bf16[768,512]{1,0:T(8,128)(2,1)S(1)}, bf16[768,512]{1,0:T(8,128)(2,1)S(1)}, u32[]{:S(2)}, u32[]{:S(2)}) collective-permute-start(bf16[768,512]{1,0:T(8,128)(2,1)S(1)} %slice_bitcast_fusion.4), channel_id=1, source_target_pairs={{0,8},{8,0},{16,24},{24,16},{1,9},{9,1},{17,25},{25,17},{2,10},{10... | collective-permute-start | bytes 2359304 | tf_op jit(solution)/shard_map/ppermute | solution.py:520
  186.1 19.7 %collective-permute-start.9 = (bf16[768,512]{1,0:T(8,128)(2,1)S(1)}, bf16[768,512]{1,0:T(8,128)(2,1)S(1)}, u32[]{:S(2)}, u32[]{:S(2)}) collective-permute-start(bf16[768,512]{1,0:T(8,128)(2,1)S(1)} %slice_bitcast_fusion.5), channel_id=1, source_target_pairs={{0,16},{8,24},{16,0},{24,8},{1,17},{9,25},{17,1},{25,9},{2,18},{10... | collective-permute-start | bytes 2359304 | tf_op jit(solution)/shard_map/ppermute | solution.py:520
  206.0 4.8 collective-permute-start.14
  206.8 28.3 %copy-start.18 = (bf16[2,768,384]{2,1,0:T(8,128)(2,1)}, bf16[2,768,384]{2,1,0:T(8,128)(2,1)S(1)}, u32[]{:S(2)}) copy-start(bf16[2,768,384]{2,1,0:T(8,128)(2,1)S(1)} %pad_maximum_fusion.8.rest_0_) | copy-start | bytes 3538948
  206.8 28.0 %collective-permute-start.13 = (bf16[2,768,384]{2,1,0:T(8,128)(2,1)S(1)}, bf16[2,768,384]{2,1,0:T(8,128)(2,1)S(1)}, u32[]{:S(2)}, u32[]{:S(2)}) collective-permute-start(bf16[2,768,384]{2,1,0:T(8,128)(2,1)S(1)} %pad_maximum_fusion.8.rest_0_), channel_id=1, source_target_pairs={{0,16},{8,24},{16,0},{24,8},{1,17},{9,25},{17,1},{25,9},{2,18},{10... | collective-permute-start | bytes 3538952 | tf_op jit(solution)/shard_map/ppermute | solution.py:520
  207.5 27.6 %collective-permute-start.12 = (bf16[2,768,384]{2,1,0:T(8,128)(2,1)S(1)}, bf16[2,768,384]{2,1,0:T(8,128)(2,1)S(1)}, u32[]{:S(2)}, u32[]{:S(2)}) collective-permute-start(bf16[2,768,384]{2,1,0:T(8,128)(2,1)S(1)} %pad_maximum_fusion.8.rest_0_), channel_id=1, source_target_pairs={{0,8},{8,0},{16,24},{24,16},{1,9},{9,1},{17,25},{25,17},{2,10},{10... | collective-permute-start | bytes 3538952 | tf_op jit(solution)/shard_map/ppermute | solution.py:520
  235.6 22.3 %collective-permute-start.17 = (bf16[3,2,768,384]{3,2,1,0:T(8,128)(2,1)S(1)}, bf16[3,2,768,384]{3,2,1,0:T(8,128)(2,1)S(1)}, u32[]{:S(2)}, u32[]{:S(2)}) collective-permute-start(bf16[3,2,768,384]{3,2,1,0:T(8,128)(2,1)S(1)} %pad_maximum_fusion.3), channel_id=1, source_target_pairs={{0,1},{1,0},{2,3},{3,2},{4,5},{5,4},{6,7},{7,6},{8,9},{9,8},{10,11... | collective-permute-start | bytes 10616840 | tf_op jit(solution)/shard_map/ppermute | solution.py:512
  239.7 18.2 %collective-permute-start.16 = (bf16[768,384]{1,0:T(8,128)(2,1)S(1)}, bf16[768,384]{1,0:T(8,128)(2,1)S(1)}, u32[]{:S(2)}, u32[]{:S(2)}) collective-permute-start(bf16[768,384]{1,0:T(8,128)(2,1)S(1)} %slice_bitcast_fusion.10), channel_id=1, source_target_pairs={{0,8},{8,0},{16,24},{24,16},{1,9},{9,1},{17,25},{25,17},{2,10},{10... | collective-permute-start | bytes 1769480 | tf_op jit(solution)/shard_map/ppermute | solution.py:520
  241.3 16.6 %collective-permute-start.15 = (bf16[768,384]{1,0:T(8,128)(2,1)S(1)}, bf16[768,384]{1,0:T(8,128)(2,1)S(1)}, u32[]{:S(2)}, u32[]{:S(2)}) collective-permute-start(bf16[768,384]{1,0:T(8,128)(2,1)S(1)} %slice_bitcast_fusion.11), channel_id=1, source_target_pairs={{0,16},{8,24},{16,0},{24,8},{1,17},{9,25},{17,1},{25,9},{2,18},{10... | collective-permute-start | bytes 1769480 | tf_op jit(solution)/shard_map/ppermute | solution.py:520
  258.1 3.7 collective-permute-start.18
  316.1 238.0 %reduce-scatter.7.cloned.1.call-start = ((), (), s32[]{:S(2)}) async-start(), calls=%async_computation.5 | async-start | bytes 9732096 | tf_op jit(solution)/shard_map/reduce_scatter | solution.py:1135
  340.2 58.4 %copy-start.23 = (bf16[512,768]{1,0:T(8,128)(2,1)}, bf16[512,768]{1,0:T(8,128)(2,1)S(1)}, u32[]{:S(2)}) copy-start(bf16[512,768]{1,0:T(8,128)(2,1)S(1)} %get-tuple-element.441.embed_ref) | copy-start | bytes 2359300
  366.2 20.1 %collective-permute-start.19 = (bf16[4,1024,512]{2,1,0:T(8,128)(2,1)}, bf16[4,1024,512]{2,1,0:T(8,128)(2,1)}, u32[]{:S(2)}, u32[]{:S(2)}) collective-permute-start(bf16[4,1024,512]{2,1,0:T(8,128)(2,1)} %get-tuple-element.291), channel_id=1, source_target_pairs={{0,1},{1,0},{2,3},{3,2},{4,5},{5,4},{6,7},{7,6},{8,9},{9,8},{10,11... | collective-permute-start | bytes 12582920 | tf_op jit(solution)/shard_map/ppermute | solution.py:512
  366.2 20.0 %collective-permute-start.20 = (bf16[4,1024,512]{2,1,0:T(8,128)(2,1)}, bf16[4,1024,512]{2,1,0:T(8,128)(2,1)}, u32[]{:S(2)}, u32[]{:S(2)}) collective-permute-start(bf16[4,1024,512]{2,1,0:T(8,128)(2,1)} %get-tuple-element.292), channel_id=1, source_target_pairs={{0,1},{1,0},{2,3},{3,2},{4,5},{5,4},{6,7},{7,6},{8,9},{9,8},{10,11... | collective-permute-start | bytes 12582920 | tf_op jit(solution)/shard_map/ppermute | solution.py:512
  391.9 47.9 %collective-permute-start.22 = (bf16[2,1024,512]{2,1,0:T(8,128)(2,1)}, bf16[2,1024,512]{2,1,0:T(8,128)(2,1)}, u32[]{:S(2)}, u32[]{:S(2)}) collective-permute-start(bf16[2,1024,512]{2,1,0:T(8,128)(2,1)} %get-tuple-element.464), channel_id=1, source_target_pairs={{0,8},{8,0},{16,24},{24,16},{1,9},{9,1},{17,25},{25,17},{2,10},{10... | collective-permute-start | bytes 6291464 | tf_op jit(solution)/shard_map/ppermute | solution.py:520
  397.4 47.7 %collective-permute-start.21 = (bf16[2,1024,512]{2,1,0:T(8,128)(2,1)}, bf16[2,1024,512]{2,1,0:T(8,128)(2,1)}, u32[]{:S(2)}, u32[]{:S(2)}) collective-permute-start(bf16[2,1024,512]{2,1,0:T(8,128)(2,1)} %get-tuple-element.466), channel_id=1, source_target_pairs={{0,16},{8,24},{16,0},{24,8},{1,17},{9,25},{17,1},{25,9},{2,18},{10... | collective-permute-start | bytes 6291464 | tf_op jit(solution)/shard_map/ppermute | solution.py:520
  445.1 160.6 %reduce-scatter.9.cloned.1.call-start = ((), (), s32[]{:S(2)}) async-start(), calls=%async_computation.6 | async-start | bytes 2621440 | tf_op jit(solution)/shard_map/reduce_scatter | solution.py:1204
  445.3 39.7 %collective-permute-start.25 = (bf16[4,1024,512]{2,1,0:T(8,128)(2,1)}, bf16[4,1024,512]{2,1,0:T(8,128)(2,1)}, u32[]{:S(2)}, u32[]{:S(2)}) collective-permute-start(bf16[4,1024,512]{2,1,0:T(8,128)(2,1)} %get-tuple-element.319), channel_id=1, source_target_pairs={{0,1},{1,0},{2,3},{3,2},{4,5},{5,4},{6,7},{7,6},{8,9},{9,8},{10,11... | collective-permute-start | bytes 12582920 | tf_op jit(solution)/shard_map/ppermute | solution.py:512
  445.4 41.0 %collective-permute-start.26 = (bf16[4,1024,512]{2,1,0:T(8,128)(2,1)}, bf16[4,1024,512]{2,1,0:T(8,128)(2,1)}, u32[]{:S(2)}, u32[]{:S(2)}) collective-permute-start(bf16[4,1024,512]{2,1,0:T(8,128)(2,1)} %get-tuple-element.320), channel_id=1, source_target_pairs={{0,1},{1,0},{2,3},{3,2},{4,5},{5,4},{6,7},{7,6},{8,9},{9,8},{10,11... | collective-permute-start | bytes 12582920 | tf_op jit(solution)/shard_map/ppermute | solution.py:512
  456.5 28.5 %collective-permute-start.23 = (bf16[1,1024,512]{2,1,0:T(8,128)(2,1)}, bf16[1,1024,512]{2,1,0:T(8,128)(2,1)S(1)}, u32[]{:S(2)}, u32[]{:S(2)}) collective-permute-start(bf16[1,1024,512]{2,1,0:T(8,128)(2,1)} %get-tuple-element.316), channel_id=1, source_target_pairs={{0,8},{8,0},{16,24},{24,16},{1,9},{9,1},{17,25},{25,17},{2,10},{10... | collective-permute-start | bytes 3145736 | tf_op jit(solution)/shard_map/ppermute | solution.py:520
  456.8 28.2 %collective-permute-start.24 = (bf16[1,1024,512]{2,1,0:T(8,128)(2,1)}, bf16[1,1024,512]{2,1,0:T(8,128)(2,1)S(1)}, u32[]{:S(2)}, u32[]{:S(2)}) collective-permute-start(bf16[1,1024,512]{2,1,0:T(8,128)(2,1)} %get-tuple-element.318), channel_id=1, source_target_pairs={{0,16},{8,24},{16,0},{24,8},{1,17},{9,25},{17,1},{25,9},{2,18},{10... | collective-permute-start | bytes 3145736 | tf_op jit(solution)/shard_map/ppermute | solution.py:520
  490.4 63.8 %collective-permute-start.28 = (bf16[2,1024,512]{2,1,0:T(8,128)(2,1)}, bf16[2,1024,512]{2,1,0:T(8,128)(2,1)}, u32[]{:S(2)}, u32[]{:S(2)}) collective-permute-start(bf16[2,1024,512]{2,1,0:T(8,128)(2,1)} %get-tuple-element.460), channel_id=1, source_target_pairs={{0,8},{8,0},{16,24},{24,16},{1,9},{9,1},{17,25},{25,17},{2,10},{10... | collective-permute-start | bytes 6291464 | tf_op jit(solution)/shard_map/ppermute | solution.py:520
  496.1 58.0 %collective-permute-start.27 = (bf16[2,1024,512]{2,1,0:T(8,128)(2,1)}, bf16[2,1024,512]{2,1,0:T(8,128)(2,1)}, u32[]{:S(2)}, u32[]{:S(2)}) collective-permute-start(bf16[2,1024,512]{2,1,0:T(8,128)(2,1)} %get-tuple-element.462), channel_id=1, source_target_pairs={{0,16},{8,24},{16,0},{24,8},{1,17},{9,25},{17,1},{25,9},{2,18},{10... | collective-permute-start | bytes 6291464 | tf_op jit(solution)/shard_map/ppermute | solution.py:520
  554.2 116.1 %reduce-scatter.11.cloned.1.call-start = ((), (), s32[]{:S(2)}) async-start(), calls=%async_computation.7 | async-start | bytes 2621440 | tf_op jit(solution)/shard_map/reduce_scatter | solution.py:1204
  558.8 38.6 %collective-permute-start.29 = (bf16[1,1024,512]{2,1,0:T(8,128)(2,1)}, bf16[1,1024,512]{2,1,0:T(8,128)(2,1)}, u32[]{:S(2)}, u32[]{:S(2)}) collective-permute-start(bf16[1,1024,512]{2,1,0:T(8,128)(2,1)} %get-tuple-element.470), channel_id=1, source_target_pairs={{0,8},{8,0},{16,24},{24,16},{1,9},{9,1},{17,25},{25,17},{2,10},{10... | collective-permute-start | bytes 3145736 | tf_op jit(solution)/shard_map/ppermute | solution.py:520
  562.5 34.8 %collective-permute-start.30 = (bf16[1,1024,512]{2,1,0:T(8,128)(2,1)}, bf16[1,1024,512]{2,1,0:T(8,128)(2,1)S(1)}, u32[]{:S(2)}, u32[]{:S(2)}) collective-permute-start(bf16[1,1024,512]{2,1,0:T(8,128)(2,1)} %get-tuple-element.468), channel_id=1, source_target_pairs={{0,16},{8,24},{16,0},{24,8},{1,17},{9,25},{17,1},{25,9},{2,18},{10... | collective-permute-start | bytes 3145736 | tf_op jit(solution)/shard_map/ppermute | solution.py:520
  564.6 32.1 %collective-permute-start.32 = (bf16[352,768]{1,0:T(8,128)(2,1)}, bf16[352,768]{1,0:T(8,128)(2,1)}, u32[]{:S(2)}, u32[]{:S(2)}) collective-permute-start(bf16[352,768]{1,0:T(8,128)(2,1)} %get-tuple-element.507), channel_id=1, source_target_pairs={{0,8},{8,0},{16,24},{24,16},{1,9},{9,1},{17,25},{25,17},{2,10},{10... | collective-permute-start | bytes 1622024 | tf_op jit(solution)/shard_map/ppermute | solution.py:520
  566.2 31.2 %collective-permute-start.31 = (bf16[352,768]{1,0:T(8,128)(2,1)}, bf16[352,768]{1,0:T(8,128)(2,1)}, u32[]{:S(2)}, u32[]{:S(2)}) collective-permute-start(bf16[352,768]{1,0:T(8,128)(2,1)} %get-tuple-element.508), channel_id=1, source_target_pairs={{0,16},{8,24},{16,0},{24,8},{1,17},{9,25},{17,1},{25,9},{2,18},{10... | collective-permute-start | bytes 1622024 | tf_op jit(solution)/shard_map/ppermute | solution.py:520
  568.4 85.9 %collective-permute-start.39 = (bf16[384,768]{1,0:T(8,128)(2,1)}, bf16[384,768]{1,0:T(8,128)(2,1)}, u32[]{:S(2)}, u32[]{:S(2)}) collective-permute-start(bf16[384,768]{1,0:T(8,128)(2,1)} %get-tuple-element.493), channel_id=1, source_target_pairs={{0,8},{8,0},{16,24},{24,16},{1,9},{9,1},{17,25},{25,17},{2,10},{10... | collective-permute-start | bytes 1769480 | tf_op jit(solution)/shard_map/ppermute | solution.py:520
  600.9 36.7 %collective-permute-start.36 = (bf16[352,768]{1,0:T(8,128)(2,1)}, bf16[352,768]{1,0:T(8,128)(2,1)}, u32[]{:S(2)}, u32[]{:S(2)}) collective-permute-start(bf16[352,768]{1,0:T(8,128)(2,1)} %get-tuple-element.505), channel_id=1, source_target_pairs={{0,16},{8,24},{16,0},{24,8},{1,17},{9,25},{17,1},{25,9},{2,18},{10... | collective-permute-start | bytes 1622024 | tf_op jit(solution)/shard_map/ppermute | solution.py:520
  602.0 36.7 %collective-permute-start.35 = (bf16[352,768]{1,0:T(8,128)(2,1)}, bf16[352,768]{1,0:T(8,128)(2,1)}, u32[]{:S(2)}, u32[]{:S(2)}) collective-permute-start(bf16[352,768]{1,0:T(8,128)(2,1)} %get-tuple-element.506), channel_id=1, source_target_pairs={{0,8},{8,0},{16,24},{24,16},{1,9},{9,1},{17,25},{25,17},{2,10},{10... | collective-permute-start | bytes 1622024 | tf_op jit(solution)/shard_map/ppermute | solution.py:520
  605.7 33.0 %collective-permute-start.34 = (bf16[2,256,512]{2,1,0:T(8,128)(2,1)}, bf16[2,256,512]{2,1,0:T(8,128)(2,1)}, u32[]{:S(2)}, u32[]{:S(2)}) collective-permute-start(bf16[2,256,512]{2,1,0:T(8,128)(2,1)} %bitcast.291), channel_id=1, source_target_pairs={{0,16},{8,24},{16,0},{24,8},{1,17},{9,25},{17,1},{25,9},{2,18},{10... | collective-permute-start | bytes 1572872 | tf_op jit(solution)/shard_map/ppermute | solution.py:520
  606.8 31.8 %collective-permute-start.33 = (bf16[2,256,512]{2,1,0:T(8,128)(2,1)}, bf16[2,256,512]{2,1,0:T(8,128)(2,1)}, u32[]{:S(2)}, u32[]{:S(2)}) collective-permute-start(bf16[2,256,512]{2,1,0:T(8,128)(2,1)} %bitcast.292), channel_id=1, source_target_pairs={{0,8},{8,0},{16,24},{24,16},{1,9},{9,1},{17,25},{25,17},{2,10},{10... | collective-permute-start | bytes 1572872 | tf_op jit(solution)/shard_map/ppermute | solution.py:520
  637.6 16.7 %collective-permute-start.38 = (bf16[384,768]{1,0:T(8,128)(2,1)}, bf16[384,768]{1,0:T(8,128)(2,1)S(1)}, u32[]{:S(2)}, u32[]{:S(2)}) collective-permute-start(bf16[384,768]{1,0:T(8,128)(2,1)} %get-tuple-element.494), channel_id=1, source_target_pairs={{0,16},{8,24},{16,0},{24,8},{1,17},{9,25},{17,1},{25,9},{2,18},{10... | collective-permute-start | bytes 1769480 | tf_op jit(solution)/shard_map/ppermute | solution.py:520
  643.3 11.0 %collective-permute-start.41 = (bf16[256,512]{1,0:T(8,128)(2,1)}, bf16[256,512]{1,0:T(8,128)(2,1)}, u32[]{:S(2)}, u32[]{:S(2)}) collective-permute-start(bf16[256,512]{1,0:T(8,128)(2,1)} %slice_bitcast_fusion.16), channel_id=1, source_target_pairs={{0,8},{8,0},{16,24},{24,16},{1,9},{9,1},{17,25},{25,17},{2,10},{10... | collective-permute-start | bytes 786440 | tf_op jit(solution)/shard_map/ppermute | solution.py:520
  644.5 10.1 %collective-permute-start.40 = (bf16[256,512]{1,0:T(8,128)(2,1)S(1)}, bf16[256,512]{1,0:T(8,128)(2,1)}, u32[]{:S(2)}, u32[]{:S(2)}) collective-permute-start(bf16[256,512]{1,0:T(8,128)(2,1)S(1)} %slice_bitcast_fusion.17), channel_id=1, source_target_pairs={{0,16},{8,24},{16,0},{24,8},{1,17},{9,25},{17,1},{25,9},{2,18},{10... | collective-permute-start | bytes 786440 | tf_op jit(solution)/shard_map/ppermute | solution.py:520
  649.4 5.2 collective-permute-start.37
  654.7 11.1 %collective-permute-start.42 = (bf16[2,144,256]{2,1,0:T(8,128)(2,1)S(1)}, bf16[2,144,256]{2,1,0:T(8,128)(2,1)S(1)}, u32[]{:S(2)}, u32[]{:S(2)}) collective-permute-start(bf16[2,144,256]{2,1,0:T(8,128)(2,1)S(1)} %dynamic-slice_bitcast_fusion.10), channel_id=1, source_target_pairs={{0,4},{1,5},{2,6},{3,7},{4,0},{5,1},{6,2},{7,3},{8,12},{9,13},{10,... | collective-permute-start | bytes 442376 | tf_op jit(solution)/shard_map/ppermute | solution.py:1300
  658.5 14.9 %collective-permute-start.45 = (bf16[384,768]{1,0:T(8,128)(2,1)}, bf16[384,768]{1,0:T(8,128)(2,1)}, u32[]{:S(2)}, u32[]{:S(2)}) collective-permute-start(bf16[384,768]{1,0:T(8,128)(2,1)} %get-tuple-element.491), channel_id=1, source_target_pairs={{0,16},{8,24},{16,0},{24,8},{1,17},{9,25},{17,1},{25,9},{2,18},{10... | collective-permute-start | bytes 1769480 | tf_op jit(solution)/shard_map/ppermute | solution.py:520
  660.1 14.5 %collective-permute-start.44 = (bf16[384,768]{1,0:T(8,128)(2,1)}, bf16[384,768]{1,0:T(8,128)(2,1)}, u32[]{:S(2)}, u32[]{:S(2)}) collective-permute-start(bf16[384,768]{1,0:T(8,128)(2,1)} %get-tuple-element.492), channel_id=1, source_target_pairs={{0,8},{8,0},{16,24},{24,16},{1,9},{9,1},{17,25},{25,17},{2,10},{10... | collective-permute-start | bytes 1769480 | tf_op jit(solution)/shard_map/ppermute | solution.py:520
  665.8 4.4 collective-permute-start.43
  674.7 14.0 %collective-permute-start.48 = (bf16[2,256,512]{2,1,0:T(8,128)(2,1)}, bf16[2,256,512]{2,1,0:T(8,128)(2,1)S(1)}, u32[]{:S(2)}, u32[]{:S(2)}) collective-permute-start(bf16[2,256,512]{2,1,0:T(8,128)(2,1)} %bitcast.294), channel_id=1, source_target_pairs={{0,16},{8,24},{16,0},{24,8},{1,17},{9,25},{17,1},{25,9},{2,18},{10... | collective-permute-start | bytes 1572872 | tf_op jit(solution)/shard_map/ppermute | solution.py:520
  675.1 13.6 %collective-permute-start.47 = (bf16[2,256,512]{2,1,0:T(8,128)(2,1)}, bf16[2,256,512]{2,1,0:T(8,128)(2,1)S(1)}, u32[]{:S(2)}, u32[]{:S(2)}) collective-permute-start(bf16[2,256,512]{2,1,0:T(8,128)(2,1)} %bitcast.295), channel_id=1, source_target_pairs={{0,8},{8,0},{16,24},{24,16},{1,9},{9,1},{17,25},{25,17},{2,10},{10... | collective-permute-start | bytes 1572872 | tf_op jit(solution)/shard_map/ppermute | solution.py:520
  676.4 12.2 %collective-permute-start.46 = (bf16[144,256]{1,0:T(8,128)(2,1)S(1)}, bf16[144,256]{1,0:T(8,128)(2,1)S(1)}, u32[]{:S(2)}, u32[]{:S(2)}) collective-permute-start(bf16[144,256]{1,0:T(8,128)(2,1)S(1)} %bitcast.297), channel_id=1, source_target_pairs={{0,8},{8,0},{16,24},{24,16},{1,9},{9,1},{17,25},{25,17},{2,10},{10... | collective-permute-start | bytes 221192 | tf_op jit(solution)/shard_map/ppermute | solution.py:520
  689.5 12.5 %collective-permute-start.50 = (bf16[256,512]{1,0:T(8,128)(2,1)}, bf16[256,512]{1,0:T(8,128)(2,1)}, u32[]{:S(2)}, u32[]{:S(2)}) collective-permute-start(bf16[256,512]{1,0:T(8,128)(2,1)} %get-tuple-element.514), channel_id=1, source_target_pairs={{0,16},{8,24},{16,0},{24,8},{1,17},{9,25},{17,1},{25,9},{2,18},{10... | collective-permute-start | bytes 786440 | tf_op jit(solution)/shard_map/ppermute | solution.py:520
  691.8 5.1 collective-permute-start.49
  693.2 10.1 %collective-permute-start.51 = (bf16[256,512]{1,0:T(8,128)(2,1)}, bf16[256,512]{1,0:T(8,128)(2,1)}, u32[]{:S(2)}, u32[]{:S(2)}) collective-permute-start(bf16[256,512]{1,0:T(8,128)(2,1)} %get-tuple-element.517), channel_id=1, source_target_pairs={{0,8},{8,0},{16,24},{24,16},{1,9},{9,1},{17,25},{25,17},{2,10},{10... | collective-permute-start | bytes 786440 | tf_op jit(solution)/shard_map/ppermute | solution.py:520
  (94 other events, 523.1 us)
Sparse Core Ops, SparseCore 0:
  16.7 50.0 all-gather.9
  69.0 44.7 all-gather.11
  115.9 29.1 all-gather.15
  146.6 83.3 all-gather.13
  316.2 97.7 reduce-scatter.4
  445.2 90.4 reduce-scatter.6
  554.3 41.7 reduce-scatter.8
  610.6 42.6 reduce-scatter.10
